TPU v7x, 128 devices: a whole 4x4x4 slice. The times are simulated.
128 devices in a mesh: leaf: 64 (over z, y, x), sub: 2 (over core).
Axes of the slice: x: 4, y: 4, z: 4, core: 2. Of those that a mesh axis runs over, the one named last changes fastest.
Arguments:
- density: bfloat16 [8, 131072], P(None, ('leaf', 'sub')), may hold values from -6 to 6
- basis: bfloat16 [2048, 64, 64], P(('leaf', 'sub')), may hold values from -0.75 to 0.75
- near_ids: int32 [2048, 24], P(('leaf', 'sub')), may hold values from 0 to 159, as said below
- near_count: int32 [2048], P(('leaf', 'sub')), may hold values from 16 to 24
- near_blocks: bfloat16 [2048, 64, 1536], P(('leaf', 'sub')), may hold values from -0.15625 to 0.15625
- local_transfer: bfloat16 [1920, 64, 128], P(('leaf', 'sub')), may hold values from -0.5 to 0.5
- local_coupling: bfloat16 [3968, 64, 1024], P(('leaf', 'sub')), may hold values from -0.1875 to 0.1875
- local_coupling_ids: int32 [3968, 16], P(('leaf', 'sub')), may hold values from 0 to 159, as said below
- top_transfer: bfloat16 [126, 64, 128], replicated, may hold values from -0.5 to 0.5
- top_coupling: bfloat16 [126, 64, 128], replicated, may hold values from -0.5 to 0.5
- top_coupling_ids: int32 [126, 2], replicated, may hold values from 0 to 63, as said below
Outputs:
- potential: float32 [8, 131072], P(None, ('leaf', 'sub'))
Inputs may be any that keep to these rules, and one draw needn't show every extreme that they name: `near_ids`: each entry is a window index of its leaf's device with n = 16; entries that name a device outside the slice read as zeros. `local_coupling_ids`: an entry of row r = d * 31 + 2 * 16 - 2 n + m is a window index of device d at the level of n = 16 >> h nodes a device, below 10 n. `top_coupling_ids`: an entry of row D - 2 n + m, for the level of n = D >> t nodes, names a node of that level, below n.
All inputs are finite; a program needn't handle non-finite values.
Results may differ from a plain program's by a relative error of at most 0.017.
Values may be sent and summed in bfloat16 or wider, within the bound.
No kernel may reach another device: no remote copies, remote signals or barrier semaphores. Data moves between devices by JAX's collectives and lax.ppermute only.
A program may use at most 64 MiB of HBM per device.

v0:
```python
import jax
import jax.numpy as jnp
from jax import lax
from jax.sharding import PartitionSpec as P

P_SIZE = 64
LOCAL_LEVELS = 5
NEAR = 24


def passed_along(value, axis, steps):
    count = lax.axis_size(axis)
    initial, last = (max(0, -steps), min(count, count - steps))
    return lax.ppermute(value, axis, [(source, source + steps) for source in range(initial, last)])


def flatten(window):
    vectors, slots, node_count, columns = window.shape
    return window.reshape(vectors, slots * node_count, columns)


def density_window(shaped):
    paired = lax.all_gather(shaped[:, None], "sub", axis=1, tiled=True)
    shifted = [passed_along(paired, "leaf", distance) for distance in (2, 1, -1, -2)]
    return flatten(jnp.concatenate(shifted[:2] + [paired] + shifted[2:], axis=1))


def level_window(values):
    paired = lax.all_gather(values[:, None], "sub", axis=1, tiled=True)
    shifted = [passed_along(paired, "leaf", distance) for distance in (2, 1, -1, -2)]
    return flatten(jnp.concatenate(shifted[:2] + [paired] + shifted[2:], axis=1))


def select_rows(values, slot_ids):
    picked = jnp.take(values, slot_ids, axis=1)
    return picked.reshape(picked.shape[0], slot_ids.shape[0], -1)


def apply_blocks(operand, blocks):
    return jnp.einsum("vnc,nkc->vnk", operand, blocks, preferred_element_type=jnp.float32)


def upward(children, transfer):
    vectors, child_count, basis_rank = children.shape
    joined = children.reshape(vectors, child_count // 2, 2 * basis_rank)
    return apply_blocks(joined, transfer).astype(jnp.bfloat16)


def downward(incoming, transfer):
    vectors, node_count, basis_rank = incoming.shape
    descent = jnp.einsum(
        "vnk,nkc->vnc", incoming.astype(jnp.bfloat16), transfer, preferred_element_type=jnp.float32
    )
    return descent.reshape(vectors, 2 * node_count, basis_rank)


def local(
    density,
    basis,
    near_ids,
    near_count,
    near_blocks,
    local_transfer,
    local_coupling,
    local_coupling_ids,
    top_transfer,
    top_coupling,
    top_coupling_ids,
):
    vectors = density.shape[0]
    leaf_count = basis.shape[0]
    shaped = density.reshape(vectors, leaf_count, P_SIZE)
    near_window = density_window(shaped)
    live_mask = jnp.arange(NEAR, dtype=jnp.int32)[None, :] < near_count[:, None]
    picked = jnp.take(near_window, near_ids, axis=1)
    picked = jnp.where(live_mask[None, :, :, None], picked, jnp.zeros_like(picked))
    near_field = apply_blocks(picked.reshape(vectors, leaf_count, NEAR * P_SIZE), near_blocks)
    coeffs = [
        jnp.einsum("vlp,lpk->vlk", shaped, basis, preferred_element_type=jnp.float32).astype(
            jnp.bfloat16
        )
    ]
    for height in range(1, LOCAL_LEVELS):
        node_count = leaf_count >> height
        offset = leaf_count - 2 * node_count
        coeffs.append(upward(coeffs[-1], local_transfer[offset : offset + node_count]))
    coupled = []
    for height in range(LOCAL_LEVELS):
        flat_window = level_window(coeffs[height])
        couple_node_count = leaf_count >> height
        couple_offset = 2 * leaf_count - 2 * couple_node_count
        couple_operand = select_rows(
            flat_window, local_coupling_ids[couple_offset : couple_offset + couple_node_count]
        )
        coupled.append(
            apply_blocks(
                couple_operand, local_coupling[couple_offset : couple_offset + couple_node_count]
            )
        )
    root_coeffs = lax.all_gather(coeffs[-1], ("leaf", "sub"), axis=1, tiled=True)
    devices = root_coeffs.shape[1]
    top_levels = devices.bit_length() - 1
    top_coeffs = [root_coeffs]
    top_coupled = [None]
    for height in range(1, top_levels):
        node_count = devices >> height
        offset = devices - 2 * node_count
        parent_coeffs = upward(top_coeffs[-1], top_transfer[offset : offset + node_count])
        top_coeffs.append(parent_coeffs)
        operand = select_rows(parent_coeffs, top_coupling_ids[offset : offset + node_count])
        top_coupled.append(apply_blocks(operand, top_coupling[offset : offset + node_count]))
    incoming = top_coupled[-1]
    for height in range(top_levels - 1, 0, -1):
        node_count = devices >> height
        offset = devices - 2 * node_count
        descent = downward(incoming, top_transfer[offset : offset + node_count])
        incoming = top_coupled[height - 1] + descent if height > 1 else descent
    own_share = lax.dynamic_slice_in_dim(incoming, lax.axis_index(("leaf", "sub")), 1, axis=1)
    incoming = coupled[-1] + own_share
    for height in range(LOCAL_LEVELS - 1, 0, -1):
        node_count = leaf_count >> height
        offset = leaf_count - 2 * node_count
        incoming = coupled[height - 1] + downward(
            incoming, local_transfer[offset : offset + node_count]
        )
    far_field = jnp.einsum(
        "vlk,lpk->vlp", incoming.astype(jnp.bfloat16), basis, preferred_element_type=jnp.float32
    )
    return (near_field + far_field).reshape(vectors, leaf_count * P_SIZE)


def solution(mesh):
    in_specs = (
        P(None, ("leaf", "sub")),
        P(("leaf", "sub"), None, None),
        P(("leaf", "sub"), None),
        P(("leaf", "sub")),
        P(("leaf", "sub"), None, None),
        P(("leaf", "sub"), None, None),
        P(("leaf", "sub"), None, None),
        P(("leaf", "sub"), None),
        P(),
        P(),
        P(),
    )
    out_specs = P(None, ("leaf", "sub"))
    return jax.shard_map(local, mesh=mesh, in_specs=in_specs, out_specs=out_specs, check_vma=False)
```

profile of v0, /device:TPU:36, one launch (start us, length us, event | category | flops | bytes accessed | tf_op | source)
XLA Modules:
  0.0 292.2 jit_solution(1928388781397510569)
XLA Ops:
  8.2 3.4 %collective-permute-start.20 = (bf16[8,2,1,64]{3,0,1,2:T(8,128)(2,1)}, bf16[8,2,1,64]{3,0,1,2:T(8,128)(2,1)}, u32[]{:S(2)}, u32[]{:S(2)}) collective-permute-start(bf16[8,2,1,64]{3,0,1,2:T(8,128)(2,1)} %bitcast.32), channel_id=1, source_target_pairs={{0,4},{2,6},{4,8},{6,10},{8,12},{10,14},{12,16},{14,18},{16,20},{1... | collective-permute-start | bytes 6152 | tf_op jit(solution)/shard_map/ppermute | solution.py:14
  11.6 4.0 %collective-permute-start.21 = (bf16[8,2,1,64]{3,0,1,2:T(8,128)(2,1)}, bf16[8,2,1,64]{3,0,1,2:T(8,128)(2,1)}, u32[]{:S(2)}, u32[]{:S(2)}) collective-permute-start(bf16[8,2,1,64]{3,0,1,2:T(8,128)(2,1)} %bitcast.32), channel_id=1, source_target_pairs={{0,2},{2,4},{4,6},{6,8},{8,10},{10,12},{12,14},{14,16},{16,18},{18... | collective-permute-start | bytes 6152 | tf_op jit(solution)/shard_map/ppermute | solution.py:14
  15.7 1.9 collective-permute-start.22
  17.6 8.1 %collective-permute-start.23 = (bf16[8,2,1,64]{3,0,1,2:T(8,128)(2,1)}, bf16[8,2,1,64]{3,0,1,2:T(8,128)(2,1)}, u32[]{:S(2)}, u32[]{:S(2)}) collective-permute-start(bf16[8,2,1,64]{3,0,1,2:T(8,128)(2,1)} %bitcast.32), channel_id=1, source_target_pairs={{4,0},{6,2},{8,4},{10,6},{12,8},{14,10},{16,12},{18,14},{20,16},{2... | collective-permute-start | bytes 6152 | tf_op jit(solution)/shard_map/ppermute | solution.py:14
  25.6 1.9 all-gather.3
  29.5 35.6 %all_gather.27 = bf16[8,128,64]{2,0,1:T(8,128)(2,1)S(1)} all-gather(bf16[8,1,64]{2,0,1:T(8,128)(2,1)S(1)} %fusion.44), channel_id=1, replica_groups=mesh['leaf'=64,'sub'=2] {'leaf','sub'}, dimensions={1}, use_global_device_ids=true | all-gather | bytes 132096 | tf_op jit(solution)/shard_map/all_gather | solution.py:100
  85.1 2.0 all-gather.1
  89.8 2.0 all-gather
  131.8 3.3 %convolution_bitcast_fusion = f32[8,64,128]{2,0,1:T(8,128)} fusion(bf16[126,64,128]{2,1,0:T(8,128)(2,1)} %param.20, bf16[126,64,128]{2,1,0:T(8,128)(2,1)} %param.19, f32[8,64,64]{2,1,0:T(8,128)} %reshape.285, bf16[8,64,128]{2,1,0:T(8,128)(2,1)S(1)} %broadcast_select_fusion.1), kind=kOutput, calls=%fused_computation.14 | convolution fusion | flops 16842752 | bytes 2752512 | tf_op jit(solution)/shard_map/vnk,nkc->vnc/dot_general | solution.py:51
  145.4 2.0 all_gather.21
  154.5 3.4 %collective-permute-start.17 = (bf16[8,2,2,64]{3,0,2,1:T(8,128)(2,1)}, bf16[8,2,2,64]{3,0,2,1:T(8,128)(2,1)S(1)}, u32[]{:S(2)}, u32[]{:S(2)}) collective-permute-start(bf16[8,2,2,64]{3,0,2,1:T(8,128)(2,1)} %bitcast.23), channel_id=1, source_target_pairs={{0,2},{2,4},{4,6},{6,8},{8,10},{10,12},{12,14},{14,16},{16,18},{18... | collective-permute-start | bytes 12296 | tf_op jit(solution)/shard_map/ppermute | solution.py:14
  158.6 2.4 collective-permute-start.18
  162.4 8.2 %collective-permute-start.19 = (bf16[8,2,2,64]{3,0,2,1:T(8,128)(2,1)}, bf16[8,2,2,64]{3,0,2,1:T(8,128)(2,1)S(1)}, u32[]{:S(2)}, u32[]{:S(2)}) collective-permute-start(bf16[8,2,2,64]{3,0,2,1:T(8,128)(2,1)} %bitcast.23), channel_id=1, source_target_pairs={{4,0},{6,2},{8,4},{10,6},{12,8},{14,10},{16,12},{18,14},{20,16},{2... | collective-permute-start | bytes 12296 | tf_op jit(solution)/shard_map/ppermute | solution.py:14
  176.6 1.9 collective-permute-start.13
  179.2 3.9 %collective-permute-start.14 = (bf16[8,2,4,64]{3,0,2,1:T(8,128)(2,1)S(1)}, bf16[8,2,4,64]{3,0,2,1:T(8,128)(2,1)S(1)}, u32[]{:S(2)}, u32[]{:S(2)}) collective-permute-start(bf16[8,2,4,64]{3,0,2,1:T(8,128)(2,1)S(1)} %bitcast.277), channel_id=1, source_target_pairs={{2,0},{4,2},{6,4},{8,6},{10,8},{12,10},{14,12},{16,14},{18,16},{20... | collective-permute-start | bytes 24584 | tf_op jit(solution)/shard_map/ppermute | solution.py:14
  183.8 9.6 %collective-permute-start.15 = (bf16[8,2,4,64]{3,0,2,1:T(8,128)(2,1)S(1)}, bf16[8,2,4,64]{3,0,2,1:T(8,128)(2,1)}, u32[]{:S(2)}, u32[]{:S(2)}) collective-permute-start(bf16[8,2,4,64]{3,0,2,1:T(8,128)(2,1)S(1)} %bitcast.278), channel_id=1, source_target_pairs={{4,0},{6,2},{8,4},{10,6},{12,8},{14,10},{16,12},{18,14},{20,16},{2... | collective-permute-start | bytes 24584 | tf_op jit(solution)/shard_map/ppermute | solution.py:14
  193.5 1.9 collective-permute-start.8
  197.6 1.9 collective-permute-start.9
  199.5 3.9 %collective-permute-start.10 = (bf16[8,2,8,64]{3,0,2,1:T(8,128)(2,1)S(1)}, bf16[8,2,8,64]{3,0,2,1:T(8,128)(2,1)}, u32[]{:S(2)}, u32[]{:S(2)}) collective-permute-start(bf16[8,2,8,64]{3,0,2,1:T(8,128)(2,1)S(1)} %bitcast.269), channel_id=1, source_target_pairs={{2,0},{4,2},{6,4},{8,6},{10,8},{12,10},{14,12},{16,14},{18,16},{20... | collective-permute-start | bytes 49160 | tf_op jit(solution)/shard_map/ppermute | solution.py:14
  204.2 9.6 %collective-permute-start.11 = (bf16[8,2,8,64]{3,0,2,1:T(8,128)(2,1)S(1)}, bf16[8,2,8,64]{3,0,2,1:T(8,128)(2,1)}, u32[]{:S(2)}, u32[]{:S(2)}) collective-permute-start(bf16[8,2,8,64]{3,0,2,1:T(8,128)(2,1)S(1)} %bitcast.270), channel_id=1, source_target_pairs={{4,0},{6,2},{8,4},{10,6},{12,8},{14,10},{16,12},{18,14},{20,16},{2... | collective-permute-start | bytes 49160 | tf_op jit(solution)/shard_map/ppermute | solution.py:14
  213.9 1.9 collective-permute-start.4
  218.8 1.9 collective-permute-start.5
  221.5 3.9 %collective-permute-start.6 = (bf16[8,2,16,64]{3,0,2,1:T(8,128)(2,1)S(1)}, bf16[8,2,16,64]{3,0,2,1:T(8,128)(2,1)}, u32[]{:S(2)}, u32[]{:S(2)}) collective-permute-start(bf16[8,2,16,64]{3,0,2,1:T(8,128)(2,1)S(1)} %bitcast.259), channel_id=1, source_target_pairs={{2,0},{4,2},{6,4},{8,6},{10,8},{12,10},{14,12},{16,14},{18,16},{20... | collective-permute-start | bytes 98312 | tf_op jit(solution)/shard_map/ppermute | solution.py:14
  226.2 9.6 %collective-permute-start.7 = (bf16[8,2,16,64]{3,0,2,1:T(8,128)(2,1)S(1)}, bf16[8,2,16,64]{3,0,2,1:T(8,128)(2,1)}, u32[]{:S(2)}, u32[]{:S(2)}) collective-permute-start(bf16[8,2,16,64]{3,0,2,1:T(8,128)(2,1)S(1)} %bitcast.260), channel_id=1, source_target_pairs={{4,0},{6,2},{8,4},{10,6},{12,8},{14,10},{16,12},{18,14},{20,16},{2... | collective-permute-start | bytes 98312 | tf_op jit(solution)/shard_map/ppermute | solution.py:14
  236.6 1.9 collective-permute-start
  248.7 3.9 %collective-permute-start.2 = (bf16[8,2,16,64]{3,2,1,0:T(8,128)(2,1)}, bf16[8,2,16,64]{3,2,1,0:T(8,128)(2,1)S(1)}, u32[]{:S(2)}, u32[]{:S(2)}) collective-permute-start(bf16[8,2,16,64]{3,2,1,0:T(8,128)(2,1)} %all_gather.21), channel_id=1, source_target_pairs={{2,0},{4,2},{6,4},{8,6},{10,8},{12,10},{14,12},{16,14},{18,16},{20... | collective-permute-start | bytes 98312 | tf_op jit(solution)/shard_map/ppermute | solution.py:14
  253.5 9.8 %collective-permute-start.3 = (bf16[8,2,16,64]{3,2,1,0:T(8,128)(2,1)}, bf16[8,2,16,64]{3,2,1,0:T(8,128)(2,1)}, u32[]{:S(2)}, u32[]{:S(2)}) collective-permute-start(bf16[8,2,16,64]{3,2,1,0:T(8,128)(2,1)} %all_gather.21), channel_id=1, source_target_pairs={{4,0},{6,2},{8,4},{10,6},{12,8},{14,10},{16,12},{18,14},{20,16},{2... | collective-permute-start | bytes 98312 | tf_op jit(solution)/shard_map/ppermute | solution.py:14
  271.0 1.9 copy.429
  272.9 2.2 gather.73
  277.6 2.6 gather_fusion
  280.2 2.2 copy.265
  285.8 3.1 %fusion.25 = f32[16,8,64]{2,1,0:T(8,128)} fusion(bf16[16,64,64]{2,1,0:T(8,128)(2,1)} %param.12, bf16[31,64,1024]{2,1,0:T(8,128)(2,1)} %param.17, bf16[8,16,1024]{2,1,0:T(8,128)(2,1)} %broadcast_select_fusion, f32[8,16,64]{2,1,0:T(8,128)} %reshape.291), kind=kOutput, calls=%fused_computation.45 | convolution fusion | flops 17842176 | bytes 2719744 | tf_op jit(solution)/shard_map/vlk,lpk->vlp/dot_general | solution.py:126
  (269 shorter events, 135.5 us)
Async XLA Ops:
  0.0 289.7 %copy-start = (bf16[16,64,1536]{2,1,0:T(8,128)(2,1)S(1)}, bf16[16,64,1536]{2,1,0:T(8,128)(2,1)}, u32[]{:S(2)}) copy-start(bf16[16,64,1536]{2,1,0:T(8,128)(2,1)} %param.15) | copy-start | bytes 9437188
  8.2 146.3 %collective-permute-start.20 = (bf16[8,2,1,64]{3,0,1,2:T(8,128)(2,1)}, bf16[8,2,1,64]{3,0,1,2:T(8,128)(2,1)}, u32[]{:S(2)}, u32[]{:S(2)}) collective-permute-start(bf16[8,2,1,64]{3,0,1,2:T(8,128)(2,1)} %bitcast.32), channel_id=1, source_target_pairs={{0,4},{2,6},{4,8},{6,10},{8,12},{10,14},{12,16},{14,18},{16,20},{1... | collective-permute-start | bytes 6152 | tf_op jit(solution)/shard_map/ppermute | solution.py:14
  11.6 147.0 %collective-permute-start.21 = (bf16[8,2,1,64]{3,0,1,2:T(8,128)(2,1)}, bf16[8,2,1,64]{3,0,1,2:T(8,128)(2,1)}, u32[]{:S(2)}, u32[]{:S(2)}) collective-permute-start(bf16[8,2,1,64]{3,0,1,2:T(8,128)(2,1)} %bitcast.32), channel_id=1, source_target_pairs={{0,2},{2,4},{4,6},{6,8},{8,10},{10,12},{12,14},{14,16},{16,18},{18... | collective-permute-start | bytes 6152 | tf_op jit(solution)/shard_map/ppermute | solution.py:14
  15.7 146.7 %collective-permute-start.22 = (bf16[8,2,1,64]{3,0,1,2:T(8,128)(2,1)}, bf16[8,2,1,64]{3,0,1,2:T(8,128)(2,1)}, u32[]{:S(2)}, u32[]{:S(2)}) collective-permute-start(bf16[8,2,1,64]{3,0,1,2:T(8,128)(2,1)} %bitcast.32), channel_id=1, source_target_pairs={{2,0},{4,2},{6,4},{8,6},{10,8},{12,10},{14,12},{16,14},{18,16},{20... | collective-permute-start | bytes 6152 | tf_op jit(solution)/shard_map/ppermute | solution.py:14
  17.6 153.7 %collective-permute-start.23 = (bf16[8,2,1,64]{3,0,1,2:T(8,128)(2,1)}, bf16[8,2,1,64]{3,0,1,2:T(8,128)(2,1)}, u32[]{:S(2)}, u32[]{:S(2)}) collective-permute-start(bf16[8,2,1,64]{3,0,1,2:T(8,128)(2,1)} %bitcast.32), channel_id=1, source_target_pairs={{4,0},{6,2},{8,4},{10,6},{12,8},{14,10},{16,12},{18,14},{20,16},{2... | collective-permute-start | bytes 6152 | tf_op jit(solution)/shard_map/ppermute | solution.py:14
  27.6 149.0 %collective-permute-start.16 = (bf16[8,2,2,64]{3,0,2,1:T(8,128)(2,1)}, bf16[8,2,2,64]{3,0,2,1:T(8,128)(2,1)}, u32[]{:S(2)}, u32[]{:S(2)}) collective-permute-start(bf16[8,2,2,64]{3,0,2,1:T(8,128)(2,1)} %bitcast.23), channel_id=1, source_target_pairs={{0,4},{2,6},{4,8},{6,10},{8,12},{10,14},{12,16},{14,18},{16,20},{1... | collective-permute-start | bytes 12296 | tf_op jit(solution)/shard_map/ppermute | solution.py:14
  131.8 6.9 %copy-start.7 = (pred[2,16]{0,1:T(8,128)(4,1)S(1)}, pred[2,16]{0,1:T(8,128)(4,1)}, u32[]{:S(2)}) copy-start(pred[2,16]{0,1:T(8,128)(4,1)} %compare_and_fusion) | copy-start | bytes 100
  131.8 13.7 %copy-start.3 = (bf16[8,1,16,64]{3,2,0,1:T(8,128)(2,1)S(1)}, bf16[8,1,16,64]{3,2,0,1:T(8,128)(2,1)}, u32[]{:S(2)}) copy-start(bf16[8,1,16,64]{3,2,0,1:T(8,128)(2,1)} %broadcast_in_dim_reshape.3) | copy-start | bytes 49156
  131.8 61.7 %copy-start.4 = (bf16[8,16,64]{2,0,1:T(8,128)(2,1)S(1)}, bf16[8,16,64]{2,0,1:T(8,128)(2,1)}, u32[]{:S(2)}) copy-start(bf16[8,16,64]{2,0,1:T(8,128)(2,1)} %all-gather.1) | copy-start | bytes 49156
  135.1 78.8 %copy-start.2 = (bf16[8,32,64]{2,0,1:T(8,128)(2,1)S(1)}, bf16[8,32,64]{2,0,1:T(8,128)(2,1)}, u32[]{:S(2)}) copy-start(bf16[8,32,64]{2,0,1:T(8,128)(2,1)} %all-gather) | copy-start | bytes 98308
  154.5 24.7 %collective-permute-start.17 = (bf16[8,2,2,64]{3,0,2,1:T(8,128)(2,1)}, bf16[8,2,2,64]{3,0,2,1:T(8,128)(2,1)S(1)}, u32[]{:S(2)}, u32[]{:S(2)}) collective-permute-start(bf16[8,2,2,64]{3,0,2,1:T(8,128)(2,1)} %bitcast.23), channel_id=1, source_target_pairs={{0,2},{2,4},{4,6},{6,8},{8,10},{10,12},{12,14},{14,16},{16,18},{18... | collective-permute-start | bytes 12296 | tf_op jit(solution)/shard_map/ppermute | solution.py:14
  158.6 25.2 %collective-permute-start.18 = (bf16[8,2,2,64]{3,0,2,1:T(8,128)(2,1)}, bf16[8,2,2,64]{3,0,2,1:T(8,128)(2,1)S(1)}, u32[]{:S(2)}, u32[]{:S(2)}) collective-permute-start(bf16[8,2,2,64]{3,0,2,1:T(8,128)(2,1)} %bitcast.23), channel_id=1, source_target_pairs={{2,0},{4,2},{6,4},{8,6},{10,8},{12,10},{14,12},{16,14},{18,16},{20... | collective-permute-start | bytes 12296 | tf_op jit(solution)/shard_map/ppermute | solution.py:14
  162.4 31.1 %collective-permute-start.19 = (bf16[8,2,2,64]{3,0,2,1:T(8,128)(2,1)}, bf16[8,2,2,64]{3,0,2,1:T(8,128)(2,1)S(1)}, u32[]{:S(2)}, u32[]{:S(2)}) collective-permute-start(bf16[8,2,2,64]{3,0,2,1:T(8,128)(2,1)} %bitcast.23), channel_id=1, source_target_pairs={{4,0},{6,2},{8,4},{10,6},{12,8},{14,10},{16,12},{18,14},{20,16},{2... | collective-permute-start | bytes 12296 | tf_op jit(solution)/shard_map/ppermute | solution.py:14
  171.3 26.3 %collective-permute-start.12 = (bf16[8,2,4,64]{3,0,2,1:T(8,128)(2,1)S(1)}, bf16[8,2,4,64]{3,0,2,1:T(8,128)(2,1)S(1)}, u32[]{:S(2)}, u32[]{:S(2)}) collective-permute-start(bf16[8,2,4,64]{3,0,2,1:T(8,128)(2,1)S(1)} %bitcast.275), channel_id=1, source_target_pairs={{0,4},{2,6},{4,8},{6,10},{8,12},{10,14},{12,16},{14,18},{16,20},{1... | collective-permute-start | bytes 24584 | tf_op jit(solution)/shard_map/ppermute | solution.py:14
  176.6 22.9 %collective-permute-start.13 = (bf16[8,2,4,64]{3,0,2,1:T(8,128)(2,1)S(1)}, bf16[8,2,4,64]{3,0,2,1:T(8,128)(2,1)}, u32[]{:S(2)}, u32[]{:S(2)}) collective-permute-start(bf16[8,2,4,64]{3,0,2,1:T(8,128)(2,1)S(1)} %bitcast.276), channel_id=1, source_target_pairs={{0,2},{2,4},{4,6},{6,8},{8,10},{10,12},{12,14},{14,16},{16,18},{18... | collective-permute-start | bytes 24584 | tf_op jit(solution)/shard_map/ppermute | solution.py:14
  179.2 25.0 %collective-permute-start.14 = (bf16[8,2,4,64]{3,0,2,1:T(8,128)(2,1)S(1)}, bf16[8,2,4,64]{3,0,2,1:T(8,128)(2,1)S(1)}, u32[]{:S(2)}, u32[]{:S(2)}) collective-permute-start(bf16[8,2,4,64]{3,0,2,1:T(8,128)(2,1)S(1)} %bitcast.277), channel_id=1, source_target_pairs={{2,0},{4,2},{6,4},{8,6},{10,8},{12,10},{14,12},{16,14},{18,16},{20... | collective-permute-start | bytes 24584 | tf_op jit(solution)/shard_map/ppermute | solution.py:14
  183.8 30.0 %collective-permute-start.15 = (bf16[8,2,4,64]{3,0,2,1:T(8,128)(2,1)S(1)}, bf16[8,2,4,64]{3,0,2,1:T(8,128)(2,1)}, u32[]{:S(2)}, u32[]{:S(2)}) collective-permute-start(bf16[8,2,4,64]{3,0,2,1:T(8,128)(2,1)S(1)} %bitcast.278), channel_id=1, source_target_pairs={{4,0},{6,2},{8,4},{10,6},{12,8},{14,10},{16,12},{18,14},{20,16},{2... | collective-permute-start | bytes 24584 | tf_op jit(solution)/shard_map/ppermute | solution.py:14
  193.5 25.3 %collective-permute-start.8 = (bf16[8,2,8,64]{3,0,2,1:T(8,128)(2,1)S(1)}, bf16[8,2,8,64]{3,0,2,1:T(8,128)(2,1)}, u32[]{:S(2)}, u32[]{:S(2)}) collective-permute-start(bf16[8,2,8,64]{3,0,2,1:T(8,128)(2,1)S(1)} %bitcast.267), channel_id=1, source_target_pairs={{0,4},{2,6},{4,8},{6,10},{8,12},{10,14},{12,16},{14,18},{16,20},{1... | collective-permute-start | bytes 49160 | tf_op jit(solution)/shard_map/ppermute | solution.py:14
  196.1 47.4 %copy-start.6 = (pred[8,1024]{1,0:T(8,128)(4,1)S(1)}, pred[8,1024]{1,0:T(8,128)(4,1)}, u32[]{:S(2)}) copy-start(pred[8,1024]{1,0:T(8,128)(4,1)} %broadcast_in_dim.237) | copy-start | bytes 24580
  197.6 24.0 %collective-permute-start.9 = (bf16[8,2,8,64]{3,0,2,1:T(8,128)(2,1)S(1)}, bf16[8,2,8,64]{3,0,2,1:T(8,128)(2,1)}, u32[]{:S(2)}, u32[]{:S(2)}) collective-permute-start(bf16[8,2,8,64]{3,0,2,1:T(8,128)(2,1)S(1)} %bitcast.268), channel_id=1, source_target_pairs={{0,2},{2,4},{4,6},{6,8},{8,10},{10,12},{12,14},{14,16},{16,18},{18... | collective-permute-start | bytes 49160 | tf_op jit(solution)/shard_map/ppermute | solution.py:14
  199.5 26.7 %collective-permute-start.10 = (bf16[8,2,8,64]{3,0,2,1:T(8,128)(2,1)S(1)}, bf16[8,2,8,64]{3,0,2,1:T(8,128)(2,1)}, u32[]{:S(2)}, u32[]{:S(2)}) collective-permute-start(bf16[8,2,8,64]{3,0,2,1:T(8,128)(2,1)S(1)} %bitcast.269), channel_id=1, source_target_pairs={{2,0},{4,2},{6,4},{8,6},{10,8},{12,10},{14,12},{16,14},{18,16},{20... | collective-permute-start | bytes 49160 | tf_op jit(solution)/shard_map/ppermute | solution.py:14
  204.2 32.5 %collective-permute-start.11 = (bf16[8,2,8,64]{3,0,2,1:T(8,128)(2,1)S(1)}, bf16[8,2,8,64]{3,0,2,1:T(8,128)(2,1)}, u32[]{:S(2)}, u32[]{:S(2)}) collective-permute-start(bf16[8,2,8,64]{3,0,2,1:T(8,128)(2,1)S(1)} %bitcast.270), channel_id=1, source_target_pairs={{4,0},{6,2},{8,4},{10,6},{12,8},{14,10},{16,12},{18,14},{20,16},{2... | collective-permute-start | bytes 49160 | tf_op jit(solution)/shard_map/ppermute | solution.py:14
  213.9 32.1 %collective-permute-start.4 = (bf16[8,2,16,64]{3,0,2,1:T(8,128)(2,1)S(1)}, bf16[8,2,16,64]{3,0,2,1:T(8,128)(2,1)}, u32[]{:S(2)}, u32[]{:S(2)}) collective-permute-start(bf16[8,2,16,64]{3,0,2,1:T(8,128)(2,1)S(1)} %bitcast.257), channel_id=1, source_target_pairs={{0,4},{2,6},{4,8},{6,10},{8,12},{10,14},{12,16},{14,18},{16,20},{1... | collective-permute-start | bytes 98312 | tf_op jit(solution)/shard_map/ppermute | solution.py:14
  218.8 29.9 %collective-permute-start.5 = (bf16[8,2,16,64]{3,0,2,1:T(8,128)(2,1)S(1)}, bf16[8,2,16,64]{3,0,2,1:T(8,128)(2,1)}, u32[]{:S(2)}, u32[]{:S(2)}) collective-permute-start(bf16[8,2,16,64]{3,0,2,1:T(8,128)(2,1)S(1)} %bitcast.258), channel_id=1, source_target_pairs={{0,2},{2,4},{4,6},{6,8},{8,10},{10,12},{12,14},{14,16},{16,18},{18... | collective-permute-start | bytes 98312 | tf_op jit(solution)/shard_map/ppermute | solution.py:14
  221.5 45.5 %collective-permute-start.6 = (bf16[8,2,16,64]{3,0,2,1:T(8,128)(2,1)S(1)}, bf16[8,2,16,64]{3,0,2,1:T(8,128)(2,1)}, u32[]{:S(2)}, u32[]{:S(2)}) collective-permute-start(bf16[8,2,16,64]{3,0,2,1:T(8,128)(2,1)S(1)} %bitcast.259), channel_id=1, source_target_pairs={{2,0},{4,2},{6,4},{8,6},{10,8},{12,10},{14,12},{16,14},{18,16},{20... | collective-permute-start | bytes 98312 | tf_op jit(solution)/shard_map/ppermute | solution.py:14
  226.2 41.6 %collective-permute-start.7 = (bf16[8,2,16,64]{3,0,2,1:T(8,128)(2,1)S(1)}, bf16[8,2,16,64]{3,0,2,1:T(8,128)(2,1)}, u32[]{:S(2)}, u32[]{:S(2)}) collective-permute-start(bf16[8,2,16,64]{3,0,2,1:T(8,128)(2,1)S(1)} %bitcast.260), channel_id=1, source_target_pairs={{4,0},{6,2},{8,4},{10,6},{12,8},{14,10},{16,12},{18,14},{20,16},{2... | collective-permute-start | bytes 98312 | tf_op jit(solution)/shard_map/ppermute | solution.py:14
  236.6 16.9 %collective-permute-start = (bf16[8,2,16,64]{3,2,1,0:T(8,128)(2,1)}, bf16[8,2,16,64]{3,2,1,0:T(8,128)(2,1)}, u32[]{:S(2)}, u32[]{:S(2)}) collective-permute-start(bf16[8,2,16,64]{3,2,1,0:T(8,128)(2,1)} %all_gather.21), channel_id=1, source_target_pairs={{0,4},{2,6},{4,8},{6,10},{8,12},{10,14},{12,16},{14,18},{16,20},{1... | collective-permute-start | bytes 98312 | tf_op jit(solution)/shard_map/ppermute | solution.py:14
  239.3 0.7 copy-start.1
  246.0 18.9 %collective-permute-start.1 = (bf16[8,2,16,64]{3,2,1,0:T(8,128)(2,1)}, bf16[8,2,16,64]{3,2,1,0:T(8,128)(2,1)S(1)}, u32[]{:S(2)}, u32[]{:S(2)}) collective-permute-start(bf16[8,2,16,64]{3,2,1,0:T(8,128)(2,1)} %all_gather.21), channel_id=1, source_target_pairs={{0,2},{2,4},{4,6},{6,8},{8,10},{10,12},{12,14},{14,16},{16,18},{18... | collective-permute-start | bytes 98312 | tf_op jit(solution)/shard_map/ppermute | solution.py:14
  248.7 20.0 %collective-permute-start.2 = (bf16[8,2,16,64]{3,2,1,0:T(8,128)(2,1)}, bf16[8,2,16,64]{3,2,1,0:T(8,128)(2,1)S(1)}, u32[]{:S(2)}, u32[]{:S(2)}) collective-permute-start(bf16[8,2,16,64]{3,2,1,0:T(8,128)(2,1)} %all_gather.21), channel_id=1, source_target_pairs={{2,0},{4,2},{6,4},{8,6},{10,8},{12,10},{14,12},{16,14},{18,16},{20... | collective-permute-start | bytes 98312 | tf_op jit(solution)/shard_map/ppermute | solution.py:14
  253.5 21.5 %collective-permute-start.3 = (bf16[8,2,16,64]{3,2,1,0:T(8,128)(2,1)}, bf16[8,2,16,64]{3,2,1,0:T(8,128)(2,1)}, u32[]{:S(2)}, u32[]{:S(2)}) collective-permute-start(bf16[8,2,16,64]{3,2,1,0:T(8,128)(2,1)} %all_gather.21), channel_id=1, source_target_pairs={{4,0},{6,2},{8,4},{10,6},{12,8},{14,10},{16,12},{18,14},{20,16},{2... | collective-permute-start | bytes 98312 | tf_op jit(solution)/shard_map/ppermute | solution.py:14
  277.6 6.5 %copy-start.5 = (pred[16,1024]{1,0:T(8,128)(4,1)S(1)}, pred[16,1024]{1,0:T(8,128)(4,1)}, u32[]{:S(2)}) copy-start(pred[16,1024]{1,0:T(8,128)(4,1)} %broadcast_in_dim.231) | copy-start | bytes 49156
where the time goes:
time: 296 us; the launch traced here: 292 us
  starting transfers between devices  103 us (35%)
  local copies, waits for them, and re-layouts  75.5 us (26%)
  blocking collectives  47.2 us (16%)
  other arithmetic  33.2 us (11%)
  matrix products  32.4 us (11%)
    ppermute x24, starting transfers between devices, passed_along(): lax.ppermute(value, axis, [(source, source + steps) for source in range(i...  103 us
    all_gather x1, blocking collectives, local(): lax.all_gather(coeffs[-1], ('leaf', 'sub'), axis=1, tiled=True)  35.6 us
    gather x31, local copies, waits for them, and re-layouts, select_rows(): picked = jnp.take(values, slot_ids, axis=1)  19.1 us
    dot_general x10, matrix products, downward(): jnp.einsum('vnk,nkc->vnc', incoming.astype(jnp.bfloat16), transfer, prefe...  15.3 us
    select_n x18, other arithmetic, select_rows(): picked = jnp.take(values, slot_ids, axis=1)  15 us
    unnamed x40, local copies, waits for them, and re-layouts  14.7 us
    dot_general x11, matrix products, apply_blocks(): jnp.einsum('vnc,nkc->vnk', operand, blocks, preferred_element_type=jnp.fl...  12.9 us
    and x11, other arithmetic, select_rows(): picked = jnp.take(values, slot_ids, axis=1)  12.8 us
  transfers between devices with their start and end apart: 24, of which 0 were waited for; matrix products, arithmetic and copies ran while one was open for 40% of the time, Pallas kernels for 0%

commit v1 on v0

v1 whole, which is shorter than its diff:
```python
import jax
import jax.numpy as jnp
from jax import lax
from jax.experimental import pallas as pl
from jax.experimental.pallas import tpu as pltpu
from jax.sharding import PartitionSpec as P

NV = 8
K = 64
LEAVES = 16
NEAR = 24
COUP = 16
HEIGHTS = 5
PAIRS = 24
NODES = 2 * PAIRS
LEVEL_OFFSETS = (16, 32, 40, 44, 46)
ZERO = 5 * 2 * NODES
TOP = 126
BF = jnp.bfloat16
F32 = jnp.float32


def dot(a, b):
    return lax.dot_general(a, b, (((1,), (0,)), ((), ())), preferred_element_type=F32)


def dot_t(a, b):
    return lax.dot_general(a, b, (((1,), (1,)), ((), ())), preferred_element_type=F32)


def beside(a, b):
    return jnp.concatenate([a, b], axis=1)


def window_nodes(ids, height, offset, leaf, sub, live):
    shift = 4 - height
    slot = jnp.right_shift(ids, shift)
    node = jnp.bitwise_and(ids, (1 << shift) - 1)
    delta = jnp.right_shift(slot, 1) - 2
    core = jnp.bitwise_and(slot, 1)
    chip = leaf + delta
    near_flip = jnp.bitwise_and(leaf, 1) ^ sub
    far_flip = jnp.bitwise_and(jnp.right_shift(leaf, 1), 1) ^ sub
    place = jnp.where(delta == 1, 1 + near_flip, jnp.where(delta == -1, 2 - near_flip, 0))
    place = jnp.where(delta == 2, 3 + far_flip, jnp.where(delta == -2, 4 - far_flip, place))
    index = (place * 2 + core) * NODES + offset + node
    live = live & (chip >= 0) & (chip < 64)
    index = jnp.where(live, index, ZERO)
    column = lax.broadcasted_iota(jnp.int32, ids.shape, 1)
    return index ^ jnp.bitwise_and(column, 1)


def upward_kernel(
    density, basis, transfer, near_ids, near_count, coupling_ids, pack, roots, near_nodes, coupling_nodes
):
    leaf, sub = lax.axis_index("leaf"), lax.axis_index("sub")
    level = []
    for p in range(8):
        pair = density[:, 128 * p : 128 * p + 128]
        pack[p] = pair
        joined = beside(dot(pair[:, :K], basis[2 * p]), dot(pair[:, K:], basis[2 * p + 1])).astype(BF)
        pack[8 + p] = joined
        level.append(joined)
    row, first = 16, 0
    while len(level) > 1:
        nodes = [dot_t(pair, transfer[first + m]) for m, pair in enumerate(level)]
        first += len(level)
        level = [beside(nodes[q], nodes[q + 1]).astype(BF) for q in range(0, len(nodes), 2)]
        for pair in level:
            pack[row] = pair
            row += 1
    root = dot_t(level[0], transfer[first])
    pack[row] = beside(root, root).astype(BF)
    sent = beside(root[:4], root[4:]).astype(BF)
    roots[...] = jnp.broadcast_to(sent[None], roots.shape)
    slots = lax.broadcasted_iota(jnp.int32, near_ids.shape, 1)
    near_nodes[...] = window_nodes(near_ids[...], 0, 0, leaf, sub, slots < near_count[...])
    for height in range(HEIGHTS):
        count = LEAVES >> height
        at = 2 * LEAVES - 2 * count
        ids = coupling_ids[at : at + count]
        coupling_nodes[at : at + count] = window_nodes(
            ids, height, LEVEL_OFFSETS[height], leaf, sub, ids >= 0
        )


def window_kernel(
    own, near_mine, near_other, far_mine, far_other, near_nodes, coupling_nodes, near_blocks, coupling,
    transfer, basis, partial, onward, window, near_held, coupling_held, near_sems, coupling_sems,
):
    near_copies = [
        pltpu.make_async_copy(near_blocks.at[pl.ds(4 * i, 4)], near_held.at[pl.ds(4 * i, 4)], near_sems.at[i])
        for i in range(4)
    ]
    spans = [(0, 4), (4, 4), (8, 4), (12, 4), (16, 8), (24, 7)]
    coupling_copies = [
        pltpu.make_async_copy(coupling.at[pl.ds(a, n)], coupling_held.at[pl.ds(a, n)], coupling_sems.at[i])
        for i, (a, n) in enumerate(spans)
    ]
    for copy in near_copies + coupling_copies:
        copy.start()
    for place, arrived in enumerate((own, near_mine, near_other, far_mine, far_other)):
        for p in range(2 * PAIRS):
            pair = arrived[p].astype(F32)
            at = 2 * (place * 2 * PAIRS + p)
            window[at] = pair
            window[at + 1] = pltpu.roll(pair, K, 1)
    window[ZERO] = jnp.zeros((NV, 128), F32)
    window[ZERO + 1] = jnp.zeros((NV, 128), F32)
    low = lax.broadcasted_iota(jnp.int32, (NV, 128), 1) < K

    def gathered(nodes, row, slots):
        parts = [
            jnp.where(low, window[nodes[row, j]], window[nodes[row, j + 1]]) for j in range(0, slots, 2)
        ]
        return jnp.concatenate(parts, axis=1).astype(BF)

    near = []
    for i in range(LEAVES):
        if i % 4 == 0:
            near_copies[i // 4].wait()
        near.append(dot_t(gathered(near_nodes, i, NEAR), near_held[i]))
    for i in range(0, LEAVES, 2):
        partial[:, K * i : K * i + 128] = beside(near[i], near[i + 1])
    coupled = []
    starts = {a: i for i, (a, _) in enumerate(spans)}
    for r in range(2 * LEAVES - 1):
        if r in starts:
            coupling_copies[starts[r]].wait()
        coupled.append(dot_t(gathered(coupling_nodes, r, COUP), coupling_held[r]))
    eye = (
        lax.broadcasted_iota(jnp.int32, (K, K), 0) == lax.broadcasted_iota(jnp.int32, (K, K), 1)
    ).astype(F32)
    state = [jnp.concatenate([coupled[30], eye], axis=0)]
    for height in range(HEIGHTS - 1, 0, -1):
        count = LEAVES >> height
        at, offset = 2 * LEAVES - 4 * count, LEAVES - 2 * count
        below = []
        for m in range(count):
            descent = dot(state[m].astype(BF), transfer[offset + m])
            added = beside(coupled[at + 2 * m], coupled[at + 2 * m + 1])
            top = descent[:NV] + added
            rest = descent[NV:]
            for half in (slice(0, K), slice(K, 128)):
                below.append(jnp.concatenate([top[:, half], rest[:, half]], axis=0))
        state = below
    for i in range(0, LEAVES, 2):
        pair = beside(dot_t(state[i].astype(BF), basis[i]), dot_t(state[i + 1].astype(BF), basis[i + 1]))
        span = slice(K * i, K * i + 128)
        partial[:, span] = partial[:, span] + pair[:NV]
        onward[:, span] = pair[NV:].astype(BF)


def top_kernel(
    roots, transfer, coupling, ids, partial, onward, potential, nodes, held, sems
):
    device = lax.axis_index("leaf") * 2 + lax.axis_index("sub")
    firsts = [128 - (128 >> (t - 1)) for t in range(1, 7)]
    rows = [first + jnp.right_shift(device, t) for t, first in enumerate(firsts, 1)]
    copies = [pltpu.make_async_copy(coupling.at[row], held.at[t], sems.at[t]) for t, row in enumerate(rows)]
    for copy in copies:
        copy.start()
    low4 = lax.broadcasted_iota(jnp.int32, (4, 128), 1) < K
    level = []
    for m in range(64):
        a, b = roots[2 * m].astype(F32), roots[2 * m + 1].astype(F32)
        upper = jnp.where(low4, a, pltpu.roll(b, K, 1))
        lower = jnp.where(low4, pltpu.roll(a, K, 1), b)
        level.append(jnp.concatenate([upper, lower], axis=0))
    for first in firsts:
        made = [dot_t(pair.astype(BF), transfer[first + m]) for m, pair in enumerate(level)]
        level = []
        for m in range(0, len(made), 2):
            pair = beside(made[m], made[m + 1]).astype(BF).astype(F32)
            nodes[first + m] = pair
            nodes[first + m + 1] = pltpu.roll(pair, K, 1)
            level.append(pair)
    low = lax.broadcasted_iota(jnp.int32, (NV, 128), 1) < K
    incoming = None
    for t in range(6, 0, -1):
        row = rows[t - 1]
        copies[t - 1].wait()
        first = firsts[t - 1]
        operand = jnp.where(low, nodes[first + ids[row, 0]], nodes[first + (ids[row, 1] ^ 1)])
        coupled = dot_t(operand.astype(BF), held[t - 1])
        incoming = coupled if incoming is None else incoming + coupled
        descent = dot(incoming.astype(BF), transfer[row])
        right = jnp.bitwise_and(jnp.right_shift(device, t - 1), 1) == 1
        incoming = jnp.where(right, descent[:, K:], descent[:, :K])
    potential[...] = partial[...] + dot(incoming.astype(BF), onward[...])


def spec(space):
    return pl.BlockSpec(memory_space=space)


VMEM, SMEM, ANY = pltpu.VMEM, pltpu.SMEM, pl.ANY


def swapped(first, second):
    return [(2 * c, 2 * (first(c) % 64)) for c in range(64)] + [
        (2 * c + 1, 2 * (second(c) % 64) + 1) for c in range(64)
    ]


NEXT = swapped(lambda c: c ^ 1, lambda c: ((c + 1) ^ 1) - 1)
SECOND = swapped(lambda c: c ^ 2, lambda c: ((c + 2) ^ 2) - 2)


def local(
    density, basis, near_ids, near_count, near_blocks, local_transfer, local_coupling, local_coupling_ids,
    top_transfer, top_coupling, top_coupling_ids,
):
    shape = jax.ShapeDtypeStruct
    pack, roots, near_nodes, coupling_nodes = pl.pallas_call(
        upward_kernel,
        out_shape=(
            shape((PAIRS, NV, 128), BF),
            shape((128, 4, 128), BF),
            shape((LEAVES, NEAR), jnp.int32),
            shape((2 * LEAVES - 1, COUP), jnp.int32),
        ),
        in_specs=[spec(VMEM)] * 6,
        out_specs=(spec(VMEM),) * 4,
        name="upward",
    )(density, basis, local_transfer, near_ids, near_count.reshape(LEAVES, 1), local_coupling_ids)
    every = ("leaf", "sub")
    own = lax.all_gather(pack, "sub", axis=0, tiled=True)
    near_mine = lax.ppermute(own, every, NEXT)
    far_mine = lax.ppermute(own, every, SECOND)
    all_roots = lax.all_to_all(roots, every, 0, 0, tiled=True)
    near_other = lax.ppermute(near_mine, "sub", [(0, 1), (1, 0)])
    far_other = lax.ppermute(far_mine, "sub", [(0, 1), (1, 0)])
    partial, onward = pl.pallas_call(
        window_kernel,
        out_shape=(shape((NV, 1024), F32), shape((K, 1024), BF)),
        in_specs=[spec(VMEM)] * 5 + [spec(SMEM)] * 2 + [spec(ANY)] * 2 + [spec(VMEM)] * 2,
        out_specs=(spec(VMEM),) * 2,
        scratch_shapes=[
            pltpu.VMEM((ZERO + 2, NV, 128), F32),
            pltpu.VMEM((LEAVES, 64, NEAR * 64), BF),
            pltpu.VMEM((2 * LEAVES - 1, K, COUP * K), BF),
            pltpu.SemaphoreType.DMA((4,)),
            pltpu.SemaphoreType.DMA((6,)),
        ],
        compiler_params=pltpu.CompilerParams(vmem_limit_bytes=24 << 20),
        cost_estimate=pl.CostEstimate(flops=120_000_000, bytes_accessed=8_000_000, transcendentals=0),
        name="window",
    )(
        own, near_mine, near_other, far_mine, far_other, near_nodes, coupling_nodes, near_blocks,
        local_coupling, local_transfer, basis,
    )
    return pl.pallas_call(
        top_kernel,
        out_shape=shape((NV, 1024), F32),
        in_specs=[spec(VMEM), spec(VMEM), spec(ANY), spec(SMEM), spec(VMEM), spec(VMEM)],
        out_specs=spec(VMEM),
        scratch_shapes=[
            pltpu.VMEM((TOP, NV, 128), F32),
            pltpu.VMEM((6, K, 128), BF),
            pltpu.SemaphoreType.DMA((6,)),
        ],
        compiler_params=pltpu.CompilerParams(vmem_limit_bytes=16 << 20),
        name="top",
    )(all_roots, top_transfer, top_coupling, top_coupling_ids, partial, onward)


def solution(mesh):
    in_specs = (
        P(None, ("leaf", "sub")),
        P(("leaf", "sub"), None, None),
        P(("leaf", "sub"), None),
        P(("leaf", "sub")),
        P(("leaf", "sub"), None, None),
        P(("leaf", "sub"), None, None),
        P(("leaf", "sub"), None, None),
        P(("leaf", "sub"), None),
        P(),
        P(),
        P(),
    )
    out_specs = P(None, ("leaf", "sub"))
    return jax.shard_map(local, mesh=mesh, in_specs=in_specs, out_specs=out_specs, check_vma=False)
```

time: 296 us -> 50.8 us (0.17)
  the two profiles are of different devices: /device:TPU:36 before, /device:TPU:1 now
where the time goes in v1:
time: 50.8 us; the launch traced here: 50.3 us
  starting transfers between devices  18.2 us (36%)
  Pallas kernels  16.1 us (32%)
  local copies, waits for them, and re-layouts  12.4 us (24%)
  blocking collectives  3.15 us (6%)
    unnamed x18, local copies, waits for them, and re-layouts  11.1 us
    ppermute x1, starting transfers between devices, local(): near_mine = lax.ppermute(own, every, NEXT)  8.49 us
    all_to_all x1, starting transfers between devices, local(): all_roots = lax.all_to_all(roots, every, 0, 0, tiled=True)  7.93 us
    pallas_call x1, Pallas kernels, local(): pl.pallas_call(top_kernel, out_shape=shape((NV, 1024), F32), in_specs=[sp...  7.02 us
    pallas_call x1, Pallas kernels, local(): pl.pallas_call(window_kernel, out_shape=(shape((NV, 1024), F32), shape((K...  6.25 us
    all_gather x1, blocking collectives, local(): own = lax.all_gather(pack, 'sub', axis=0, tiled=True)  3.15 us
    pallas_call x1, Pallas kernels, local(): pl.pallas_call(upward_kernel, out_shape=(shape((PAIRS, NV, 128), BF), sha...  2.8 us
    reshape x1, local copies, waits for them, and re-layouts, local(): near_count.reshape(LEAVES, 1)  1.32 us
  transfers between devices with their start and end apart: 5, of which 1 were waited for; matrix products, arithmetic and copies ran while one was open for 2% of the time, Pallas kernels for 12%

profile of v1, /device:TPU:1, one launch (start us, length us, event | category | flops | bytes accessed | tf_op | source)
XLA Modules:
  0.0 50.3 jit_solution(16104579660515373516)
XLA Ops:
  0.0 1.4 %copy.16.coupling_ids = s32[31,16]{1,0:T(8,128)} copy(s32[31,16]{0,1:T(8,128)} %param.18) | data formatting | bytes 3968 | tf_op args[7]
  1.4 1.3 %copy.15.near_count = s32[16,1]{1,0:T(8,128)} copy(s32[16,1]{0,1:T(1,128)} %bitcast.1) | data formatting | bytes 128 | tf_op jit(solution)/shard_map/reshape | solution.py:226
  2.7 2.8 %upward.1 = (bf16[24,8,128]{2,1,0:T(8,128)(2,1)}, bf16[128,4,128]{2,1,0:T(4,128)(2,1)}, s32[16,24]{1,0:T(8,128)}, s32[31,16]{1,0:T(8,128)}) custom-call(bf16[8,1024]{1,0:T(8,128)(2,1)} %density.1, bf16[16,64,64]{2,1,0:T(8,128)(2,1)} %basis.3, bf16[15,64,128]{2,1,0:T(8,128)(2,1)} %transfer.4, s32[16,24]{1,0:T(8,128)} %near_ids.1, s32[16,1]{1,0:T(8,128)} %copy.15.near_count, ...), custom_call_target="tpu_custom_call" | custom-call | tf_op jit(solution)/shard_map/upward/pallas_call | solution.py:215
  5.5 3.1 %all_gather.3.own = bf16[48,8,128]{2,1,0:T(8,128)(2,1)S(1)} all-gather(bf16[24,8,128]{2,1,0:T(8,128)(2,1)} %get-tuple-element.12), channel_id=1, replica_groups=mesh['leaf'=64,'sub'=2] {'sub'}, dimensions={0}, use_global_device_ids=true | all-gather | bytes 147456 | tf_op jit(solution)/shard_map/all_gather | solution.py:228
  8.7 8.5 %collective-permute-start = (bf16[48,8,128]{2,1,0:T(8,128)(2,1)S(1)}, bf16[48,8,128]{2,1,0:T(8,128)(2,1)S(1)}, u32[]{:S(2)}, u32[]{:S(2)}) collective-permute-start(bf16[48,8,128]{2,1,0:T(8,128)(2,1)S(1)} %all_gather.3.own), channel_id=1, source_target_pairs={{0,2},{2,0},{4,6},{6,4},{8,10},{10,8},{12,14},{14,12},{16,18},{18,... | collective-permute-start | bytes 294920 | tf_op jit(solution)/shard_map/ppermute | solution.py:229
  17.1 0.5 %collective-permute-start.2 = (bf16[48,8,128]{2,1,0:T(8,128)(2,1)S(1)}, bf16[48,8,128]{2,1,0:T(8,128)(2,1)S(1)}, u32[]{:S(2)}, u32[]{:S(2)}) collective-permute-start(bf16[48,8,128]{2,1,0:T(8,128)(2,1)S(1)} %all_gather.3.own), channel_id=1, source_target_pairs={{0,4},{2,6},{4,0},{6,2},{8,12},{10,14},{12,8},{14,10},{16,20},{18,... | collective-permute-start | bytes 294920 | tf_op jit(solution)/shard_map/ppermute | solution.py:230
  17.7 7.9 %all-to-all-start = ((bf16[128,4,128]{2,1,0:T(4,128)(2,1)}), bf16[128,4,128]{2,1,0:T(4,128)(2,1)S(1)}, u32[]{:S(2)}, u32[]{:S(2)}) async-start(bf16[128,4,128]{2,1,0:T(4,128)(2,1)} %get-tuple-element.11), calls=%async_computation | async-start | bytes 262144 | tf_op jit(solution)/shard_map/all_to_all | solution.py:231
  25.6 0.0 collective-permute-done.near_mine
  25.6 1.1 %collective-permute-start.1 = (bf16[48,8,128]{2,1,0:T(8,128)(2,1)S(1)}, bf16[48,8,128]{2,1,0:T(8,128)(2,1)S(1)}, u32[]{:S(2)}, u32[]{:S(2)}) collective-permute-start(bf16[48,8,128]{2,1,0:T(8,128)(2,1)S(1)} %collective-permute-done.near_mine), channel_id=1, source_target_pairs={{0,1},{1,0},{2,3},{3,2},{4,5},{5,4},{6,7},{7,6},{8,9},{9,8},{10,11... | collective-permute-start | bytes 294920 | tf_op jit(solution)/shard_map/ppermute | solution.py:232
  26.8 0.0 collective-permute-done.2.far_mine
  26.8 0.1 collective-permute-start.3
  26.9 0.8 %copy.17.ids = s32[126,2]{1,0:T(8,128)S(1)} copy(s32[126,2]{0,1:T(2,128)} %param.21) | data formatting | bytes 2016 | tf_op args[10]
  27.7 0.0 collective-permute-done.1.near_other
  27.7 0.4 collective-permute-done.3.far_other
  28.1 0.0 copy-start
  28.1 2.1 %copy-done = bf16[31,64,1024]{2,1,0:T(8,128)(2,1)S(1)} copy-done((bf16[31,64,1024]{2,1,0:T(8,128)(2,1)S(1)}, bf16[31,64,1024]{2,1,0:T(8,128)(2,1)}, u32[]{:S(2)}) %copy-start) | copy-done | bytes 4063256
  30.2 0.0 copy-start.1
  30.2 1.9 %copy-done.1 = bf16[16,64,1536]{2,1,0:T(8,128)(2,1)S(1)} copy-done((bf16[16,64,1536]{2,1,0:T(8,128)(2,1)S(1)}, bf16[16,64,1536]{2,1,0:T(8,128)(2,1)}, u32[]{:S(2)}) %copy-start.1) | copy-done | bytes 3145752
  32.1 0.0 copy-start.4
  32.1 0.9 %copy-done.4 = bf16[16,64,64]{2,1,0:T(8,128)(2,1)S(1)} copy-done((bf16[16,64,64]{2,1,0:T(8,128)(2,1)S(1)}, bf16[16,64,64]{2,1,0:T(8,128)(2,1)}, u32[]{:S(2)}) %copy-start.4) | copy-done | bytes 131096
  33.1 0.0 copy-start.5
  33.1 0.9 %copy-done.5 = bf16[15,64,128]{2,1,0:T(8,128)(2,1)S(1)} copy-done((bf16[15,64,128]{2,1,0:T(8,128)(2,1)S(1)}, bf16[15,64,128]{2,1,0:T(8,128)(2,1)}, u32[]{:S(2)}) %copy-start.5) | copy-done | bytes 245784
  34.0 0.0 copy-start.6
  34.0 0.7 %copy-done.6 = s32[31,16]{1,0:T(8,128)S(1)} copy-done((s32[31,16]{1,0:T(8,128)S(1)}, s32[31,16]{1,0:T(8,128)}, u32[]{:S(2)}) %copy-start.6) | copy-done | bytes 2008
  34.7 0.7 %copy-done.7 = s32[16,24]{1,0:T(8,128)S(1)} copy-done((s32[16,24]{1,0:T(8,128)S(1)}, s32[16,24]{1,0:T(8,128)}, u32[]{:S(2)}) %copy-start.7) | copy-done | bytes 1560
  35.4 0.0 copy-start.2
  35.4 6.2 %window.1 = (f32[8,1024]{1,0:T(8,128)S(1)}, bf16[64,1024]{1,0:T(8,128)(2,1)S(1)}) custom-call(bf16[48,8,128]{2,1,0:T(8,128)(2,1)S(1)} %all_gather.3.own, bf16[48,8,128]{2,1,0:T(8,128)(2,1)S(1)} %collective-permute-done.near_mine, bf16[48,8,128]{2,1,0:T(8,128)(2,1)S(1)} %collective-permute-done.1.near_other, ...), custom_call_target="tpu_custom_call" | custom-call | flops 120000000 | bytes 8000000 | tf_op jit(solution)/shard_map/window/pallas_call | solution.py:234
  41.7 0.0 all-to-all-done.roots
  41.7 0.0 copy-done.2
  41.7 0.0 copy-start.3
  41.7 1.6 %copy-done.3 = bf16[126,64,128]{2,1,0:T(8,128)(2,1)S(1)} copy-done((bf16[126,64,128]{2,1,0:T(8,128)(2,1)S(1)}, bf16[126,64,128]{2,1,0:T(8,128)(2,1)}, u32[]{:S(2)}) %copy-start.3) | copy-done | bytes 2064408
  43.3 7.0 %top.1 = f32[8,1024]{1,0:T(8,128)} custom-call(bf16[128,4,128]{2,1,0:T(4,128)(2,1)S(1)} %all-to-all-done.roots, bf16[126,64,128]{2,1,0:T(8,128)(2,1)S(1)} %copy-done.2, bf16[126,64,128]{2,1,0:T(8,128)(2,1)S(1)} %copy-done.3, s32[126,2]{1,0:T(8,128)S(1)} %copy.17.ids, f32[8,1024]{1,0:T(8,128)S(1)} %get-tuple-element.15.partial, ...), custom_call_target="tpu_custom_call" | custom-call | tf_op jit(solution)/shard_map/top/pallas_call | solution.py:253
  (1 shorter events, 0.0 us)
Async XLA Ops:
  8.7 16.9 %collective-permute-start = (bf16[48,8,128]{2,1,0:T(8,128)(2,1)S(1)}, bf16[48,8,128]{2,1,0:T(8,128)(2,1)S(1)}, u32[]{:S(2)}, u32[]{:S(2)}) collective-permute-start(bf16[48,8,128]{2,1,0:T(8,128)(2,1)S(1)} %all_gather.3.own), channel_id=1, source_target_pairs={{0,2},{2,0},{4,6},{6,4},{8,10},{10,8},{12,14},{14,12},{16,18},{18,... | collective-permute-start | bytes 294920 | tf_op jit(solution)/shard_map/ppermute | solution.py:229
  17.1 9.6 %collective-permute-start.2 = (bf16[48,8,128]{2,1,0:T(8,128)(2,1)S(1)}, bf16[48,8,128]{2,1,0:T(8,128)(2,1)S(1)}, u32[]{:S(2)}, u32[]{:S(2)}) collective-permute-start(bf16[48,8,128]{2,1,0:T(8,128)(2,1)S(1)} %all_gather.3.own), channel_id=1, source_target_pairs={{0,4},{2,6},{4,0},{6,2},{8,12},{10,14},{12,8},{14,10},{16,20},{18,... | collective-permute-start | bytes 294920 | tf_op jit(solution)/shard_map/ppermute | solution.py:230
  17.7 24.0 %all-to-all-start = ((bf16[128,4,128]{2,1,0:T(4,128)(2,1)}), bf16[128,4,128]{2,1,0:T(4,128)(2,1)S(1)}, u32[]{:S(2)}, u32[]{:S(2)}) async-start(bf16[128,4,128]{2,1,0:T(4,128)(2,1)} %get-tuple-element.11), calls=%async_computation | async-start | bytes 262144 | tf_op jit(solution)/shard_map/all_to_all | solution.py:231
  25.6 2.1 %collective-permute-start.1 = (bf16[48,8,128]{2,1,0:T(8,128)(2,1)S(1)}, bf16[48,8,128]{2,1,0:T(8,128)(2,1)S(1)}, u32[]{:S(2)}, u32[]{:S(2)}) collective-permute-start(bf16[48,8,128]{2,1,0:T(8,128)(2,1)S(1)} %collective-permute-done.near_mine), channel_id=1, source_target_pairs={{0,1},{1,0},{2,3},{3,2},{4,5},{5,4},{6,7},{7,6},{8,9},{9,8},{10,11... | collective-permute-start | bytes 294920 | tf_op jit(solution)/shard_map/ppermute | solution.py:232
  26.8 1.3 %collective-permute-start.3 = (bf16[48,8,128]{2,1,0:T(8,128)(2,1)S(1)}, bf16[48,8,128]{2,1,0:T(8,128)(2,1)S(1)}, u32[]{:S(2)}, u32[]{:S(2)}) collective-permute-start(bf16[48,8,128]{2,1,0:T(8,128)(2,1)S(1)} %collective-permute-done.2.far_mine), channel_id=1, source_target_pairs={{0,1},{1,0},{2,3},{3,2},{4,5},{5,4},{6,7},{7,6},{8,9},{9,8},{10,11... | collective-permute-start | bytes 294920 | tf_op jit(solution)/shard_map/ppermute | solution.py:233
  28.1 2.2 %copy-start = (bf16[31,64,1024]{2,1,0:T(8,128)(2,1)S(1)}, bf16[31,64,1024]{2,1,0:T(8,128)(2,1)}, u32[]{:S(2)}) copy-start(bf16[31,64,1024]{2,1,0:T(8,128)(2,1)} %coupling.2) | copy-start | bytes 12189700
  30.2 1.9 %copy-start.1 = (bf16[16,64,1536]{2,1,0:T(8,128)(2,1)S(1)}, bf16[16,64,1536]{2,1,0:T(8,128)(2,1)}, u32[]{:S(2)}) copy-start(bf16[16,64,1536]{2,1,0:T(8,128)(2,1)} %near_blocks.1) | copy-start | bytes 9437188
  32.1 0.9 %copy-start.4 = (bf16[16,64,64]{2,1,0:T(8,128)(2,1)S(1)}, bf16[16,64,64]{2,1,0:T(8,128)(2,1)}, u32[]{:S(2)}) copy-start(bf16[16,64,64]{2,1,0:T(8,128)(2,1)} %basis.3) | copy-start | bytes 393220
  33.1 0.9 %copy-start.5 = (bf16[15,64,128]{2,1,0:T(8,128)(2,1)S(1)}, bf16[15,64,128]{2,1,0:T(8,128)(2,1)}, u32[]{:S(2)}) copy-start(bf16[15,64,128]{2,1,0:T(8,128)(2,1)} %transfer.4) | copy-start | bytes 737284
  34.0 0.7 %copy-start.6 = (s32[31,16]{1,0:T(8,128)S(1)}, s32[31,16]{1,0:T(8,128)}, u32[]{:S(2)}) copy-start(s32[31,16]{1,0:T(8,128)} %get-tuple-element.14.coupling_nodes) | copy-start | bytes 5956
  34.7 0.7 %copy-start.7 = (s32[16,24]{1,0:T(8,128)S(1)}, s32[16,24]{1,0:T(8,128)}, u32[]{:S(2)}) copy-start(s32[16,24]{1,0:T(8,128)} %get-tuple-element.13.near_nodes) | copy-start | bytes 4612
  35.4 6.3 %copy-start.2 = (bf16[126,64,128]{2,1,0:T(8,128)(2,1)S(1)}, bf16[126,64,128]{2,1,0:T(8,128)(2,1)}, u32[]{:S(2)}) copy-start(bf16[126,64,128]{2,1,0:T(8,128)(2,1)} %transfer.5) | copy-start | bytes 6193156
  41.7 1.6 %copy-start.3 = (bf16[126,64,128]{2,1,0:T(8,128)(2,1)S(1)}, bf16[126,64,128]{2,1,0:T(8,128)(2,1)}, u32[]{:S(2)}) copy-start(bf16[126,64,128]{2,1,0:T(8,128)(2,1)} %coupling.3) | copy-start | bytes 6193156

commit v2 on v1

v2 whole, which is shorter than its diff:
```python
import jax
import jax.numpy as jnp
from jax import lax
from jax.experimental import pallas as pl
from jax.experimental.pallas import tpu as pltpu
from jax.sharding import PartitionSpec as P

NV = 8
K = 64
LEAVES = 16
NEAR = 24
COUP = 16
HEIGHTS = 5
PAIRS = 24
NODES = 2 * PAIRS
LEVEL_OFFSETS = (16, 32, 40, 44, 46)
ZERO = 5 * 2 * NODES
TOP = 126
AHEAD = 3
FIRSTS = (0, 64, 96, 112, 120, 124)
BF = jnp.bfloat16
F32 = jnp.float32


def dot(a, b):
    return lax.dot_general(a, b, (((1,), (0,)), ((), ())), preferred_element_type=F32)


def dot_t(a, b):
    return lax.dot_general(a, b, (((1,), (1,)), ((), ())), preferred_element_type=F32)


def unit(n):
    return (lax.broadcasted_iota(jnp.int32, (n, n), 0) == lax.broadcasted_iota(jnp.int32, (n, n), 1)).astype(BF)


def stacked(*parts):
    return jnp.concatenate(parts, axis=0)


def turned(columns):
    high = columns.astype(BF)
    rest = (columns - high.astype(F32)).astype(BF)
    return dot_t(unit(NV), high) + dot_t(unit(NV), rest)


def beside(a, b):
    return jnp.concatenate([a, b], axis=1)


def window_nodes(ids, height, offset, leaf, sub, live, slot_axis):
    shift = jnp.broadcast_to(4 - height, ids.shape)
    slot = jnp.right_shift(ids, shift)
    node = ids - jnp.left_shift(slot, shift)
    delta = jnp.right_shift(slot, 1) - 2
    core = jnp.bitwise_and(slot, 1)
    chip = leaf + delta
    near_flip = jnp.bitwise_and(leaf, 1) ^ sub
    far_flip = jnp.bitwise_and(jnp.right_shift(leaf, 1), 1) ^ sub
    place = jnp.where(delta == 1, 1 + near_flip, jnp.where(delta == -1, 2 - near_flip, 0))
    place = jnp.where(delta == 2, 3 + far_flip, jnp.where(delta == -2, 4 - far_flip, place))
    index = (place * 2 + core) * NODES + offset + node
    live = live & (chip >= 0) & (chip < 64)
    index = jnp.where(live, index, ZERO)
    column = lax.broadcasted_iota(jnp.int32, ids.shape, slot_axis)
    return index ^ jnp.bitwise_and(column, 1)


def upward_kernel(
    density, basis, transfer, near_ids, near_count, coupling_ids, pack, roots, near_nodes, coupling_nodes
):
    leaf, sub = lax.axis_index("leaf"), lax.axis_index("sub")
    level = []
    for p in range(8):
        pair = density[:, 128 * p : 128 * p + 128]
        pack[p] = pair
        joined = beside(dot(pair[:, :K], basis[2 * p]), dot(pair[:, K:], basis[2 * p + 1])).astype(BF)
        pack[8 + p] = joined
        level.append(joined)
    made = [dot_t(transfer[m], pair).astype(BF) for m, pair in enumerate(level)]
    columns, first = list(made), 8
    while len(made) > 1:
        made = [
            dot(transfer[first + q], stacked(made[2 * q], made[2 * q + 1])).astype(BF)
            for q in range(len(made) // 2)
        ]
        first += len(made)
        columns += made
    rows = dot_t(unit(NV), stacked(*columns))
    for q in range(7):
        pack[16 + q] = rows[:, 128 * q : 128 * q + 128].astype(BF)
    root = rows[:, 896:]
    pack[23] = beside(root, root).astype(BF)
    sent = beside(root[:4], root[4:]).astype(BF)
    roots[...] = jnp.broadcast_to(sent[None], roots.shape)
    slots = lax.broadcasted_iota(jnp.int32, near_ids.shape, 1)
    diagonal = lax.broadcasted_iota(jnp.int32, (LEAVES, LEAVES), 0) == lax.broadcasted_iota(
        jnp.int32, (LEAVES, LEAVES), 1
    )
    counts = jnp.sum(jnp.where(diagonal, near_count[...], 0), axis=1, keepdims=True)
    near_nodes[...] = window_nodes(near_ids[...], 0, 0, leaf, sub, slots < counts, 1)
    ids = coupling_ids[...]
    rows = lax.broadcasted_iota(jnp.int32, ids.shape, 1)
    height = sum((rows >= 2 * LEAVES - 2 * (LEAVES >> h)).astype(jnp.int32) for h in range(1, HEIGHTS))
    offset = jnp.zeros(ids.shape, jnp.int32)
    for h, place in enumerate(LEVEL_OFFSETS):
        offset = jnp.where(height == h, place, offset)
    coupling_nodes[...] = window_nodes(ids, height, offset, leaf, sub, ids >= 0, 0)


def window_kernel(
    own, near_mine, near_other, far_mine, far_other, near_nodes, coupling_nodes, near_blocks, coupling,
    transfer, basis, top_transfer, top_coupling, partial, onward, shares, window, arrived, near_ids,
    coupling_ids, near_held, coupling_held, transfer_held, basis_held, rows_held, links_held, id_sems,
    arrival_sems, near_sems, coupling_sems, small_sems, row_sems, link_sems,
):
    device = lax.axis_index("leaf") * 2 + lax.axis_index("sub")
    copy = pltpu.make_async_copy
    id_copies = [copy(coupling_nodes, coupling_ids, id_sems.at[0]), copy(near_nodes, near_ids, id_sems.at[1])]
    arrivals = [
        copy(source, arrived.at[i], arrival_sems.at[i])
        for i, source in enumerate((own, near_mine, near_other, far_mine, far_other))
    ]
    small_copies = [copy(transfer, transfer_held, small_sems.at[0]), copy(basis, basis_held, small_sems.at[1])]
    places = [first + jnp.right_shift(device, t) for t, first in enumerate(FIRSTS, 1)]
    row_copies = [copy(top_transfer.at[row], rows_held.at[t], row_sems.at[t]) for t, row in enumerate(places)]
    link_copies = [copy(top_coupling.at[row], links_held.at[t], link_sems.at[t]) for t, row in enumerate(places)]
    coupling_copies = [
        copy(coupling.at[pl.ds(a, n)], coupling_held.at[pl.ds(a, n)], coupling_sems.at[i])
        for i, (a, n) in enumerate(((16, 15), (0, 16)))
    ]
    near_copies = [
        copy(near_blocks.at[pl.ds(a, 8)], near_held.at[pl.ds(a, 8)], near_sems.at[a // 8])
        for a in range(0, LEAVES, 8)
    ]
    queue = coupling_copies + near_copies
    for one in id_copies + arrivals + queue[:1] + row_copies + link_copies + small_copies + queue[1:AHEAD]:
        one.start()

    def take(index):
        queue[index].wait()
        if index + AHEAD < len(queue):
            queue[index + AHEAD].start()

    window[ZERO] = jnp.zeros((NV, 128), F32)
    window[ZERO + 1] = jnp.zeros((NV, 128), F32)
    for one in arrivals:
        one.wait()
    for place in range(5):
        for p in range(2 * PAIRS):
            pair = arrived[place, p].astype(F32)
            at = 2 * (place * 2 * PAIRS + p)
            window[at] = pair
            window[at + 1] = pltpu.roll(pair, K, 1)
    low = lax.broadcasted_iota(jnp.int32, (NV, 128), 1) < K

    def gathered(node, slots):
        parts = [jnp.where(low, window[node(j)], window[node(j + 1)]) for j in range(0, slots, 2)]
        return jnp.concatenate(parts, axis=1).astype(BF)

    def coupled(r):
        return dot_t(gathered(lambda j: coupling_ids[j, r], COUP), coupling_held[r])

    def near(i):
        return dot_t(gathered(lambda j: near_ids[i, j], NEAR), near_held[i])

    def descend(node, transfer_row, first):
        return dot(node.astype(BF), transfer_held[transfer_row]), beside(coupled_rows[first], coupled_rows[first + 1])

    def split(descent, added):
        top, rest = descent[:NV] + added, descent[NV:]
        return [stacked(top[:, :K], rest[:, :K]), stacked(top[:, K:], rest[:, K:])]

    def level(state, height):
        count = LEAVES >> height
        at, offset = 2 * LEAVES - 4 * count, LEAVES - 2 * count
        made = [descend(state[m], offset + m, at + 2 * m) for m in range(count)]
        return [child for one in made for child in split(*one)]

    for one in id_copies + row_copies + link_copies + small_copies:
        one.wait()
    coupled_rows = {}
    path = unit(K)
    take(0)
    for t in range(6):
        right = jnp.bitwise_and(jnp.right_shift(device, t), 1) == 1
        step = jnp.where(right, rows_held[t, :, K:], rows_held[t, :, :K])
        path = dot_t(path, step).astype(BF)
        for r in range(30 - 3 * t, max(27 - 3 * t, 15), -1):
            coupled_rows[r] = coupled(r)
        shares[:, 128 * t : 128 * t + 128] = dot(path, links_held[t]).astype(BF)
    state = [stacked(coupled_rows[30], unit(K).astype(F32))]
    take(1)
    for height in (4, 3, 2):
        state = level(state, height)
        for r in range(5 * (4 - height), 5 * (4 - height) + 5):
            coupled_rows[r] = coupled(r)
    coupled_rows[15] = coupled(15)
    take(2)
    near_rows = [near(i) for i in range(2)]
    state = level(state, 1)
    near_rows += [near(i) for i in range(2, 8)]
    ends = [dot_t(state[i].astype(BF), basis_held[i]) for i in range(LEAVES)]
    take(3)
    near_rows += [near(i) for i in range(8, LEAVES)]
    for i in range(0, LEAVES, 2):
        span = slice(K * i, K * i + 128)
        pair = beside(ends[i], ends[i + 1])
        partial[:, span] = pair[:NV] + beside(near_rows[i], near_rows[i + 1])
        onward[:, span] = pair[NV:].astype(BF)


def top_kernel(
    roots, transfer, ids, partial, onward, shares, potential, nodes, held_ids, held, roots_held, partial_held,
    onward_held, shares_held, sems,
):
    device = lax.axis_index("leaf") * 2 + lax.axis_index("sub")
    copy = pltpu.make_async_copy
    root_copy = copy(roots, roots_held, sems.at[0])
    spans = ((0, 32), (32, 32), (64, 62))
    copies = [
        copy(transfer.at[pl.ds(a, n)], held.at[pl.ds(a, n)], sems.at[1 + i]) for i, (a, n) in enumerate(spans)
    ]
    id_copy = copy(ids, held_ids, sems.at[4])
    last_copies = [
        copy(shares, shares_held, sems.at[5]),
        copy(onward, onward_held, sems.at[6]),
        copy(partial, partial_held, sems.at[7]),
    ]
    for one in [root_copy] + copies + [id_copy] + last_copies:
        one.start()
    low4 = lax.broadcasted_iota(jnp.int32, (4, 128), 1) < K
    root_copy.wait()
    made = []
    for m in range(64):
        a, b = roots_held[2 * m].astype(F32), roots_held[2 * m + 1].astype(F32)
        upper = jnp.where(low4, a, pltpu.roll(b, K, 1))
        lower = jnp.where(low4, pltpu.roll(a, K, 1), b)
        if m % 32 == 0:
            copies[m // 32].wait()
        made.append(dot_t(held[m], stacked(upper, lower).astype(BF)).astype(BF))
    copies[2].wait()
    for t, first in enumerate(FIRSTS):
        if t:
            made = [
                dot(held[first + m], stacked(made[2 * m], made[2 * m + 1])).astype(BF)
                for m in range(len(made) // 2)
            ]
        for m, node in enumerate(made):
            nodes[first + m] = node
    id_copy.wait()
    sources = []
    for t, first in enumerate(FIRSTS, 1):
        row = first + jnp.right_shift(device, t)
        sources += [nodes[first + held_ids[0, row]], nodes[first + held_ids[1, row]]]
    for one in last_copies:
        one.wait()
    incoming = dot(shares_held[...], stacked(*sources)).astype(BF)
    incoming = dot_t(unit(NV), incoming).astype(BF)
    potential[...] = partial_held[...] + dot(incoming, onward_held[...])


def spec(space):
    return pl.BlockSpec(memory_space=space)


VMEM, SMEM, ANY = pltpu.VMEM, pltpu.SMEM, pl.ANY


def swapped(first, second):
    return [(2 * c, 2 * (first(c) % 64)) for c in range(64)] + [
        (2 * c + 1, 2 * (second(c) % 64) + 1) for c in range(64)
    ]


NEXT = swapped(lambda c: c ^ 1, lambda c: ((c + 1) ^ 1) - 1)
SECOND = swapped(lambda c: c ^ 2, lambda c: ((c + 2) ^ 2) - 2)


def local(
    density, basis, near_ids, near_count, near_blocks, local_transfer, local_coupling, local_coupling_ids,
    top_transfer, top_coupling, top_coupling_ids,
):
    shape = jax.ShapeDtypeStruct
    pack, roots, near_nodes, coupling_nodes = pl.pallas_call(
        upward_kernel,
        out_shape=(
            shape((PAIRS, NV, 128), BF),
            shape((128, 4, 128), BF),
            shape((LEAVES, NEAR), jnp.int32),
            shape((COUP, 2 * LEAVES - 1), jnp.int32),
        ),
        in_specs=[spec(VMEM)] * 6,
        out_specs=(spec(VMEM),) * 4,
        cost_estimate=pl.CostEstimate(flops=20_000_000, bytes_accessed=1_000_000, transcendentals=0),
        compiler_params=pltpu.CompilerParams(vmem_limit_bytes=56 << 20),
        name="upward",
    )(density, basis, local_transfer, near_ids, near_count.reshape(1, LEAVES), local_coupling_ids.T)
    every = ("leaf", "sub")
    own = lax.all_gather(pack, "sub", axis=0, tiled=True)
    near_mine = lax.ppermute(own, every, NEXT)
    far_mine = lax.ppermute(own, every, SECOND)
    all_roots = lax.all_to_all(roots, every, 0, 0, tiled=True)
    near_other = lax.ppermute(near_mine, "sub", [(0, 1), (1, 0)])
    far_other = lax.ppermute(far_mine, "sub", [(0, 1), (1, 0)])
    partial, onward, shares = pl.pallas_call(
        window_kernel,
        out_shape=(
            shape((NV, 1024), F32),
            shape((K, 1024), BF),
            shape((K, 768), BF),
        ),
        in_specs=[spec(ANY)] * 13,
        out_specs=(spec(VMEM),) * 3,
        scratch_shapes=[
            pltpu.VMEM((ZERO + 2, NV, 128), F32),
            pltpu.VMEM((5, 2 * PAIRS, NV, 128), BF),
            pltpu.SMEM((LEAVES, NEAR), jnp.int32),
            pltpu.SMEM((COUP, 2 * LEAVES - 1), jnp.int32),
            pltpu.VMEM((LEAVES, 64, NEAR * 64), BF),
            pltpu.VMEM((2 * LEAVES - 1, K, COUP * K), BF),
            pltpu.VMEM((LEAVES - 1, K, 128), BF),
            pltpu.VMEM((LEAVES, 64, K), BF),
            pltpu.VMEM((6, K, 128), BF),
            pltpu.VMEM((6, K, 128), BF),
            pltpu.SemaphoreType.DMA((2,)),
            pltpu.SemaphoreType.DMA((5,)),
            pltpu.SemaphoreType.DMA((4,)),
            pltpu.SemaphoreType.DMA((3,)),
            pltpu.SemaphoreType.DMA((2,)),
            pltpu.SemaphoreType.DMA((6,)),
            pltpu.SemaphoreType.DMA((6,)),
        ],
        compiler_params=pltpu.CompilerParams(vmem_limit_bytes=56 << 20),
        cost_estimate=pl.CostEstimate(flops=120_000_000, bytes_accessed=8_000_000, transcendentals=0),
        name="window",
    )(
        own, near_mine, near_other, far_mine, far_other, near_nodes, coupling_nodes, near_blocks,
        local_coupling, local_transfer, basis, top_transfer, top_coupling,
    )
    return pl.pallas_call(
        top_kernel,
        out_shape=shape((NV, 1024), F32),
        in_specs=[spec(ANY)] * 6,
        out_specs=spec(VMEM),
        scratch_shapes=[
            pltpu.VMEM((TOP, K, NV), BF),
            pltpu.SMEM((2, TOP), jnp.int32),
            pltpu.VMEM((TOP, K, 128), BF),
            pltpu.VMEM((128, 4, 128), BF),
            pltpu.VMEM((NV, 1024), F32),
            pltpu.VMEM((K, 1024), BF),
            pltpu.VMEM((K, 768), BF),
            pltpu.SemaphoreType.DMA((8,)),
        ],
        compiler_params=pltpu.CompilerParams(vmem_limit_bytes=56 << 20),
        name="top",
    )(all_roots, top_transfer, top_coupling_ids.T, partial, onward, shares)


def solution(mesh):
    in_specs = (
        P(None, ("leaf", "sub")),
        P(("leaf", "sub"), None, None),
        P(("leaf", "sub"), None),
        P(("leaf", "sub")),
        P(("leaf", "sub"), None, None),
        P(("leaf", "sub"), None, None),
        P(("leaf", "sub"), None, None),
        P(("leaf", "sub"), None),
        P(),
        P(),
        P(),
    )
    out_specs = P(None, ("leaf", "sub"))
    return jax.shard_map(local, mesh=mesh, in_specs=in_specs, out_specs=out_specs, check_vma=False)
```

time: 50.8 us -> 37.6 us (0.74)
  local copies, waits for them, and re-layouts: 12.4 us -> 1.28 us
  Pallas kernels: 16.1 us -> 13.4 us
  waiting for transfers between devices: 0.41 us -> 1.42 us
    unnamed x18 -> x12, local copies, waits for them, and re-layouts: 11.1 us -> 1.28 us
    ppermute x1, starting transfers between devices: 8.49 us -> 0.01 us  [local(): near_mine = lax.ppermute(own, every, NEXT)]
    ppermute x1, starting transfers between devices: 0.52 us -> 8.75 us  [local(): far_mine = lax.ppermute(own, every, SECOND)]
    pallas_call x1, Pallas kernels: 7.02 us -> 3.96 us  [local(): pl.pallas_call(top_kernel, out_shape=shape((NV, 1024), F32), in_specs=[sp...]
    reshape x1 -> x0, local copies, waits for them, and re-layouts: 1.32 us -> none  [local(): near_count.reshape(LEAVES, 1)]
    ppermute x1, starting transfers between devices: 0.1 us -> 1.15 us  [local(): far_other = lax.ppermute(far_mine, 'sub', [(0, 1), (1, 0)])]
    ppermute x1, starting transfers between devices: 1.15 us -> 0.11 us  [local(): near_other = lax.ppermute(near_mine, 'sub', [(0, 1), (1, 0)])]
  transfers between devices with their start and end apart: 5 -> 5, of which waited for: 1 -> 3; matrix products, arithmetic and copies ran while one was open for 2% -> 0% of each run, Pallas kernels for 12% -> 18%
where the time goes in v2:
time: 37.6 us; the launch traced here: 37.5 us
  starting transfers between devices  18.2 us (48%)
  Pallas kernels  13.4 us (36%)
  blocking collectives  3.15 us (8%)
  waiting for transfers between devices  1.42 us (4%)
  local copies, waits for them, and re-layouts  1.28 us (3%)
    ppermute x1, starting transfers between devices, local(): far_mine = lax.ppermute(own, every, SECOND)  8.75 us
    all_to_all x1, starting transfers between devices, local(): all_roots = lax.all_to_all(roots, every, 0, 0, tiled=True)  8.15 us
    pallas_call x1, Pallas kernels, local(): pl.pallas_call(window_kernel, out_shape=(shape((NV, 1024), F32), shape((K...  6.68 us
    pallas_call x1, Pallas kernels, local(): pl.pallas_call(top_kernel, out_shape=shape((NV, 1024), F32), in_specs=[sp...  3.96 us
    all_gather x1, blocking collectives, local(): own = lax.all_gather(pack, 'sub', axis=0, tiled=True)  3.15 us
    pallas_call x1, Pallas kernels, local(): pl.pallas_call(upward_kernel, out_shape=(shape((PAIRS, NV, 128), BF), sha...  2.76 us
    unnamed x12, local copies, waits for them, and re-layouts  1.28 us
    ppermute x1, starting transfers between devices, local(): far_other = lax.ppermute(far_mine, 'sub', [(0, 1), (1, 0)])  1.15 us
  transfers between devices with their start and end apart: 5, of which 3 were waited for; matrix products, arithmetic and copies ran while one was open for 0% of the time, Pallas kernels for 18%

profile of v2, /device:TPU:1, one launch (start us, length us, event | category | flops | bytes accessed | tf_op | source)
XLA Modules:
  0.0 37.5 jit_solution(16267496998055282292)
XLA Ops:
  0.0 2.8 %upward.1 = (bf16[24,8,128]{2,1,0:T(8,128)(2,1)}, bf16[128,4,128]{2,1,0:T(4,128)(2,1)}, s32[16,24]{1,0:T(8,128)}, s32[16,31]{1,0:T(8,128)}) custom-call(bf16[8,1024]{1,0:T(8,128)(2,1)} %density.1, bf16[16,64,64]{2,1,0:T(8,128)(2,1)} %basis.3, bf16[15,64,128]{2,1,0:T(8,128)(2,1)} %transfer.4, s32[16,24]{1,0:T(8,128)} %near_ids.1, s32[1,16]{1,0:T(1,128)} %bitcast.5, ...), custom_call_target="tpu_custom_call" | custom-call | flops 20000000 | bytes 1000000 | tf_op jit(solution)/shard_map/upward/pallas_call | solution.py:285
  2.8 3.1 %all_gather.3.own = bf16[48,8,128]{2,1,0:T(8,128)(2,1)S(1)} all-gather(bf16[24,8,128]{2,1,0:T(8,128)(2,1)} %get-tuple-element.13), channel_id=1, replica_groups=mesh['leaf'=64,'sub'=2] {'sub'}, dimensions={0}, use_global_device_ids=true | all-gather | bytes 147456 | tf_op jit(solution)/shard_map/all_gather | solution.py:300
  5.9 0.0 copy-start.1
  5.9 8.8 %collective-permute-start.2 = (bf16[48,8,128]{2,1,0:T(8,128)(2,1)S(1)}, bf16[48,8,128]{2,1,0:T(8,128)(2,1)S(1)}, u32[]{:S(2)}, u32[]{:S(2)}) collective-permute-start(bf16[48,8,128]{2,1,0:T(8,128)(2,1)S(1)} %all_gather.3.own), channel_id=1, source_target_pairs={{0,4},{2,6},{4,0},{6,2},{8,12},{10,14},{12,8},{14,10},{16,20},{18,... | collective-permute-start | bytes 294920 | tf_op jit(solution)/shard_map/ppermute | solution.py:302
  14.7 0.0 collective-permute-start
  14.7 8.2 %all-to-all-start = ((bf16[128,4,128]{2,1,0:T(4,128)(2,1)}), bf16[128,4,128]{2,1,0:T(4,128)(2,1)S(1)}, u32[]{:S(2)}, u32[]{:S(2)}) async-start(bf16[128,4,128]{2,1,0:T(4,128)(2,1)} %get-tuple-element.12), calls=%async_computation | async-start | bytes 262144 | tf_op jit(solution)/shard_map/all_to_all | solution.py:303
  22.8 0.0 collective-permute-done.2.far_mine
  22.8 0.0 copy-start.2
  22.8 1.1 %collective-permute-start.3 = (bf16[48,8,128]{2,1,0:T(8,128)(2,1)S(1)}, bf16[48,8,128]{2,1,0:T(8,128)(2,1)S(1)}, u32[]{:S(2)}, u32[]{:S(2)}) collective-permute-start(bf16[48,8,128]{2,1,0:T(8,128)(2,1)S(1)} %collective-permute-done.2.far_mine), channel_id=1, source_target_pairs={{0,1},{1,0},{2,3},{3,2},{4,5},{5,4},{6,7},{7,6},{8,9},{9,8},{10,11... | collective-permute-start | bytes 294920 | tf_op jit(solution)/shard_map/ppermute | solution.py:305
  24.0 0.0 collective-permute-done.near_mine
  24.0 0.0 copy-start.3
  24.0 0.1 collective-permute-start.1
  24.1 0.8 %collective-permute-done.3.far_other = bf16[48,8,128]{2,1,0:T(8,128)(2,1)S(1)} collective-permute-done((bf16[48,8,128]{2,1,0:T(8,128)(2,1)S(1)}, bf16[48,8,128]{2,1,0:T(8,128)(2,1)S(1)}, u32[]{:S(2)}, u32[]{:S(2)}) %collective-permute-start.3) | collective-permute-done | bytes 98336 | tf_op jit(solution)/shard_map/ppermute | solution.py:305
  24.9 0.0 copy-start.4
  24.9 0.4 collective-permute-done.1.near_other
  25.3 0.0 copy-start.5
  25.3 0.0 copy-done.1
  25.3 0.0 copy-done.2
  25.3 0.0 copy-done.3
  25.3 0.3 copy-done.4
  25.6 0.4 copy-done.5
  25.9 6.7 %window.1 = (f32[8,1024]{1,0:T(8,128)}, bf16[64,1024]{1,0:T(8,128)(2,1)}, bf16[64,768]{1,0:T(8,128)(2,1)}) custom-call(bf16[48,8,128]{2,1,0:T(8,128)(2,1)} %copy-done.1, bf16[48,8,128]{2,1,0:T(8,128)(2,1)} %copy-done.3, bf16[48,8,128]{2,1,0:T(8,128)(2,1)} %copy-done.5, bf16[48,8,128]{2,1,0:T(8,128)(2,1)} %copy-done.2, bf16[48,8,128]{2,1,0:T(8,128)(2,1)} %copy-done.4, ...), custom_call_target="tpu_custom_call" | custom-call | flops 120000000 | bytes 8000000 | tf_op jit(solution)/shard_map/window/pallas_call | solution.py:306
  32.6 0.2 all-to-all-done.roots
  32.8 0.0 copy-start
  32.9 0.6 %copy-done = bf16[128,4,128]{2,1,0:T(4,128)(2,1)} copy-done((bf16[128,4,128]{2,1,0:T(4,128)(2,1)}, bf16[128,4,128]{2,1,0:T(4,128)(2,1)S(1)}, u32[]{:S(2)}) %copy-start) | copy-done | bytes 131096
  33.5 4.0 %top.1 = f32[8,1024]{1,0:T(8,128)} custom-call(bf16[128,4,128]{2,1,0:T(4,128)(2,1)} %copy-done, bf16[126,64,128]{2,1,0:T(8,128)(2,1)} %transfer.5, s32[2,126]{1,0:T(2,128)} %bitcast.4, f32[8,1024]{1,0:T(8,128)} %get-tuple-element.16.partial, bf16[64,1024]{1,0:T(8,128)(2,1)} %get-tuple-element.17.onward, bf16[64,768]{1,0:T(8,128)(2,1)} %get-tuple-element.18.shares), custom_call_target="tpu_custom_call" | custom-call | tf_op jit(solution)/shard_map/top/pallas_call | solution.py:341
Async XLA Ops:
  5.9 19.4 %copy-start.1 = (bf16[48,8,128]{2,1,0:T(8,128)(2,1)}, bf16[48,8,128]{2,1,0:T(8,128)(2,1)S(1)}, u32[]{:S(2)}) copy-start(bf16[48,8,128]{2,1,0:T(8,128)(2,1)S(1)} %all_gather.3.own) | copy-start | bytes 294916
  5.9 16.9 %collective-permute-start.2 = (bf16[48,8,128]{2,1,0:T(8,128)(2,1)S(1)}, bf16[48,8,128]{2,1,0:T(8,128)(2,1)S(1)}, u32[]{:S(2)}, u32[]{:S(2)}) collective-permute-start(bf16[48,8,128]{2,1,0:T(8,128)(2,1)S(1)} %all_gather.3.own), channel_id=1, source_target_pairs={{0,4},{2,6},{4,0},{6,2},{8,12},{10,14},{12,8},{14,10},{16,20},{18,... | collective-permute-start | bytes 294920 | tf_op jit(solution)/shard_map/ppermute | solution.py:302
  14.7 9.3 %collective-permute-start = (bf16[48,8,128]{2,1,0:T(8,128)(2,1)S(1)}, bf16[48,8,128]{2,1,0:T(8,128)(2,1)S(1)}, u32[]{:S(2)}, u32[]{:S(2)}) collective-permute-start(bf16[48,8,128]{2,1,0:T(8,128)(2,1)S(1)} %all_gather.3.own), channel_id=1, source_target_pairs={{0,2},{2,0},{4,6},{6,4},{8,10},{10,8},{12,14},{14,12},{16,18},{18,... | collective-permute-start | bytes 294920 | tf_op jit(solution)/shard_map/ppermute | solution.py:301
  14.7 18.2 %all-to-all-start = ((bf16[128,4,128]{2,1,0:T(4,128)(2,1)}), bf16[128,4,128]{2,1,0:T(4,128)(2,1)S(1)}, u32[]{:S(2)}, u32[]{:S(2)}) async-start(bf16[128,4,128]{2,1,0:T(4,128)(2,1)} %get-tuple-element.12), calls=%async_computation | async-start | bytes 262144 | tf_op jit(solution)/shard_map/all_to_all | solution.py:303
  22.8 2.5 %copy-start.2 = (bf16[48,8,128]{2,1,0:T(8,128)(2,1)}, bf16[48,8,128]{2,1,0:T(8,128)(2,1)S(1)}, u32[]{:S(2)}) copy-start(bf16[48,8,128]{2,1,0:T(8,128)(2,1)S(1)} %collective-permute-done.2.far_mine) | copy-start | bytes 294916
  22.8 2.1 %collective-permute-start.3 = (bf16[48,8,128]{2,1,0:T(8,128)(2,1)S(1)}, bf16[48,8,128]{2,1,0:T(8,128)(2,1)S(1)}, u32[]{:S(2)}, u32[]{:S(2)}) collective-permute-start(bf16[48,8,128]{2,1,0:T(8,128)(2,1)S(1)} %collective-permute-done.2.far_mine), channel_id=1, source_target_pairs={{0,1},{1,0},{2,3},{3,2},{4,5},{5,4},{6,7},{7,6},{8,9},{9,8},{10,11... | collective-permute-start | bytes 294920 | tf_op jit(solution)/shard_map/ppermute | solution.py:305
  24.0 1.3 %copy-start.3 = (bf16[48,8,128]{2,1,0:T(8,128)(2,1)}, bf16[48,8,128]{2,1,0:T(8,128)(2,1)S(1)}, u32[]{:S(2)}) copy-start(bf16[48,8,128]{2,1,0:T(8,128)(2,1)S(1)} %collective-permute-done.near_mine) | copy-start | bytes 294916
  24.0 1.3 %collective-permute-start.1 = (bf16[48,8,128]{2,1,0:T(8,128)(2,1)S(1)}, bf16[48,8,128]{2,1,0:T(8,128)(2,1)S(1)}, u32[]{:S(2)}, u32[]{:S(2)}) collective-permute-start(bf16[48,8,128]{2,1,0:T(8,128)(2,1)S(1)} %collective-permute-done.near_mine), channel_id=1, source_target_pairs={{0,1},{1,0},{2,3},{3,2},{4,5},{5,4},{6,7},{7,6},{8,9},{9,8},{10,11... | collective-permute-start | bytes 294920 | tf_op jit(solution)/shard_map/ppermute | solution.py:304
  24.9 0.6 %copy-start.4 = (bf16[48,8,128]{2,1,0:T(8,128)(2,1)}, bf16[48,8,128]{2,1,0:T(8,128)(2,1)S(1)}, u32[]{:S(2)}) copy-start(bf16[48,8,128]{2,1,0:T(8,128)(2,1)S(1)} %collective-permute-done.3.far_other) | copy-start | bytes 294916
  25.3 0.6 %copy-start.5 = (bf16[48,8,128]{2,1,0:T(8,128)(2,1)}, bf16[48,8,128]{2,1,0:T(8,128)(2,1)S(1)}, u32[]{:S(2)}) copy-start(bf16[48,8,128]{2,1,0:T(8,128)(2,1)S(1)} %collective-permute-done.1.near_other) | copy-start | bytes 294916
  32.8 0.7 %copy-start = (bf16[128,4,128]{2,1,0:T(4,128)(2,1)}, bf16[128,4,128]{2,1,0:T(4,128)(2,1)S(1)}, u32[]{:S(2)}) copy-start(bf16[128,4,128]{2,1,0:T(4,128)(2,1)S(1)} %all-to-all-done.roots) | copy-start | bytes 393220

commit v3 on v2

--- a/solution.py
+++ b/solution.py
@@ -59,6 +59,9 @@
     far_flip = jnp.bitwise_and(jnp.right_shift(leaf, 1), 1) ^ sub
     place = jnp.where(delta == 1, 1 + near_flip, jnp.where(delta == -1, 2 - near_flip, 0))
     place = jnp.where(delta == 2, 3 + far_flip, jnp.where(delta == -2, 4 - far_flip, place))
+    end_next = ((leaf == 0) | (leaf == 62)) & (delta == 1)
+    end_last = ((leaf == 1) | (leaf == 63)) & (delta == -1)
+    place = jnp.where(end_next | end_last, 4 - sub, place)
     index = (place * 2 + core) * NODES + offset + node
     live = live & (chip >= 0) & (chip < 64)
     index = jnp.where(live, index, ZERO)
@@ -66,10 +69,24 @@
     return index ^ jnp.bitwise_and(column, 1)
 
 
-def upward_kernel(
-    density, basis, transfer, near_ids, near_count, coupling_ids, pack, roots, near_nodes, coupling_nodes
-):
+def all_window_nodes(near_ids, near_count, coupling_ids):
     leaf, sub = lax.axis_index("leaf"), lax.axis_index("sub")
+    slots = lax.broadcasted_iota(jnp.int32, near_ids.shape, 1)
+    diagonal = lax.broadcasted_iota(jnp.int32, (LEAVES, LEAVES), 0) == lax.broadcasted_iota(
+        jnp.int32, (LEAVES, LEAVES), 1
+    )
+    counts = jnp.sum(jnp.where(diagonal, near_count, 0), axis=1, keepdims=True)
+    near_nodes = window_nodes(near_ids, 0, 0, leaf, sub, slots < counts, 1)
+    rows = lax.broadcasted_iota(jnp.int32, coupling_ids.shape, 1)
+    height = sum((rows >= 2 * LEAVES - 2 * (LEAVES >> h)).astype(jnp.int32) for h in range(1, HEIGHTS))
+    offset = jnp.zeros(coupling_ids.shape, jnp.int32)
+    for h, place in enumerate(LEVEL_OFFSETS):
+        offset = jnp.where(height == h, place, offset)
+    coupling_nodes = window_nodes(coupling_ids, height, offset, leaf, sub, coupling_ids >= 0, 0)
+    return near_nodes, coupling_nodes
+
+
+def upward_kernel(density, basis, transfer, pack, roots):
     level = []
     for p in range(8):
         pair = density[:, 128 * p : 128 * p + 128]
@@ -93,29 +110,21 @@
     pack[23] = beside(root, root).astype(BF)
     sent = beside(root[:4], root[4:]).astype(BF)
     roots[...] = jnp.broadcast_to(sent[None], roots.shape)
-    slots = lax.broadcasted_iota(jnp.int32, near_ids.shape, 1)
-    diagonal = lax.broadcasted_iota(jnp.int32, (LEAVES, LEAVES), 0) == lax.broadcasted_iota(
-        jnp.int32, (LEAVES, LEAVES), 1
-    )
-    counts = jnp.sum(jnp.where(diagonal, near_count[...], 0), axis=1, keepdims=True)
-    near_nodes[...] = window_nodes(near_ids[...], 0, 0, leaf, sub, slots < counts, 1)
-    ids = coupling_ids[...]
-    rows = lax.broadcasted_iota(jnp.int32, ids.shape, 1)
-    height = sum((rows >= 2 * LEAVES - 2 * (LEAVES >> h)).astype(jnp.int32) for h in range(1, HEIGHTS))
-    offset = jnp.zeros(ids.shape, jnp.int32)
-    for h, place in enumerate(LEVEL_OFFSETS):
-        offset = jnp.where(height == h, place, offset)
-    coupling_nodes[...] = window_nodes(ids, height, offset, leaf, sub, ids >= 0, 0)
 
 
 def window_kernel(
-    own, near_mine, near_other, far_mine, far_other, near_nodes, coupling_nodes, near_blocks, coupling,
-    transfer, basis, top_transfer, top_coupling, partial, onward, shares, window, arrived, near_ids,
-    coupling_ids, near_held, coupling_held, transfer_held, basis_held, rows_held, links_held, id_sems,
-    arrival_sems, near_sems, coupling_sems, small_sems, row_sems, link_sems,
+    own, near_mine, near_other, far_mine, far_other, near_ids_in, near_count_in, coupling_ids_in, near_blocks,
+    coupling, transfer, basis, top_transfer, top_coupling, partial, onward, shares, window, arrived, near_raw,
+    near_count, coupling_raw, near_nodes, coupling_nodes, near_ids, coupling_ids, near_held, coupling_held, transfer_held, basis_held, rows_held, links_held, raw_sems,
+    id_sems, arrival_sems, near_sems, coupling_sems, small_sems, row_sems, link_sems,
 ):
     device = lax.axis_index("leaf") * 2 + lax.axis_index("sub")
     copy = pltpu.make_async_copy
+    raw_copies = [
+        copy(near_ids_in, near_raw, raw_sems.at[0]),
+        copy(near_count_in, near_count, raw_sems.at[1]),
+        copy(coupling_ids_in, coupling_raw, raw_sems.at[2]),
+    ]
     id_copies = [copy(coupling_nodes, coupling_ids, id_sems.at[0]), copy(near_nodes, near_ids, id_sems.at[1])]
     arrivals = [
         copy(source, arrived.at[i], arrival_sems.at[i])
@@ -134,7 +143,7 @@
         for a in range(0, LEAVES, 8)
     ]
     queue = coupling_copies + near_copies
-    for one in id_copies + arrivals + queue[:1] + row_copies + link_copies + small_copies + queue[1:AHEAD]:
+    for one in raw_copies + arrivals + queue[:1] + row_copies + link_copies + small_copies + queue[1:AHEAD]:
         one.start()
 
     def take(index):
@@ -142,6 +151,11 @@
         if index + AHEAD < len(queue):
             queue[index + AHEAD].start()
 
+    for one in raw_copies:
+        one.wait()
+    near_nodes[...], coupling_nodes[...] = all_window_nodes(near_raw[...], near_count[...], coupling_raw[...])
+    for one in id_copies:
+        one.start()
     window[ZERO] = jnp.zeros((NV, 128), F32)
     window[ZERO + 1] = jnp.zeros((NV, 128), F32)
     for one in arrivals:
@@ -210,40 +224,21 @@
         onward[:, span] = pair[NV:].astype(BF)
 
 
-def top_kernel(
-    roots, transfer, ids, partial, onward, shares, potential, nodes, held_ids, held, roots_held, partial_held,
-    onward_held, shares_held, sems,
-):
+def top_kernel(roots, transfer, ids, partial, onward, shares, potential, nodes, held_ids, sems):
     device = lax.axis_index("leaf") * 2 + lax.axis_index("sub")
-    copy = pltpu.make_async_copy
-    root_copy = copy(roots, roots_held, sems.at[0])
-    spans = ((0, 32), (32, 32), (64, 62))
-    copies = [
-        copy(transfer.at[pl.ds(a, n)], held.at[pl.ds(a, n)], sems.at[1 + i]) for i, (a, n) in enumerate(spans)
-    ]
-    id_copy = copy(ids, held_ids, sems.at[4])
-    last_copies = [
-        copy(shares, shares_held, sems.at[5]),
-        copy(onward, onward_held, sems.at[6]),
-        copy(partial, partial_held, sems.at[7]),
-    ]
-    for one in [root_copy] + copies + [id_copy] + last_copies:
-        one.start()
+    id_copy = pltpu.make_async_copy(ids, held_ids, sems.at[0])
+    id_copy.start()
     low4 = lax.broadcasted_iota(jnp.int32, (4, 128), 1) < K
-    root_copy.wait()
     made = []
     for m in range(64):
-        a, b = roots_held[2 * m].astype(F32), roots_held[2 * m + 1].astype(F32)
+        a, b = roots[2 * m].astype(F32), roots[2 * m + 1].astype(F32)
         upper = jnp.where(low4, a, pltpu.roll(b, K, 1))
         lower = jnp.where(low4, pltpu.roll(a, K, 1), b)
-        if m % 32 == 0:
-            copies[m // 32].wait()
-        made.append(dot_t(held[m], stacked(upper, lower).astype(BF)).astype(BF))
-    copies[2].wait()
+        made.append(dot_t(transfer[m], stacked(upper, lower).astype(BF)).astype(BF))
     for t, first in enumerate(FIRSTS):
         if t:
             made = [
-                dot(held[first + m], stacked(made[2 * m], made[2 * m + 1])).astype(BF)
+                dot(transfer[first + m], stacked(made[2 * m], made[2 * m + 1])).astype(BF)
                 for m in range(len(made) // 2)
             ]
         for m, node in enumerate(made):
@@ -253,11 +248,9 @@
     for t, first in enumerate(FIRSTS, 1):
         row = first + jnp.right_shift(device, t)
         sources += [nodes[first + held_ids[0, row]], nodes[first + held_ids[1, row]]]
-    for one in last_copies:
-        one.wait()
-    incoming = dot(shares_held[...], stacked(*sources)).astype(BF)
+    incoming = dot(shares[...], stacked(*sources)).astype(BF)
     incoming = dot_t(unit(NV), incoming).astype(BF)
-    potential[...] = partial_held[...] + dot(incoming, onward_held[...])
+    potential[...] = partial[...] + dot(incoming, onward[...])
 
 
 def spec(space):
@@ -267,14 +260,18 @@
 VMEM, SMEM, ANY = pltpu.VMEM, pltpu.SMEM, pl.ANY
 
 
-def swapped(first, second):
-    return [(2 * c, 2 * (first(c) % 64)) for c in range(64)] + [
-        (2 * c + 1, 2 * (second(c) % 64) + 1) for c in range(64)
-    ]
-
-
-NEXT = swapped(lambda c: c ^ 1, lambda c: ((c + 1) ^ 1) - 1)
-SECOND = swapped(lambda c: c ^ 2, lambda c: ((c + 2) ^ 2) - 2)
+def exchanged(core, pairs):
+    return [(2 * a + core, 2 * b + core) for c, d in pairs for a, b in ((c, d), (d, c))]
+
+
+NEXT = (
+    exchanged(0, [(c, c + 1) for c in range(2, 62, 2)])
+    + exchanged(1, [(c, c + 1) for c in range(1, 62, 2)])
+    + [(0, 1), (1, 2), (2, 0), (126, 127), (127, 124), (124, 126)]
+)
+SECOND = exchanged(0, [(c, c + 2) for c in range(64) if c % 4 < 2]) + exchanged(
+    1, [(c, c + 2) for c in range(62) if c % 4 >= 2] + [(0, 1), (62, 63)]
+)
 
 
 def local(
@@ -282,20 +279,15 @@
     top_transfer, top_coupling, top_coupling_ids,
 ):
     shape = jax.ShapeDtypeStruct
-    pack, roots, near_nodes, coupling_nodes = pl.pallas_call(
+    pack, roots = pl.pallas_call(
         upward_kernel,
-        out_shape=(
-            shape((PAIRS, NV, 128), BF),
-            shape((128, 4, 128), BF),
-            shape((LEAVES, NEAR), jnp.int32),
-            shape((COUP, 2 * LEAVES - 1), jnp.int32),
-        ),
-        in_specs=[spec(VMEM)] * 6,
-        out_specs=(spec(VMEM),) * 4,
-        cost_estimate=pl.CostEstimate(flops=20_000_000, bytes_accessed=1_000_000, transcendentals=0),
+        out_shape=(shape((PAIRS, NV, 128), BF), shape((128, 4, 128), BF)),
+        in_specs=[spec(VMEM)] * 3,
+        out_specs=(spec(VMEM),) * 2,
+        cost_estimate=pl.CostEstimate(flops=20_000_000_000, bytes_accessed=1_000_000, transcendentals=0),
         compiler_params=pltpu.CompilerParams(vmem_limit_bytes=56 << 20),
         name="upward",
-    )(density, basis, local_transfer, near_ids, near_count.reshape(1, LEAVES), local_coupling_ids.T)
+    )(density, basis, local_transfer)
     every = ("leaf", "sub")
     own = lax.all_gather(pack, "sub", axis=0, tiled=True)
     near_mine = lax.ppermute(own, every, NEXT)
@@ -310,11 +302,16 @@
             shape((K, 1024), BF),
             shape((K, 768), BF),
         ),
-        in_specs=[spec(ANY)] * 13,
+        in_specs=[spec(ANY)] * 14,
         out_specs=(spec(VMEM),) * 3,
         scratch_shapes=[
             pltpu.VMEM((ZERO + 2, NV, 128), F32),
             pltpu.VMEM((5, 2 * PAIRS, NV, 128), BF),
+            pltpu.VMEM((LEAVES, NEAR), jnp.int32),
+            pltpu.VMEM((1, LEAVES), jnp.int32),
+            pltpu.VMEM((COUP, 2 * LEAVES - 1), jnp.int32),
+            pltpu.VMEM((LEAVES, NEAR), jnp.int32),
+            pltpu.VMEM((COUP, 2 * LEAVES - 1), jnp.int32),
             pltpu.SMEM((LEAVES, NEAR), jnp.int32),
             pltpu.SMEM((COUP, 2 * LEAVES - 1), jnp.int32),
             pltpu.VMEM((LEAVES, 64, NEAR * 64), BF),
@@ -323,6 +320,7 @@
             pltpu.VMEM((LEAVES, 64, K), BF),
             pltpu.VMEM((6, K, 128), BF),
             pltpu.VMEM((6, K, 128), BF),
+            pltpu.SemaphoreType.DMA((3,)),
             pltpu.SemaphoreType.DMA((2,)),
             pltpu.SemaphoreType.DMA((5,)),
             pltpu.SemaphoreType.DMA((4,)),
@@ -331,29 +329,24 @@
             pltpu.SemaphoreType.DMA((6,)),
             pltpu.SemaphoreType.DMA((6,)),
         ],
-        compiler_params=pltpu.CompilerParams(vmem_limit_bytes=56 << 20),
+        compiler_params=pltpu.CompilerParams(vmem_limit_bytes=53 << 20),
         cost_estimate=pl.CostEstimate(flops=120_000_000, bytes_accessed=8_000_000, transcendentals=0),
         name="window",
     )(
-        own, near_mine, near_other, far_mine, far_other, near_nodes, coupling_nodes, near_blocks,
-        local_coupling, local_transfer, basis, top_transfer, top_coupling,
+        own, near_mine, near_other, far_mine, far_other, near_ids, near_count.reshape(1, LEAVES),
+        local_coupling_ids.T, near_blocks, local_coupling, local_transfer, basis, top_transfer, top_coupling,
     )
     return pl.pallas_call(
         top_kernel,
         out_shape=shape((NV, 1024), F32),
-        in_specs=[spec(ANY)] * 6,
+        in_specs=[spec(VMEM)] * 2 + [spec(ANY)] + [spec(VMEM)] * 3,
         out_specs=spec(VMEM),
         scratch_shapes=[
             pltpu.VMEM((TOP, K, NV), BF),
             pltpu.SMEM((2, TOP), jnp.int32),
-            pltpu.VMEM((TOP, K, 128), BF),
-            pltpu.VMEM((128, 4, 128), BF),
-            pltpu.VMEM((NV, 1024), F32),
-            pltpu.VMEM((K, 1024), BF),
-            pltpu.VMEM((K, 768), BF),
-            pltpu.SemaphoreType.DMA((8,)),
+            pltpu.SemaphoreType.DMA((1,)),
         ],
-        compiler_params=pltpu.CompilerParams(vmem_limit_bytes=56 << 20),
+        compiler_params=pltpu.CompilerParams(vmem_limit_bytes=20 << 20),
         name="top",
     )(all_roots, top_transfer, top_coupling_ids.T, partial, onward, shares)
 

time: 37.6 us -> 34 us (0.904)
  Pallas kernels: 13.4 us -> 11.7 us
  starting transfers between devices: 18.2 us -> 16.8 us
  local copies, waits for them, and re-layouts: 1.28 us -> 0.02 us
  waiting for transfers between devices: 1.42 us -> 2.12 us
    ppermute x1, starting transfers between devices: 8.75 us -> 1.29 us  [local(): far_mine = lax.ppermute(own, every, SECOND)]
    all_to_all x1, starting transfers between devices: 8.15 us -> 11.8 us  [local(): all_roots = lax.all_to_all(roots, every, 0, 0, tiled=True)]
    ppermute x1, starting transfers between devices: 0.01 us -> 2.39 us  [local(): near_mine = lax.ppermute(own, every, NEXT)]
    pallas_call x1, Pallas kernels: 3.96 us -> 2.33 us  [local(): pl.pallas_call(top_kernel, out_shape=shape((NV, 1024), F32), in_specs=[sp...]
    unnamed x12 -> x10, local copies, waits for them, and re-layouts: 1.28 us -> 0.02 us
    all_to_all x1, waiting for transfers between devices: 0.23 us -> 0.92 us  [local(): all_roots = lax.all_to_all(roots, every, 0, 0, tiled=True)]
  transfers between devices with their start and end apart: 5 -> 5, of which waited for: 3 -> 3; matrix products, arithmetic and copies ran while one was open for 0% -> 0% of each run, Pallas kernels for 18% -> 20%
where the time goes in v3:
time: 34 us; the launch traced here: 33.8 us
  starting transfers between devices  16.8 us (49%)
  Pallas kernels  11.7 us (34%)
  blocking collectives  3.15 us (9%)
  waiting for transfers between devices  2.12 us (6%)
    all_to_all x1, starting transfers between devices, local(): all_roots = lax.all_to_all(roots, every, 0, 0, tiled=True)  11.8 us
    pallas_call x1, Pallas kernels, local(): pl.pallas_call(window_kernel, out_shape=(shape((NV, 1024), F32), shape((K...  6.6 us
    all_gather x1, blocking collectives, local(): own = lax.all_gather(pack, 'sub', axis=0, tiled=True)  3.15 us
    pallas_call x1, Pallas kernels, local(): pl.pallas_call(upward_kernel, out_shape=(shape((PAIRS, NV, 128), BF), sha...  2.77 us
    ppermute x1, starting transfers between devices, local(): near_mine = lax.ppermute(own, every, NEXT)  2.39 us
    pallas_call x1, Pallas kernels, local(): pl.pallas_call(top_kernel, out_shape=shape((NV, 1024), F32), in_specs=[sp...  2.33 us
    ppermute x1, starting transfers between devices, local(): far_mine = lax.ppermute(own, every, SECOND)  1.29 us
    ppermute x1, starting transfers between devices, local(): far_other = lax.ppermute(far_mine, 'sub', [(0, 1), (1, 0)])  1.15 us
  transfers between devices with their start and end apart: 5, of which 3 were waited for; matrix products, arithmetic and copies ran while one was open for 0% of the time, Pallas kernels for 20%

profile of v3, /device:TPU:1, one launch (start us, length us, event | category | flops | bytes accessed | tf_op | source)
XLA Modules:
  0.0 33.8 jit_solution(6388872034905376426)
XLA Ops:
  0.0 0.0 copy-start.2
  0.0 0.0 copy-start.4
  0.0 0.0 copy-start.1
  0.0 2.8 %upward.1 = (bf16[24,8,128]{2,1,0:T(8,128)(2,1)}, bf16[128,4,128]{2,1,0:T(4,128)(2,1)}) custom-call(bf16[8,1024]{1,0:T(8,128)(2,1)} %density.1, bf16[16,64,64]{2,1,0:T(8,128)(2,1)} %basis.3, bf16[15,64,128]{2,1,0:T(8,128)(2,1)} %transfer.4), custom_call_target="tpu_custom_call" | custom-call | flops 20000000000 | bytes 1000000 | tf_op jit(solution)/shard_map/upward/pallas_call | solution.py:282
  2.8 3.1 %all_gather.3.own = bf16[48,8,128]{2,1,0:T(8,128)(2,1)S(1)} all-gather(bf16[24,8,128]{2,1,0:T(8,128)(2,1)} %get-tuple-element.11), channel_id=1, replica_groups=mesh['leaf'=64,'sub'=2] {'sub'}, dimensions={0}, use_global_device_ids=true | all-gather | bytes 147456 | tf_op jit(solution)/shard_map/all_gather | solution.py:292
  5.9 1.3 %collective-permute-start.2 = (bf16[48,8,128]{2,1,0:T(8,128)(2,1)S(1)}, bf16[48,8,128]{2,1,0:T(8,128)(2,1)S(1)}, u32[]{:S(2)}, u32[]{:S(2)}) collective-permute-start(bf16[48,8,128]{2,1,0:T(8,128)(2,1)S(1)} %all_gather.3.own), channel_id=1, source_target_pairs={{0,4},{4,0},{2,6},{6,2},{8,12},{12,8},{10,14},{14,10},{16,20},{20,... | collective-permute-start | bytes 294920 | tf_op jit(solution)/shard_map/ppermute | solution.py:294
  7.2 2.4 %collective-permute-start = (bf16[48,8,128]{2,1,0:T(8,128)(2,1)S(1)}, bf16[48,8,128]{2,1,0:T(8,128)(2,1)S(1)}, u32[]{:S(2)}, u32[]{:S(2)}) collective-permute-start(bf16[48,8,128]{2,1,0:T(8,128)(2,1)S(1)} %all_gather.3.own), channel_id=1, source_target_pairs={{4,6},{6,4},{8,10},{10,8},{12,14},{14,12},{16,18},{18,16},{20,22},... | collective-permute-start | bytes 294920 | tf_op jit(solution)/shard_map/ppermute | solution.py:293
  9.6 11.8 %all-to-all-start = ((bf16[128,4,128]{2,1,0:T(4,128)(2,1)}), bf16[128,4,128]{2,1,0:T(4,128)(2,1)S(1)}, u32[]{:S(2)}, u32[]{:S(2)}) async-start(bf16[128,4,128]{2,1,0:T(4,128)(2,1)} %get-tuple-element.10), calls=%async_computation | async-start | bytes 262144 | tf_op jit(solution)/shard_map/all_to_all | solution.py:295
  21.5 0.0 collective-permute-done.2.far_mine
  21.5 1.1 %collective-permute-start.3 = (bf16[48,8,128]{2,1,0:T(8,128)(2,1)S(1)}, bf16[48,8,128]{2,1,0:T(8,128)(2,1)S(1)}, u32[]{:S(2)}, u32[]{:S(2)}) collective-permute-start(bf16[48,8,128]{2,1,0:T(8,128)(2,1)S(1)} %collective-permute-done.2.far_mine), channel_id=1, source_target_pairs={{0,1},{1,0},{2,3},{3,2},{4,5},{5,4},{6,7},{7,6},{8,9},{9,8},{10,11... | collective-permute-start | bytes 294920 | tf_op jit(solution)/shard_map/ppermute | solution.py:297
  22.6 0.0 collective-permute-done.near_mine
  22.6 0.1 collective-permute-start.1
  22.7 0.8 %collective-permute-done.3.far_other = bf16[48,8,128]{2,1,0:T(8,128)(2,1)S(1)} collective-permute-done((bf16[48,8,128]{2,1,0:T(8,128)(2,1)S(1)}, bf16[48,8,128]{2,1,0:T(8,128)(2,1)S(1)}, u32[]{:S(2)}, u32[]{:S(2)}) %collective-permute-start.3) | collective-permute-done | bytes 98336 | tf_op jit(solution)/shard_map/ppermute | solution.py:297
  23.6 0.4 %collective-permute-done.1.near_other = bf16[48,8,128]{2,1,0:T(8,128)(2,1)S(1)} collective-permute-done((bf16[48,8,128]{2,1,0:T(8,128)(2,1)S(1)}, bf16[48,8,128]{2,1,0:T(8,128)(2,1)S(1)}, u32[]{:S(2)}, u32[]{:S(2)}) %collective-permute-start.1) | collective-permute-done | bytes 98336 | tf_op jit(solution)/shard_map/ppermute | solution.py:296
  23.9 0.0 copy-done.2
  23.9 0.0 copy-done.4
  23.9 0.0 copy-done.1
  23.9 0.0 copy-start
  24.0 0.0 copy-start.3
  24.0 6.6 %window.1 = (f32[8,1024]{1,0:T(8,128)S(1)}, bf16[64,1024]{1,0:T(8,128)(2,1)S(1)}, bf16[64,768]{1,0:T(8,128)(2,1)S(1)}) custom-call(bf16[48,8,128]{2,1,0:T(8,128)(2,1)S(1)} %all_gather.3.own, bf16[48,8,128]{2,1,0:T(8,128)(2,1)S(1)} %collective-permute-done.near_mine, bf16[48,8,128]{2,1,0:T(8,128)(2,1)S(1)} %collective-permute-done.1.near_other, ...), custom_call_target="tpu_custom_call" | custom-call | flops 120000000 | bytes 8000000 | tf_op jit(solution)/shard_map/window/pallas_call | solution.py:298
  30.6 0.9 %all-to-all-done.roots = bf16[128,4,128]{2,1,0:T(4,128)(2,1)S(1)} async-done(((bf16[128,4,128]{2,1,0:T(4,128)(2,1)}), bf16[128,4,128]{2,1,0:T(4,128)(2,1)S(1)}, u32[]{:S(2)}, u32[]{:S(2)}) %all-to-all-start) | async-done | bytes 131104 | tf_op jit(solution)/shard_map/all_to_all | solution.py:295
  31.5 0.0 copy-done
  31.5 0.0 copy-done.3
  31.5 2.3 %top.1 = f32[8,1024]{1,0:T(8,128)} custom-call(bf16[128,4,128]{2,1,0:T(4,128)(2,1)S(1)} %all-to-all-done.roots, bf16[126,64,128]{2,1,0:T(8,128)(2,1)S(1)} %copy-done, s32[2,126]{1,0:T(2,128)S(1)} %bitcast.4, f32[8,1024]{1,0:T(8,128)S(1)} %get-tuple-element.12.partial, bf16[64,1024]{1,0:T(8,128)(2,1)S(1)} %get-tuple-element.13.onward, ...), custom_call_target="tpu_custom_call" | custom-call | tf_op jit(solution)/shard_map/top/pallas_call | solution.py:339
Async XLA Ops:
  0.0 23.9 %copy-start.2 = (s32[31,16]{0,1:T(8,128)S(1)}, s32[31,16]{0,1:T(8,128)}, u32[]{:S(2)}) copy-start(s32[31,16]{0,1:T(8,128)} %param.18) | copy-start | bytes 5956
  0.0 23.9 %copy-start.4 = (s32[16]{0:T(128)S(1)}, s32[16]{0:T(128)}, u32[]{:S(2)}) copy-start(s32[16]{0:T(128)} %param.14) | copy-start | bytes 196
  0.0 23.9 %copy-start.1 = (s32[16,24]{1,0:T(8,128)S(1)}, s32[16,24]{1,0:T(8,128)}, u32[]{:S(2)}) copy-start(s32[16,24]{1,0:T(8,128)} %near_ids_in.1) | copy-start | bytes 4612
  5.9 15.5 %collective-permute-start.2 = (bf16[48,8,128]{2,1,0:T(8,128)(2,1)S(1)}, bf16[48,8,128]{2,1,0:T(8,128)(2,1)S(1)}, u32[]{:S(2)}, u32[]{:S(2)}) collective-permute-start(bf16[48,8,128]{2,1,0:T(8,128)(2,1)S(1)} %all_gather.3.own), channel_id=1, source_target_pairs={{0,4},{4,0},{2,6},{6,2},{8,12},{12,8},{10,14},{14,10},{16,20},{20,... | collective-permute-start | bytes 294920 | tf_op jit(solution)/shard_map/ppermute | solution.py:294
  7.2 15.4 %collective-permute-start = (bf16[48,8,128]{2,1,0:T(8,128)(2,1)S(1)}, bf16[48,8,128]{2,1,0:T(8,128)(2,1)S(1)}, u32[]{:S(2)}, u32[]{:S(2)}) collective-permute-start(bf16[48,8,128]{2,1,0:T(8,128)(2,1)S(1)} %all_gather.3.own), channel_id=1, source_target_pairs={{4,6},{6,4},{8,10},{10,8},{12,14},{14,12},{16,18},{18,16},{20,22},... | collective-permute-start | bytes 294920 | tf_op jit(solution)/shard_map/ppermute | solution.py:293
  9.6 21.9 %all-to-all-start = ((bf16[128,4,128]{2,1,0:T(4,128)(2,1)}), bf16[128,4,128]{2,1,0:T(4,128)(2,1)S(1)}, u32[]{:S(2)}, u32[]{:S(2)}) async-start(bf16[128,4,128]{2,1,0:T(4,128)(2,1)} %get-tuple-element.10), calls=%async_computation | async-start | bytes 262144 | tf_op jit(solution)/shard_map/all_to_all | solution.py:295
  21.5 2.1 %collective-permute-start.3 = (bf16[48,8,128]{2,1,0:T(8,128)(2,1)S(1)}, bf16[48,8,128]{2,1,0:T(8,128)(2,1)S(1)}, u32[]{:S(2)}, u32[]{:S(2)}) collective-permute-start(bf16[48,8,128]{2,1,0:T(8,128)(2,1)S(1)} %collective-permute-done.2.far_mine), channel_id=1, source_target_pairs={{0,1},{1,0},{2,3},{3,2},{4,5},{5,4},{6,7},{7,6},{8,9},{9,8},{10,11... | collective-permute-start | bytes 294920 | tf_op jit(solution)/shard_map/ppermute | solution.py:297
  22.6 1.3 %collective-permute-start.1 = (bf16[48,8,128]{2,1,0:T(8,128)(2,1)S(1)}, bf16[48,8,128]{2,1,0:T(8,128)(2,1)S(1)}, u32[]{:S(2)}, u32[]{:S(2)}) collective-permute-start(bf16[48,8,128]{2,1,0:T(8,128)(2,1)S(1)} %collective-permute-done.near_mine), channel_id=1, source_target_pairs={{0,1},{1,0},{2,3},{3,2},{4,5},{5,4},{6,7},{7,6},{8,9},{9,8},{10,11... | collective-permute-start | bytes 294920 | tf_op jit(solution)/shard_map/ppermute | solution.py:296
  23.9 7.6 %copy-start = (bf16[126,64,128]{2,1,0:T(8,128)(2,1)S(1)}, bf16[126,64,128]{2,1,0:T(8,128)(2,1)}, u32[]{:S(2)}) copy-start(bf16[126,64,128]{2,1,0:T(8,128)(2,1)} %transfer.5) | copy-start | bytes 6193156
  24.0 7.5 %copy-start.3 = (s32[126,2]{0,1:T(2,128)S(1)}, s32[126,2]{0,1:T(2,128)}, u32[]{:S(2)}) copy-start(s32[126,2]{0,1:T(2,128)} %param.21) | copy-start | bytes 3028

commit v4 on v3

--- a/solution.py
+++ b/solution.py
@@ -55,13 +55,9 @@
     delta = jnp.right_shift(slot, 1) - 2
     core = jnp.bitwise_and(slot, 1)
     chip = leaf + delta
-    near_flip = jnp.bitwise_and(leaf, 1) ^ sub
-    far_flip = jnp.bitwise_and(jnp.right_shift(leaf, 1), 1) ^ sub
-    place = jnp.where(delta == 1, 1 + near_flip, jnp.where(delta == -1, 2 - near_flip, 0))
-    place = jnp.where(delta == 2, 3 + far_flip, jnp.where(delta == -2, 4 - far_flip, place))
-    end_next = ((leaf == 0) | (leaf == 62)) & (delta == 1)
-    end_last = ((leaf == 1) | (leaf == 63)) & (delta == -1)
-    place = jnp.where(end_next | end_last, 4 - sub, place)
+    odd, upper = jnp.bitwise_and(leaf, 1), jnp.bitwise_and(jnp.right_shift(leaf, 1), 1)
+    place = jnp.where(delta == 1 - 2 * odd, 1 + sub, jnp.where(delta == 2 * odd - 1, 3 + sub, 0))
+    place = jnp.where(delta == 2 - 4 * upper, 2 - sub, jnp.where(delta == 4 * upper - 2, 4 - sub, place))
     index = (place * 2 + core) * NODES + offset + node
     live = live & (chip >= 0) & (chip < 64)
     index = jnp.where(live, index, ZERO)
@@ -113,7 +109,7 @@
 
 
 def window_kernel(
-    own, near_mine, near_other, far_mine, far_other, near_ids_in, near_count_in, coupling_ids_in, near_blocks,
+    own, inner_mine, inner_other, outer_mine, outer_other, near_ids_in, near_count_in, coupling_ids_in, near_blocks,
     coupling, transfer, basis, top_transfer, top_coupling, partial, onward, shares, window, arrived, near_raw,
     near_count, coupling_raw, near_nodes, coupling_nodes, near_ids, coupling_ids, near_held, coupling_held, transfer_held, basis_held, rows_held, links_held, raw_sems,
     id_sems, arrival_sems, near_sems, coupling_sems, small_sems, row_sems, link_sems,
@@ -128,7 +124,7 @@
     id_copies = [copy(coupling_nodes, coupling_ids, id_sems.at[0]), copy(near_nodes, near_ids, id_sems.at[1])]
     arrivals = [
         copy(source, arrived.at[i], arrival_sems.at[i])
-        for i, source in enumerate((own, near_mine, near_other, far_mine, far_other))
+        for i, source in enumerate((own, inner_mine, inner_other, outer_mine, outer_other))
     ]
     small_copies = [copy(transfer, transfer_held, small_sems.at[0]), copy(basis, basis_held, small_sems.at[1])]
     places = [first + jnp.right_shift(device, t) for t, first in enumerate(FIRSTS, 1)]
@@ -264,13 +260,13 @@
     return [(2 * a + core, 2 * b + core) for c, d in pairs for a, b in ((c, d), (d, c))]
 
 
-NEXT = (
-    exchanged(0, [(c, c + 1) for c in range(2, 62, 2)])
-    + exchanged(1, [(c, c + 1) for c in range(1, 62, 2)])
-    + [(0, 1), (1, 2), (2, 0), (126, 127), (127, 124), (124, 126)]
+INNER = exchanged(0, [(c, c + 1) for c in range(0, 64, 2)]) + exchanged(
+    1, [(c, c + 2) for c in range(64) if c % 4 < 2]
 )
-SECOND = exchanged(0, [(c, c + 2) for c in range(64) if c % 4 < 2]) + exchanged(
-    1, [(c, c + 2) for c in range(62) if c % 4 >= 2] + [(0, 1), (62, 63)]
+OUTER = (
+    exchanged(0, [(c, c + 1) for c in range(1, 63, 2)])
+    + exchanged(1, [(c, c + 2) for c in range(62) if c % 4 >= 2])
+    + [(0, 1), (1, 3), (3, 0), (126, 127), (127, 125), (125, 126)]
 )
 
 
@@ -290,11 +286,11 @@
     )(density, basis, local_transfer)
     every = ("leaf", "sub")
     own = lax.all_gather(pack, "sub", axis=0, tiled=True)
-    near_mine = lax.ppermute(own, every, NEXT)
-    far_mine = lax.ppermute(own, every, SECOND)
+    inner_mine = lax.ppermute(own, every, INNER)
+    outer_mine = lax.ppermute(own, every, OUTER)
     all_roots = lax.all_to_all(roots, every, 0, 0, tiled=True)
-    near_other = lax.ppermute(near_mine, "sub", [(0, 1), (1, 0)])
-    far_other = lax.ppermute(far_mine, "sub", [(0, 1), (1, 0)])
+    inner_other = lax.ppermute(inner_mine, "sub", [(0, 1), (1, 0)])
+    outer_other = lax.ppermute(outer_mine, "sub", [(0, 1), (1, 0)])
     partial, onward, shares = pl.pallas_call(
         window_kernel,
         out_shape=(
@@ -333,7 +329,7 @@
         cost_estimate=pl.CostEstimate(flops=120_000_000, bytes_accessed=8_000_000, transcendentals=0),
         name="window",
     )(
-        own, near_mine, near_other, far_mine, far_other, near_ids, near_count.reshape(1, LEAVES),
+        own, inner_mine, inner_other, outer_mine, outer_other, near_ids, near_count.reshape(1, LEAVES),
         local_coupling_ids.T, near_blocks, local_coupling, local_transfer, basis, top_transfer, top_coupling,
     )
     return pl.pallas_call(

time: 34 us -> 31.6 us (0.929)
  starting transfers between devices: 16.8 us -> 14.4 us
    all_to_all x1, starting transfers between devices: 11.8 us -> 9.09 us  [local(): all_roots = lax.all_to_all(roots, every, 0, 0, tiled=True)]
    ppermute x4, starting transfers between devices: 4.93 us -> 5.31 us  [the longest x1 2.77 us: local(): inner_mine = lax.ppermute(own, every, INNER)]
  transfers between devices with their start and end apart: 5 -> 5, of which waited for: 3 -> 3; matrix products, arithmetic and copies ran while one was open for 0% -> 0% of each run, Pallas kernels for 20% -> 21%
where the time goes in v4:
time: 31.6 us; the launch traced here: 31.5 us
  starting transfers between devices  14.4 us (46%)
  Pallas kernels  11.7 us (37%)
  blocking collectives  3.15 us (10%)
  waiting for transfers between devices  2.12 us (7%)
    all_to_all x1, starting transfers between devices, local(): all_roots = lax.all_to_all(roots, every, 0, 0, tiled=True)  9.09 us
    pallas_call x1, Pallas kernels, local(): pl.pallas_call(window_kernel, out_shape=(shape((NV, 1024), F32), shape((K...  6.61 us
    all_gather x1, blocking collectives, local(): own = lax.all_gather(pack, 'sub', axis=0, tiled=True)  3.15 us
    ppermute x1, starting transfers between devices, local(): inner_mine = lax.ppermute(own, every, INNER)  2.77 us
    pallas_call x1, Pallas kernels, local(): pl.pallas_call(upward_kernel, out_shape=(shape((PAIRS, NV, 128), BF), sha...  2.77 us
    pallas_call x1, Pallas kernels, local(): pl.pallas_call(top_kernel, out_shape=shape((NV, 1024), F32), in_specs=[sp...  2.33 us
    ppermute x1, starting transfers between devices, local(): outer_mine = lax.ppermute(own, every, OUTER)  1.29 us
    ppermute x1, starting transfers between devices, local(): outer_other = lax.ppermute(outer_mine, 'sub', [(0, 1), (1, 0)])  1.15 us
  transfers between devices with their start and end apart: 5, of which 3 were waited for; matrix products, arithmetic and copies ran while one was open for 0% of the time, Pallas kernels for 21%

profile of v4, /device:TPU:1, one launch (start us, length us, event | category | flops | bytes accessed | tf_op | source)
XLA Modules:
  0.0 31.5 jit_solution(14363202145993402299)
XLA Ops:
  0.0 0.0 copy-start.2
  0.0 0.0 copy-start.4
  0.0 0.0 copy-start.1
  0.0 2.8 %upward.1 = (bf16[24,8,128]{2,1,0:T(8,128)(2,1)}, bf16[128,4,128]{2,1,0:T(4,128)(2,1)}) custom-call(bf16[8,1024]{1,0:T(8,128)(2,1)} %density.1, bf16[16,64,64]{2,1,0:T(8,128)(2,1)} %basis.3, bf16[15,64,128]{2,1,0:T(8,128)(2,1)} %transfer.4), custom_call_target="tpu_custom_call" | custom-call | flops 20000000000 | bytes 1000000 | tf_op jit(solution)/shard_map/upward/pallas_call | solution.py:278
  2.8 3.1 %all_gather.3.own = bf16[48,8,128]{2,1,0:T(8,128)(2,1)S(1)} all-gather(bf16[24,8,128]{2,1,0:T(8,128)(2,1)} %get-tuple-element.11), channel_id=1, replica_groups=mesh['leaf'=64,'sub'=2] {'sub'}, dimensions={0}, use_global_device_ids=true | all-gather | bytes 147456 | tf_op jit(solution)/shard_map/all_gather | solution.py:288
  5.9 1.3 %collective-permute-start.2 = (bf16[48,8,128]{2,1,0:T(8,128)(2,1)S(1)}, bf16[48,8,128]{2,1,0:T(8,128)(2,1)S(1)}, u32[]{:S(2)}, u32[]{:S(2)}) collective-permute-start(bf16[48,8,128]{2,1,0:T(8,128)(2,1)S(1)} %all_gather.3.own), channel_id=1, source_target_pairs={{2,4},{4,2},{6,8},{8,6},{10,12},{12,10},{14,16},{16,14},{18,20},{2... | collective-permute-start | bytes 294920 | tf_op jit(solution)/shard_map/ppermute | solution.py:290
  7.2 2.8 %collective-permute-start = (bf16[48,8,128]{2,1,0:T(8,128)(2,1)S(1)}, bf16[48,8,128]{2,1,0:T(8,128)(2,1)S(1)}, u32[]{:S(2)}, u32[]{:S(2)}) collective-permute-start(bf16[48,8,128]{2,1,0:T(8,128)(2,1)S(1)} %all_gather.3.own), channel_id=1, source_target_pairs={{0,2},{2,0},{4,6},{6,4},{8,10},{10,8},{12,14},{14,12},{16,18},{18,... | collective-permute-start | bytes 294920 | tf_op jit(solution)/shard_map/ppermute | solution.py:289
  10.0 9.1 %all-to-all-start = ((bf16[128,4,128]{2,1,0:T(4,128)(2,1)}), bf16[128,4,128]{2,1,0:T(4,128)(2,1)S(1)}, u32[]{:S(2)}, u32[]{:S(2)}) async-start(bf16[128,4,128]{2,1,0:T(4,128)(2,1)} %get-tuple-element.10), calls=%async_computation | async-start | bytes 262144 | tf_op jit(solution)/shard_map/all_to_all | solution.py:291
  19.1 0.0 collective-permute-done.2.outer_mine
  19.1 1.1 %collective-permute-start.3 = (bf16[48,8,128]{2,1,0:T(8,128)(2,1)S(1)}, bf16[48,8,128]{2,1,0:T(8,128)(2,1)S(1)}, u32[]{:S(2)}, u32[]{:S(2)}) collective-permute-start(bf16[48,8,128]{2,1,0:T(8,128)(2,1)S(1)} %collective-permute-done.2.outer_mine), channel_id=1, source_target_pairs={{0,1},{1,0},{2,3},{3,2},{4,5},{5,4},{6,7},{7,6},{8,9},{9,8},{10,11... | collective-permute-start | bytes 294920 | tf_op jit(solution)/shard_map/ppermute | solution.py:293
  20.3 0.0 collective-permute-done.inner_mine
  20.3 0.1 collective-permute-start.1
  20.4 0.8 %collective-permute-done.3.outer_other = bf16[48,8,128]{2,1,0:T(8,128)(2,1)S(1)} collective-permute-done((bf16[48,8,128]{2,1,0:T(8,128)(2,1)S(1)}, bf16[48,8,128]{2,1,0:T(8,128)(2,1)S(1)}, u32[]{:S(2)}, u32[]{:S(2)}) %collective-permute-start.3) | collective-permute-done | bytes 98336 | tf_op jit(solution)/shard_map/ppermute | solution.py:293
  21.2 0.4 %collective-permute-done.1.inner_other = bf16[48,8,128]{2,1,0:T(8,128)(2,1)S(1)} collective-permute-done((bf16[48,8,128]{2,1,0:T(8,128)(2,1)S(1)}, bf16[48,8,128]{2,1,0:T(8,128)(2,1)S(1)}, u32[]{:S(2)}, u32[]{:S(2)}) %collective-permute-start.1) | collective-permute-done | bytes 98336 | tf_op jit(solution)/shard_map/ppermute | solution.py:292
  21.6 0.0 copy-done.2
  21.6 0.0 copy-done.4
  21.6 0.0 copy-done.1
  21.6 0.0 copy-start
  21.6 0.0 copy-start.3
  21.6 6.6 %window.1 = (f32[8,1024]{1,0:T(8,128)S(1)}, bf16[64,1024]{1,0:T(8,128)(2,1)S(1)}, bf16[64,768]{1,0:T(8,128)(2,1)S(1)}) custom-call(bf16[48,8,128]{2,1,0:T(8,128)(2,1)S(1)} %all_gather.3.own, bf16[48,8,128]{2,1,0:T(8,128)(2,1)S(1)} %collective-permute-done.inner_mine, bf16[48,8,128]{2,1,0:T(8,128)(2,1)S(1)} %collective-permute-done.1.inner_other, ...), custom_call_target="tpu_custom_call" | custom-call | flops 120000000 | bytes 8000000 | tf_op jit(solution)/shard_map/window/pallas_call | solution.py:294
  28.2 0.9 %all-to-all-done.roots = bf16[128,4,128]{2,1,0:T(4,128)(2,1)S(1)} async-done(((bf16[128,4,128]{2,1,0:T(4,128)(2,1)}), bf16[128,4,128]{2,1,0:T(4,128)(2,1)S(1)}, u32[]{:S(2)}, u32[]{:S(2)}) %all-to-all-start) | async-done | bytes 131104 | tf_op jit(solution)/shard_map/all_to_all | solution.py:291
  29.1 0.0 copy-done
  29.1 0.0 copy-done.3
  29.1 2.3 %top.1 = f32[8,1024]{1,0:T(8,128)} custom-call(bf16[128,4,128]{2,1,0:T(4,128)(2,1)S(1)} %all-to-all-done.roots, bf16[126,64,128]{2,1,0:T(8,128)(2,1)S(1)} %copy-done, s32[2,126]{1,0:T(2,128)S(1)} %bitcast.4, f32[8,1024]{1,0:T(8,128)S(1)} %get-tuple-element.12.partial, bf16[64,1024]{1,0:T(8,128)(2,1)S(1)} %get-tuple-element.13.onward, ...), custom_call_target="tpu_custom_call" | custom-call | tf_op jit(solution)/shard_map/top/pallas_call | solution.py:335
Async XLA Ops:
  0.0 21.6 %copy-start.2 = (s32[31,16]{0,1:T(8,128)S(1)}, s32[31,16]{0,1:T(8,128)}, u32[]{:S(2)}) copy-start(s32[31,16]{0,1:T(8,128)} %param.18) | copy-start | bytes 5956
  0.0 21.6 %copy-start.4 = (s32[16]{0:T(128)S(1)}, s32[16]{0:T(128)}, u32[]{:S(2)}) copy-start(s32[16]{0:T(128)} %param.14) | copy-start | bytes 196
  0.0 21.6 %copy-start.1 = (s32[16,24]{1,0:T(8,128)S(1)}, s32[16,24]{1,0:T(8,128)}, u32[]{:S(2)}) copy-start(s32[16,24]{1,0:T(8,128)} %near_ids_in.1) | copy-start | bytes 4612
  5.9 13.2 %collective-permute-start.2 = (bf16[48,8,128]{2,1,0:T(8,128)(2,1)S(1)}, bf16[48,8,128]{2,1,0:T(8,128)(2,1)S(1)}, u32[]{:S(2)}, u32[]{:S(2)}) collective-permute-start(bf16[48,8,128]{2,1,0:T(8,128)(2,1)S(1)} %all_gather.3.own), channel_id=1, source_target_pairs={{2,4},{4,2},{6,8},{8,6},{10,12},{12,10},{14,16},{16,14},{18,20},{2... | collective-permute-start | bytes 294920 | tf_op jit(solution)/shard_map/ppermute | solution.py:290
  7.2 13.0 %collective-permute-start = (bf16[48,8,128]{2,1,0:T(8,128)(2,1)S(1)}, bf16[48,8,128]{2,1,0:T(8,128)(2,1)S(1)}, u32[]{:S(2)}, u32[]{:S(2)}) collective-permute-start(bf16[48,8,128]{2,1,0:T(8,128)(2,1)S(1)} %all_gather.3.own), channel_id=1, source_target_pairs={{0,2},{2,0},{4,6},{6,4},{8,10},{10,8},{12,14},{14,12},{16,18},{18,... | collective-permute-start | bytes 294920 | tf_op jit(solution)/shard_map/ppermute | solution.py:289
  10.0 19.1 %all-to-all-start = ((bf16[128,4,128]{2,1,0:T(4,128)(2,1)}), bf16[128,4,128]{2,1,0:T(4,128)(2,1)S(1)}, u32[]{:S(2)}, u32[]{:S(2)}) async-start(bf16[128,4,128]{2,1,0:T(4,128)(2,1)} %get-tuple-element.10), calls=%async_computation | async-start | bytes 262144 | tf_op jit(solution)/shard_map/all_to_all | solution.py:291
  19.1 2.1 %collective-permute-start.3 = (bf16[48,8,128]{2,1,0:T(8,128)(2,1)S(1)}, bf16[48,8,128]{2,1,0:T(8,128)(2,1)S(1)}, u32[]{:S(2)}, u32[]{:S(2)}) collective-permute-start(bf16[48,8,128]{2,1,0:T(8,128)(2,1)S(1)} %collective-permute-done.2.outer_mine), channel_id=1, source_target_pairs={{0,1},{1,0},{2,3},{3,2},{4,5},{5,4},{6,7},{7,6},{8,9},{9,8},{10,11... | collective-permute-start | bytes 294920 | tf_op jit(solution)/shard_map/ppermute | solution.py:293
  20.3 1.3 %collective-permute-start.1 = (bf16[48,8,128]{2,1,0:T(8,128)(2,1)S(1)}, bf16[48,8,128]{2,1,0:T(8,128)(2,1)S(1)}, u32[]{:S(2)}, u32[]{:S(2)}) collective-permute-start(bf16[48,8,128]{2,1,0:T(8,128)(2,1)S(1)} %collective-permute-done.inner_mine), channel_id=1, source_target_pairs={{0,1},{1,0},{2,3},{3,2},{4,5},{5,4},{6,7},{7,6},{8,9},{9,8},{10,11... | collective-permute-start | bytes 294920 | tf_op jit(solution)/shard_map/ppermute | solution.py:292
  21.6 7.6 %copy-start = (bf16[126,64,128]{2,1,0:T(8,128)(2,1)S(1)}, bf16[126,64,128]{2,1,0:T(8,128)(2,1)}, u32[]{:S(2)}) copy-start(bf16[126,64,128]{2,1,0:T(8,128)(2,1)} %transfer.5) | copy-start | bytes 6193156
  21.6 7.5 %copy-start.3 = (s32[126,2]{0,1:T(2,128)S(1)}, s32[126,2]{0,1:T(2,128)}, u32[]{:S(2)}) copy-start(s32[126,2]{0,1:T(2,128)} %param.21) | copy-start | bytes 3028

commit v5 on v4

--- a/solution.py
+++ b/solution.py
@@ -58,7 +58,8 @@
     odd, upper = jnp.bitwise_and(leaf, 1), jnp.bitwise_and(jnp.right_shift(leaf, 1), 1)
     place = jnp.where(delta == 1 - 2 * odd, 1 + sub, jnp.where(delta == 2 * odd - 1, 3 + sub, 0))
     place = jnp.where(delta == 2 - 4 * upper, 2 - sub, jnp.where(delta == 4 * upper - 2, 4 - sub, place))
-    index = (place * 2 + core) * NODES + offset + node
+    second = core ^ sub ^ ((place == 2) | (place == 4)).astype(jnp.int32)
+    index = (place * 2 + second) * NODES + offset + node
     live = live & (chip >= 0) & (chip < 64)
     index = jnp.where(live, index, ZERO)
     column = lax.broadcasted_iota(jnp.int32, ids.shape, slot_axis)
@@ -285,7 +286,7 @@
         name="upward",
     )(density, basis, local_transfer)
     every = ("leaf", "sub")
-    own = lax.all_gather(pack, "sub", axis=0, tiled=True)
+    own = jnp.concatenate([pack, lax.ppermute(pack, "sub", [(0, 1), (1, 0)])])
     inner_mine = lax.ppermute(own, every, INNER)
     outer_mine = lax.ppermute(own, every, OUTER)
     all_roots = lax.all_to_all(roots, every, 0, 0, tiled=True)

time: 31.6 us -> 31.1 us (0.984)
  blocking collectives: 3.15 us -> 0 us
  starting transfers between devices: 14.4 us -> 15.9 us
  local copies, waits for them, and re-layouts: 0.02 us -> 0.84 us
    all_gather x1 -> x0, blocking collectives: 3.15 us -> none  [local(): own = lax.all_gather(pack, 'sub', axis=0, tiled=True)]
    ppermute x0 -> x1, starting transfers between devices: none -> 1.42 us  [local(): own = jnp.concatenate([pack, lax.ppermute(pack, 'sub', [(0, 1), (1, 0)])])]
    unnamed x10 -> x11, local copies, waits for them, and re-layouts: 0.02 us -> 0.83 us
  transfers between devices with their start and end apart: 5 -> 6, of which waited for: 3 -> 4; matrix products, arithmetic and copies ran while one was open for 0% -> 3% of each run, Pallas kernels for 21% -> 21%
where the time goes in v5:
time: 31.1 us; the launch traced here: 30.9 us
  starting transfers between devices  15.9 us (51%)
  Pallas kernels  11.7 us (38%)
  waiting for transfers between devices  2.41 us (8%)
  local copies, waits for them, and re-layouts  0.84 us (3%)
    all_to_all x1, starting transfers between devices, local(): all_roots = lax.all_to_all(roots, every, 0, 0, tiled=True)  9.09 us
    pallas_call x1, Pallas kernels, local(): pl.pallas_call(window_kernel, out_shape=(shape((NV, 1024), F32), shape((K...  6.61 us
    ppermute x1, starting transfers between devices, local(): inner_mine = lax.ppermute(own, every, INNER)  2.77 us
    pallas_call x1, Pallas kernels, local(): pl.pallas_call(upward_kernel, out_shape=(shape((PAIRS, NV, 128), BF), sha...  2.77 us
    pallas_call x1, Pallas kernels, local(): pl.pallas_call(top_kernel, out_shape=shape((NV, 1024), F32), in_specs=[sp...  2.34 us
    ppermute x1, starting transfers between devices, local(): own = jnp.concatenate([pack, lax.ppermute(pack, 'sub', [(0, 1), (1, 0)])])  1.42 us
    ppermute x1, starting transfers between devices, local(): outer_mine = lax.ppermute(own, every, OUTER)  1.38 us
    ppermute x1, starting transfers between devices, local(): outer_other = lax.ppermute(outer_mine, 'sub', [(0, 1), (1, 0)])  1.15 us
  transfers between devices with their start and end apart: 6, of which 4 were waited for; matrix products, arithmetic and copies ran while one was open for 3% of the time, Pallas kernels for 21%

profile of v5, /device:TPU:1, one launch (start us, length us, event | category | flops | bytes accessed | tf_op | source)
XLA Modules:
  0.0 30.9 jit_solution(16277191200051090642)
XLA Ops:
  0.0 0.0 copy-start.2
  0.0 0.0 copy-start.4
  0.0 0.0 copy-start.1
  0.0 2.8 %upward.1 = (bf16[24,8,128]{2,1,0:T(8,128)(2,1)}, bf16[128,4,128]{2,1,0:T(4,128)(2,1)}) custom-call(bf16[8,1024]{1,0:T(8,128)(2,1)} %density.1, bf16[16,64,64]{2,1,0:T(8,128)(2,1)} %basis.3, bf16[15,64,128]{2,1,0:T(8,128)(2,1)} %transfer.4), custom_call_target="tpu_custom_call" | custom-call | flops 20000000000 | bytes 1000000 | tf_op jit(solution)/shard_map/upward/pallas_call | solution.py:279
  2.8 1.4 %collective-permute-start = (bf16[24,8,128]{2,1,0:T(8,128)(2,1)}, bf16[24,8,128]{2,1,0:T(8,128)(2,1)S(1)}, u32[]{:S(2)}, u32[]{:S(2)}) collective-permute-start(bf16[24,8,128]{2,1,0:T(8,128)(2,1)} %get-tuple-element.11), channel_id=1, source_target_pairs={{0,1},{1,0},{2,3},{3,2},{4,5},{5,4},{6,7},{7,6},{8,9},{9,8},{10,11... | collective-permute-start | bytes 147464 | tf_op jit(solution)/shard_map/ppermute | solution.py:289
  4.2 0.8 %constant_dynamic-update-slice_fusion.1 = bf16[48,8,128]{2,1,0:T(8,128)(2,1)S(1)} fusion(bf16[24,8,128]{2,1,0:T(8,128)(2,1)} %get-tuple-element.11), kind=kLoop, calls=%fused_computation.1 | loop fusion | bytes 98304
  5.0 0.3 collective-permute-done
  5.3 1.4 %collective-permute-start.3 = (bf16[48,8,128]{2,1,0:T(8,128)(2,1)S(1)}, bf16[48,8,128]{2,1,0:T(8,128)(2,1)S(1)}, u32[]{:S(2)}, u32[]{:S(2)}) collective-permute-start(bf16[48,8,128]{2,1,0:T(8,128)(2,1)S(1)} %constant_dynamic-update-slice_fusion.own), channel_id=1, source_target_pairs={{2,4},{4,2},{6,8},{8,6},{10,12},{12,10},{14,16},{16,14},{18,20},{2... | collective-permute-start | bytes 294920 | tf_op jit(solution)/shard_map/ppermute | solution.py:291
  6.7 2.8 %collective-permute-start.1 = (bf16[48,8,128]{2,1,0:T(8,128)(2,1)S(1)}, bf16[48,8,128]{2,1,0:T(8,128)(2,1)S(1)}, u32[]{:S(2)}, u32[]{:S(2)}) collective-permute-start(bf16[48,8,128]{2,1,0:T(8,128)(2,1)S(1)} %constant_dynamic-update-slice_fusion.own), channel_id=1, source_target_pairs={{0,2},{2,0},{4,6},{6,4},{8,10},{10,8},{12,14},{14,12},{16,18},{18,... | collective-permute-start | bytes 294920 | tf_op jit(solution)/shard_map/ppermute | solution.py:290
  9.5 9.1 %all-to-all-start = ((bf16[128,4,128]{2,1,0:T(4,128)(2,1)}), bf16[128,4,128]{2,1,0:T(4,128)(2,1)S(1)}, u32[]{:S(2)}, u32[]{:S(2)}) async-start(bf16[128,4,128]{2,1,0:T(4,128)(2,1)} %get-tuple-element.10), calls=%async_computation | async-start | bytes 262144 | tf_op jit(solution)/shard_map/all_to_all | solution.py:292
  18.5 0.0 collective-permute-done.3.outer_mine
  18.6 1.1 %collective-permute-start.4 = (bf16[48,8,128]{2,1,0:T(8,128)(2,1)S(1)}, bf16[48,8,128]{2,1,0:T(8,128)(2,1)S(1)}, u32[]{:S(2)}, u32[]{:S(2)}) collective-permute-start(bf16[48,8,128]{2,1,0:T(8,128)(2,1)S(1)} %collective-permute-done.3.outer_mine), channel_id=1, source_target_pairs={{0,1},{1,0},{2,3},{3,2},{4,5},{5,4},{6,7},{7,6},{8,9},{9,8},{10,11... | collective-permute-start | bytes 294920 | tf_op jit(solution)/shard_map/ppermute | solution.py:294
  19.7 0.0 collective-permute-done.1.inner_mine
  19.7 0.1 collective-permute-start.2
  19.8 0.8 %collective-permute-done.4.outer_other = bf16[48,8,128]{2,1,0:T(8,128)(2,1)S(1)} collective-permute-done((bf16[48,8,128]{2,1,0:T(8,128)(2,1)S(1)}, bf16[48,8,128]{2,1,0:T(8,128)(2,1)S(1)}, u32[]{:S(2)}, u32[]{:S(2)}) %collective-permute-start.4) | collective-permute-done | bytes 98336 | tf_op jit(solution)/shard_map/ppermute | solution.py:294
  20.7 0.4 %collective-permute-done.2.inner_other = bf16[48,8,128]{2,1,0:T(8,128)(2,1)S(1)} collective-permute-done((bf16[48,8,128]{2,1,0:T(8,128)(2,1)S(1)}, bf16[48,8,128]{2,1,0:T(8,128)(2,1)S(1)}, u32[]{:S(2)}, u32[]{:S(2)}) %collective-permute-start.2) | collective-permute-done | bytes 98336 | tf_op jit(solution)/shard_map/ppermute | solution.py:293
  21.0 0.0 copy-done.2
  21.0 0.0 copy-done.4
  21.0 0.0 copy-done.1
  21.0 0.0 copy-start
  21.0 0.0 copy-start.3
  21.0 6.6 %window.1 = (f32[8,1024]{1,0:T(8,128)S(1)}, bf16[64,1024]{1,0:T(8,128)(2,1)S(1)}, bf16[64,768]{1,0:T(8,128)(2,1)S(1)}) custom-call(bf16[48,8,128]{2,1,0:T(8,128)(2,1)S(1)} %constant_dynamic-update-slice_fusion.own, bf16[48,8,128]{2,1,0:T(8,128)(2,1)S(1)} %collective-permute-done.1.inner_mine, bf16[48,8,128]{2,1,0:T(8,128)(2,1)S(1)} %collective-permute-done.2.inner_other, ...), custom_call_target="tpu_custom_call" | custom-call | flops 120000000 | bytes 8000000 | tf_op jit(solution)/shard_map/window/pallas_call | solution.py:295
  27.7 0.9 %all-to-all-done.roots = bf16[128,4,128]{2,1,0:T(4,128)(2,1)S(1)} async-done(((bf16[128,4,128]{2,1,0:T(4,128)(2,1)}), bf16[128,4,128]{2,1,0:T(4,128)(2,1)S(1)}, u32[]{:S(2)}, u32[]{:S(2)}) %all-to-all-start) | async-done | bytes 131104 | tf_op jit(solution)/shard_map/all_to_all | solution.py:292
  28.6 0.0 copy-done
  28.6 0.0 copy-done.3
  28.6 2.3 %top.1 = f32[8,1024]{1,0:T(8,128)} custom-call(bf16[128,4,128]{2,1,0:T(4,128)(2,1)S(1)} %all-to-all-done.roots, bf16[126,64,128]{2,1,0:T(8,128)(2,1)S(1)} %copy-done, s32[2,126]{1,0:T(2,128)S(1)} %bitcast.4, f32[8,1024]{1,0:T(8,128)S(1)} %get-tuple-element.12.partial, bf16[64,1024]{1,0:T(8,128)(2,1)S(1)} %get-tuple-element.13.onward, ...), custom_call_target="tpu_custom_call" | custom-call | tf_op jit(solution)/shard_map/top/pallas_call | solution.py:336
  (1 shorter events, 0.0 us)
Async XLA Ops:
  0.0 21.0 %copy-start.2 = (s32[31,16]{0,1:T(8,128)S(1)}, s32[31,16]{0,1:T(8,128)}, u32[]{:S(2)}) copy-start(s32[31,16]{0,1:T(8,128)} %param.18) | copy-start | bytes 5956
  0.0 21.0 %copy-start.4 = (s32[16]{0:T(128)S(1)}, s32[16]{0:T(128)}, u32[]{:S(2)}) copy-start(s32[16]{0:T(128)} %param.14) | copy-start | bytes 196
  0.0 21.0 %copy-start.1 = (s32[16,24]{1,0:T(8,128)S(1)}, s32[16,24]{1,0:T(8,128)}, u32[]{:S(2)}) copy-start(s32[16,24]{1,0:T(8,128)} %near_ids_in.1) | copy-start | bytes 4612
  2.8 2.5 %collective-permute-start = (bf16[24,8,128]{2,1,0:T(8,128)(2,1)}, bf16[24,8,128]{2,1,0:T(8,128)(2,1)S(1)}, u32[]{:S(2)}, u32[]{:S(2)}) collective-permute-start(bf16[24,8,128]{2,1,0:T(8,128)(2,1)} %get-tuple-element.11), channel_id=1, source_target_pairs={{0,1},{1,0},{2,3},{3,2},{4,5},{5,4},{6,7},{7,6},{8,9},{9,8},{10,11... | collective-permute-start | bytes 147464 | tf_op jit(solution)/shard_map/ppermute | solution.py:289
  5.3 13.2 %collective-permute-start.3 = (bf16[48,8,128]{2,1,0:T(8,128)(2,1)S(1)}, bf16[48,8,128]{2,1,0:T(8,128)(2,1)S(1)}, u32[]{:S(2)}, u32[]{:S(2)}) collective-permute-start(bf16[48,8,128]{2,1,0:T(8,128)(2,1)S(1)} %constant_dynamic-update-slice_fusion.own), channel_id=1, source_target_pairs={{2,4},{4,2},{6,8},{8,6},{10,12},{12,10},{14,16},{16,14},{18,20},{2... | collective-permute-start | bytes 294920 | tf_op jit(solution)/shard_map/ppermute | solution.py:291
  6.7 13.0 %collective-permute-start.1 = (bf16[48,8,128]{2,1,0:T(8,128)(2,1)S(1)}, bf16[48,8,128]{2,1,0:T(8,128)(2,1)S(1)}, u32[]{:S(2)}, u32[]{:S(2)}) collective-permute-start(bf16[48,8,128]{2,1,0:T(8,128)(2,1)S(1)} %constant_dynamic-update-slice_fusion.own), channel_id=1, source_target_pairs={{0,2},{2,0},{4,6},{6,4},{8,10},{10,8},{12,14},{14,12},{16,18},{18,... | collective-permute-start | bytes 294920 | tf_op jit(solution)/shard_map/ppermute | solution.py:290
  9.5 19.1 %all-to-all-start = ((bf16[128,4,128]{2,1,0:T(4,128)(2,1)}), bf16[128,4,128]{2,1,0:T(4,128)(2,1)S(1)}, u32[]{:S(2)}, u32[]{:S(2)}) async-start(bf16[128,4,128]{2,1,0:T(4,128)(2,1)} %get-tuple-element.10), calls=%async_computation | async-start | bytes 262144 | tf_op jit(solution)/shard_map/all_to_all | solution.py:292
  18.6 2.1 %collective-permute-start.4 = (bf16[48,8,128]{2,1,0:T(8,128)(2,1)S(1)}, bf16[48,8,128]{2,1,0:T(8,128)(2,1)S(1)}, u32[]{:S(2)}, u32[]{:S(2)}) collective-permute-start(bf16[48,8,128]{2,1,0:T(8,128)(2,1)S(1)} %collective-permute-done.3.outer_mine), channel_id=1, source_target_pairs={{0,1},{1,0},{2,3},{3,2},{4,5},{5,4},{6,7},{7,6},{8,9},{9,8},{10,11... | collective-permute-start | bytes 294920 | tf_op jit(solution)/shard_map/ppermute | solution.py:294
  19.7 1.3 %collective-permute-start.2 = (bf16[48,8,128]{2,1,0:T(8,128)(2,1)S(1)}, bf16[48,8,128]{2,1,0:T(8,128)(2,1)S(1)}, u32[]{:S(2)}, u32[]{:S(2)}) collective-permute-start(bf16[48,8,128]{2,1,0:T(8,128)(2,1)S(1)} %collective-permute-done.1.inner_mine), channel_id=1, source_target_pairs={{0,1},{1,0},{2,3},{3,2},{4,5},{5,4},{6,7},{7,6},{8,9},{9,8},{10,11... | collective-permute-start | bytes 294920 | tf_op jit(solution)/shard_map/ppermute | solution.py:293
  21.0 7.6 %copy-start = (bf16[126,64,128]{2,1,0:T(8,128)(2,1)S(1)}, bf16[126,64,128]{2,1,0:T(8,128)(2,1)}, u32[]{:S(2)}) copy-start(bf16[126,64,128]{2,1,0:T(8,128)(2,1)} %transfer.5) | copy-start | bytes 6193156
  21.0 7.5 %copy-start.3 = (s32[126,2]{0,1:T(2,128)S(1)}, s32[126,2]{0,1:T(2,128)}, u32[]{:S(2)}) copy-start(s32[126,2]{0,1:T(2,128)} %param.21) | copy-start | bytes 3028

commit v6 on v5

--- a/solution.py
+++ b/solution.py
@@ -91,16 +91,21 @@
         joined = beside(dot(pair[:, :K], basis[2 * p]), dot(pair[:, K:], basis[2 * p + 1])).astype(BF)
         pack[8 + p] = joined
         level.append(joined)
-    made = [dot_t(transfer[m], pair).astype(BF) for m, pair in enumerate(level)]
-    columns, first = list(made), 8
-    while len(made) > 1:
-        made = [
-            dot(transfer[first + q], stacked(made[2 * q], made[2 * q + 1])).astype(BF)
-            for q in range(len(made) // 2)
-        ]
-        first += len(made)
-        columns += made
-    rows = dot_t(unit(NV), stacked(*columns))
+    grand = [
+        beside(
+            dot(transfer[8 + q, :, :K], transfer[2 * q]).astype(BF),
+            dot(transfer[8 + q, :, K:], transfer[2 * q + 1]).astype(BF),
+        )
+        for q in range(4)
+    ]
+    root_map = beside(
+        dot(transfer[14, :, :K], transfer[12]).astype(BF), dot(transfer[14, :, K:], transfer[13]).astype(BF)
+    )
+    second = [dot_t(grand[q], beside(level[2 * q], level[2 * q + 1])).astype(BF) for q in range(4)]
+    first = [dot_t(transfer[m], pair).astype(BF) for m, pair in enumerate(level)]
+    top = dot(root_map, stacked(*second)).astype(BF)
+    third = [dot(transfer[12 + q], stacked(second[2 * q], second[2 * q + 1])).astype(BF) for q in range(2)]
+    rows = stacked(*first, *second, *third, top).astype(F32).T
     for q in range(7):
         pack[16 + q] = rows[:, 128 * q : 128 * q + 128].astype(BF)
     root = rows[:, 896:]
@@ -111,9 +116,9 @@
 
 def window_kernel(
     own, inner_mine, inner_other, outer_mine, outer_other, near_ids_in, near_count_in, coupling_ids_in, near_blocks,
-    coupling, transfer, basis, top_transfer, top_coupling, partial, onward, shares, window, arrived, near_raw,
-    near_count, coupling_raw, near_nodes, coupling_nodes, near_ids, coupling_ids, near_held, coupling_held, transfer_held, basis_held, rows_held, links_held, raw_sems,
-    id_sems, arrival_sems, near_sems, coupling_sems, small_sems, row_sems, link_sems,
+    coupling, transfer, basis, top_transfer, top_coupling, partial, onward, shares, fifth, sixth, window, arrived, near_raw,
+    near_count, coupling_raw, near_nodes, coupling_nodes, near_ids, coupling_ids, near_held, coupling_held, transfer_held, basis_held, rows_held, links_held, tall, raw_sems,
+    id_sems, arrival_sems, near_sems, coupling_sems, small_sems, row_sems, link_sems, tall_sems,
 ):
     device = lax.axis_index("leaf") * 2 + lax.axis_index("sub")
     copy = pltpu.make_async_copy
@@ -130,6 +135,7 @@
     small_copies = [copy(transfer, transfer_held, small_sems.at[0]), copy(basis, basis_held, small_sems.at[1])]
     places = [first + jnp.right_shift(device, t) for t, first in enumerate(FIRSTS, 1)]
     row_copies = [copy(top_transfer.at[row], rows_held.at[t], row_sems.at[t]) for t, row in enumerate(places)]
+    tall_copy = copy(top_transfer.at[pl.ds(112, 14)], tall, tall_sems.at[0])
     link_copies = [copy(top_coupling.at[row], links_held.at[t], link_sems.at[t]) for t, row in enumerate(places)]
     coupling_copies = [
         copy(coupling.at[pl.ds(a, n)], coupling_held.at[pl.ds(a, n)], coupling_sems.at[i])
@@ -140,7 +146,7 @@
         for a in range(0, LEAVES, 8)
     ]
     queue = coupling_copies + near_copies
-    for one in raw_copies + arrivals + queue[:1] + row_copies + link_copies + small_copies + queue[1:AHEAD]:
+    for one in raw_copies + arrivals + queue[:1] + row_copies + link_copies + small_copies + [tall_copy] + queue[1:AHEAD]:
         one.start()
 
     def take(index):
@@ -188,7 +194,7 @@
         made = [descend(state[m], offset + m, at + 2 * m) for m in range(count)]
         return [child for one in made for child in split(*one)]
 
-    for one in id_copies + row_copies + link_copies + small_copies:
+    for one in id_copies + row_copies + link_copies + small_copies + [tall_copy]:
         one.wait()
     coupled_rows = {}
     path = unit(K)
@@ -200,6 +206,12 @@
         for r in range(30 - 3 * t, max(27 - 3 * t, 15), -1):
             coupled_rows[r] = coupled(r)
         shares[:, 128 * t : 128 * t + 128] = dot(path, links_held[t]).astype(BF)
+        if t < 4:
+            fifth[t, :, :128] = dot(tall[8 + t, :, :K], tall[2 * t]).astype(BF)
+            fifth[t, :, 128:] = dot(tall[8 + t, :, K:], tall[2 * t + 1]).astype(BF)
+        else:
+            sixth[t - 4, :, :256] = dot(tall[8 + t, :, :K], fifth[2 * t - 8]).astype(BF)
+            sixth[t - 4, :, 256:] = dot(tall[8 + t, :, K:], fifth[2 * t - 7]).astype(BF)
     state = [stacked(coupled_rows[30], unit(K).astype(F32))]
     take(1)
     for height in (4, 3, 2):
@@ -221,7 +233,7 @@
         onward[:, span] = pair[NV:].astype(BF)
 
 
-def top_kernel(roots, transfer, ids, partial, onward, shares, potential, nodes, held_ids, sems):
+def top_kernel(roots, transfer, ids, partial, onward, shares, fifth, sixth, potential, nodes, held_ids, sems):
     device = lax.axis_index("leaf") * 2 + lax.axis_index("sub")
     id_copy = pltpu.make_async_copy(ids, held_ids, sems.at[0])
     id_copy.start()
@@ -233,11 +245,17 @@
         lower = jnp.where(low4, pltpu.roll(a, K, 1), b)
         made.append(dot_t(transfer[m], stacked(upper, lower).astype(BF)).astype(BF))
     for t, first in enumerate(FIRSTS):
-        if t:
+        if 0 < t < 4:
             made = [
                 dot(transfer[first + m], stacked(made[2 * m], made[2 * m + 1])).astype(BF)
                 for m in range(len(made) // 2)
             ]
+        elif t == 4:
+            made = [dot(fifth[m], stacked(*third[4 * m : 4 * m + 4])).astype(BF) for m in range(4)]
+        elif t == 5:
+            made = [dot(sixth[m], stacked(*third[8 * m : 8 * m + 8])).astype(BF) for m in range(2)]
+        if t == 2:
+            third = made
         for m, node in enumerate(made):
             nodes[first + m] = node
     id_copy.wait()
@@ -245,8 +263,7 @@
     for t, first in enumerate(FIRSTS, 1):
         row = first + jnp.right_shift(device, t)
         sources += [nodes[first + held_ids[0, row]], nodes[first + held_ids[1, row]]]
-    incoming = dot(shares[...], stacked(*sources)).astype(BF)
-    incoming = dot_t(unit(NV), incoming).astype(BF)
+    incoming = dot(shares[...], stacked(*sources)).T.astype(BF)
     potential[...] = partial[...] + dot(incoming, onward[...])
 
 
@@ -292,15 +309,17 @@
     all_roots = lax.all_to_all(roots, every, 0, 0, tiled=True)
     inner_other = lax.ppermute(inner_mine, "sub", [(0, 1), (1, 0)])
     outer_other = lax.ppermute(outer_mine, "sub", [(0, 1), (1, 0)])
-    partial, onward, shares = pl.pallas_call(
+    partial, onward, shares, fifth, sixth = pl.pallas_call(
         window_kernel,
         out_shape=(
             shape((NV, 1024), F32),
             shape((K, 1024), BF),
             shape((K, 768), BF),
+            shape((4, K, 256), BF),
+            shape((2, K, 512), BF),
         ),
         in_specs=[spec(ANY)] * 14,
-        out_specs=(spec(VMEM),) * 3,
+        out_specs=(spec(VMEM),) * 5,
         scratch_shapes=[
             pltpu.VMEM((ZERO + 2, NV, 128), F32),
             pltpu.VMEM((5, 2 * PAIRS, NV, 128), BF),
@@ -317,6 +336,7 @@
             pltpu.VMEM((LEAVES, 64, K), BF),
             pltpu.VMEM((6, K, 128), BF),
             pltpu.VMEM((6, K, 128), BF),
+            pltpu.VMEM((14, K, 128), BF),
             pltpu.SemaphoreType.DMA((3,)),
             pltpu.SemaphoreType.DMA((2,)),
             pltpu.SemaphoreType.DMA((5,)),
@@ -325,8 +345,9 @@
             pltpu.SemaphoreType.DMA((2,)),
             pltpu.SemaphoreType.DMA((6,)),
             pltpu.SemaphoreType.DMA((6,)),
+            pltpu.SemaphoreType.DMA((1,)),
         ],
-        compiler_params=pltpu.CompilerParams(vmem_limit_bytes=53 << 20),
+        compiler_params=pltpu.CompilerParams(vmem_limit_bytes=52 << 20),
         cost_estimate=pl.CostEstimate(flops=120_000_000, bytes_accessed=8_000_000, transcendentals=0),
         name="window",
     )(
@@ -336,7 +357,7 @@
     return pl.pallas_call(
         top_kernel,
         out_shape=shape((NV, 1024), F32),
-        in_specs=[spec(VMEM)] * 2 + [spec(ANY)] + [spec(VMEM)] * 3,
+        in_specs=[spec(VMEM)] * 2 + [spec(ANY)] + [spec(VMEM)] * 5,
         out_specs=spec(VMEM),
         scratch_shapes=[
             pltpu.VMEM((TOP, K, NV), BF),
@@ -345,7 +366,7 @@
         ],
         compiler_params=pltpu.CompilerParams(vmem_limit_bytes=20 << 20),
         name="top",
-    )(all_roots, top_transfer, top_coupling_ids.T, partial, onward, shares)
+    )(all_roots, top_transfer, top_coupling_ids.T, partial, onward, shares, fifth, sixth)
 
 
 def solution(mesh):

time: 31.1 us -> 30.7 us (0.987)
  Pallas kernels: 11.7 us -> 10.8 us
  waiting for transfers between devices: 2.41 us -> 2.87 us
    pallas_call x1, Pallas kernels: 6.61 us -> 6.13 us  [local(): pl.pallas_call(window_kernel, out_shape=(shape((NV, 1024), F32), shape((K...]
    all_to_all x1, waiting for transfers between devices: 0.91 us -> 1.37 us  [local(): all_roots = lax.all_to_all(roots, every, 0, 0, tiled=True)]
    unnamed x11 -> x15, local copies, waits for them, and re-layouts: 0.83 us -> 0.83 us
  transfers between devices with their start and end apart: 6 -> 6, of which waited for: 4 -> 4; matrix products, arithmetic and copies ran while one was open for 3% -> 3% of each run, Pallas kernels for 21% -> 20%
where the time goes in v6:
time: 30.7 us; the launch traced here: 30.5 us
  starting transfers between devices  15.9 us (52%)
  Pallas kernels  10.8 us (35%)
  waiting for transfers between devices  2.87 us (9%)
  local copies, waits for them, and re-layouts  0.84 us (3%)
    all_to_all x1, starting transfers between devices, local(): all_roots = lax.all_to_all(roots, every, 0, 0, tiled=True)  9.09 us
    pallas_call x1, Pallas kernels, local(): pl.pallas_call(window_kernel, out_shape=(shape((NV, 1024), F32), shape((K...  6.13 us
    ppermute x1, starting transfers between devices, local(): inner_mine = lax.ppermute(own, every, INNER)  2.77 us
    pallas_call x1, Pallas kernels, local(): pl.pallas_call(upward_kernel, out_shape=(shape((PAIRS, NV, 128), BF), sha...  2.5 us
    pallas_call x1, Pallas kernels, local(): pl.pallas_call(top_kernel, out_shape=shape((NV, 1024), F32), in_specs=[sp...  2.12 us
    ppermute x1, starting transfers between devices, local(): own = jnp.concatenate([pack, lax.ppermute(pack, 'sub', [(0, 1), (1, 0)])])  1.41 us
    ppermute x1, starting transfers between devices, local(): outer_mine = lax.ppermute(own, every, OUTER)  1.39 us
    all_to_all x1, waiting for transfers between devices, local(): all_roots = lax.all_to_all(roots, every, 0, 0, tiled=True)  1.37 us
  transfers between devices with their start and end apart: 6, of which 4 were waited for; matrix products, arithmetic and copies ran while one was open for 3% of the time, Pallas kernels for 20%

profile of v6, /device:TPU:1, one launch (start us, length us, event | category | flops | bytes accessed | tf_op | source)
XLA Modules:
  0.0 30.5 jit_solution(10326205602180408428)
XLA Ops:
  0.0 0.0 copy-start.2
  0.0 0.0 copy-start.1
  0.0 0.0 copy-start.4
  0.0 0.0 copy-start.6
  0.0 0.0 copy-start.3
  0.0 2.5 %upward.1 = (bf16[24,8,128]{2,1,0:T(8,128)(2,1)}, bf16[128,4,128]{2,1,0:T(4,128)(2,1)}) custom-call(bf16[8,1024]{1,0:T(8,128)(2,1)} %density.1, bf16[16,64,64]{2,1,0:T(8,128)(2,1)} %basis.3, bf16[15,64,128]{2,1,0:T(8,128)(2,1)} %transfer.4), custom_call_target="tpu_custom_call" | custom-call | flops 20000000000 | bytes 1000000 | tf_op jit(solution)/shard_map/upward/pallas_call | solution.py:296
  2.5 1.4 %collective-permute-start = (bf16[24,8,128]{2,1,0:T(8,128)(2,1)}, bf16[24,8,128]{2,1,0:T(8,128)(2,1)S(1)}, u32[]{:S(2)}, u32[]{:S(2)}) collective-permute-start(bf16[24,8,128]{2,1,0:T(8,128)(2,1)} %get-tuple-element.13), channel_id=1, source_target_pairs={{0,1},{1,0},{2,3},{3,2},{4,5},{5,4},{6,7},{7,6},{8,9},{9,8},{10,11... | collective-permute-start | bytes 147464 | tf_op jit(solution)/shard_map/ppermute | solution.py:306
  3.9 0.8 %constant_dynamic-update-slice_fusion.1 = bf16[48,8,128]{2,1,0:T(8,128)(2,1)S(1)} fusion(bf16[24,8,128]{2,1,0:T(8,128)(2,1)} %get-tuple-element.13), kind=kLoop, calls=%fused_computation.1 | loop fusion | bytes 98304
  4.7 0.3 collective-permute-done
  5.0 1.4 %collective-permute-start.3 = (bf16[48,8,128]{2,1,0:T(8,128)(2,1)S(1)}, bf16[48,8,128]{2,1,0:T(8,128)(2,1)S(1)}, u32[]{:S(2)}, u32[]{:S(2)}) collective-permute-start(bf16[48,8,128]{2,1,0:T(8,128)(2,1)S(1)} %constant_dynamic-update-slice_fusion.own), channel_id=1, source_target_pairs={{2,4},{4,2},{6,8},{8,6},{10,12},{12,10},{14,16},{16,14},{18,20},{2... | collective-permute-start | bytes 294920 | tf_op jit(solution)/shard_map/ppermute | solution.py:308
  6.4 2.8 %collective-permute-start.1 = (bf16[48,8,128]{2,1,0:T(8,128)(2,1)S(1)}, bf16[48,8,128]{2,1,0:T(8,128)(2,1)S(1)}, u32[]{:S(2)}, u32[]{:S(2)}) collective-permute-start(bf16[48,8,128]{2,1,0:T(8,128)(2,1)S(1)} %constant_dynamic-update-slice_fusion.own), channel_id=1, source_target_pairs={{0,2},{2,0},{4,6},{6,4},{8,10},{10,8},{12,14},{14,12},{16,18},{18,... | collective-permute-start | bytes 294920 | tf_op jit(solution)/shard_map/ppermute | solution.py:307
  9.2 9.1 %all-to-all-start = ((bf16[128,4,128]{2,1,0:T(4,128)(2,1)}), bf16[128,4,128]{2,1,0:T(4,128)(2,1)S(1)}, u32[]{:S(2)}, u32[]{:S(2)}) async-start(bf16[128,4,128]{2,1,0:T(4,128)(2,1)} %get-tuple-element.12), calls=%async_computation | async-start | bytes 262144 | tf_op jit(solution)/shard_map/all_to_all | solution.py:309
  18.3 0.0 collective-permute-done.3.outer_mine
  18.3 1.1 %collective-permute-start.4 = (bf16[48,8,128]{2,1,0:T(8,128)(2,1)S(1)}, bf16[48,8,128]{2,1,0:T(8,128)(2,1)S(1)}, u32[]{:S(2)}, u32[]{:S(2)}) collective-permute-start(bf16[48,8,128]{2,1,0:T(8,128)(2,1)S(1)} %collective-permute-done.3.outer_mine), channel_id=1, source_target_pairs={{0,1},{1,0},{2,3},{3,2},{4,5},{5,4},{6,7},{7,6},{8,9},{9,8},{10,11... | collective-permute-start | bytes 294920 | tf_op jit(solution)/shard_map/ppermute | solution.py:311
  19.5 0.0 collective-permute-done.1.inner_mine
  19.5 0.1 collective-permute-start.2
  19.6 0.8 %collective-permute-done.4.outer_other = bf16[48,8,128]{2,1,0:T(8,128)(2,1)S(1)} collective-permute-done((bf16[48,8,128]{2,1,0:T(8,128)(2,1)S(1)}, bf16[48,8,128]{2,1,0:T(8,128)(2,1)S(1)}, u32[]{:S(2)}, u32[]{:S(2)}) %collective-permute-start.4) | collective-permute-done | bytes 98336 | tf_op jit(solution)/shard_map/ppermute | solution.py:311
  20.4 0.4 %collective-permute-done.2.inner_other = bf16[48,8,128]{2,1,0:T(8,128)(2,1)S(1)} collective-permute-done((bf16[48,8,128]{2,1,0:T(8,128)(2,1)S(1)}, bf16[48,8,128]{2,1,0:T(8,128)(2,1)S(1)}, u32[]{:S(2)}, u32[]{:S(2)}) %collective-permute-start.2) | collective-permute-done | bytes 98336 | tf_op jit(solution)/shard_map/ppermute | solution.py:310
  20.8 0.0 copy-done.2
  20.8 0.0 copy-done.1
  20.8 0.0 copy-done.4
  20.8 0.0 copy-done.6
  20.8 0.0 copy-done.3
  20.8 0.0 copy-start
  20.8 0.0 copy-start.5
  20.8 6.1 %window.1 = (f32[8,1024]{1,0:T(8,128)S(1)}, bf16[64,1024]{1,0:T(8,128)(2,1)S(1)}, bf16[64,768]{1,0:T(8,128)(2,1)S(1)}, bf16[4,64,256]{2,1,0:T(8,128)(2,1)S(1)}, bf16[2,64,512]{2,1,0:T(8,128)(2,1)S(1)}) custom-call(bf16[48,8,128]{2,1,0:T(8,128)(2,1)S(1)} %constant_dynamic-update-slice_fusion.own, bf16[48,8,128]{2,1,0:T(8,128)(2,1)S(1)} %collective-permute-done.1.inner_mine, ...), custom_call_target="tpu_custom_call" | custom-call | flops 120000000 | bytes 8000000 | tf_op jit(solution)/shard_map/window/pallas_call | solution.py:312
  27.0 1.4 %all-to-all-done.roots = bf16[128,4,128]{2,1,0:T(4,128)(2,1)S(1)} async-done(((bf16[128,4,128]{2,1,0:T(4,128)(2,1)}), bf16[128,4,128]{2,1,0:T(4,128)(2,1)S(1)}, u32[]{:S(2)}, u32[]{:S(2)}) %all-to-all-start) | async-done | bytes 131104 | tf_op jit(solution)/shard_map/all_to_all | solution.py:309
  28.3 0.0 copy-done
  28.3 0.0 copy-done.5
  28.3 2.1 %top.1 = f32[8,1024]{1,0:T(8,128)} custom-call(bf16[128,4,128]{2,1,0:T(4,128)(2,1)S(1)} %all-to-all-done.roots, bf16[126,64,128]{2,1,0:T(8,128)(2,1)S(1)} %copy-done, s32[2,126]{1,0:T(2,128)S(1)} %bitcast.4, f32[8,1024]{1,0:T(8,128)S(1)} %get-tuple-element.14.partial, bf16[64,1024]{1,0:T(8,128)(2,1)S(1)} %get-tuple-element.15.onward, ...), custom_call_target="tpu_custom_call" | custom-call | tf_op jit(solution)/shard_map/top/pallas_call | solution.py:357
  (1 shorter events, 0.0 us)
Async XLA Ops:
  0.0 20.8 %copy-start.2 = (bf16[15,64,128]{2,1,0:T(8,128)(2,1)S(1)}, bf16[15,64,128]{2,1,0:T(8,128)(2,1)}, u32[]{:S(2)}) copy-start(bf16[15,64,128]{2,1,0:T(8,128)(2,1)} %transfer.4) | copy-start | bytes 737284
  0.0 20.8 %copy-start.1 = (bf16[16,64,64]{2,1,0:T(8,128)(2,1)S(1)}, bf16[16,64,64]{2,1,0:T(8,128)(2,1)}, u32[]{:S(2)}) copy-start(bf16[16,64,64]{2,1,0:T(8,128)(2,1)} %basis.3) | copy-start | bytes 393220
  0.0 20.8 %copy-start.4 = (s32[31,16]{0,1:T(8,128)S(1)}, s32[31,16]{0,1:T(8,128)}, u32[]{:S(2)}) copy-start(s32[31,16]{0,1:T(8,128)} %param.18) | copy-start | bytes 5956
  0.0 20.8 %copy-start.6 = (s32[16]{0:T(128)S(1)}, s32[16]{0:T(128)}, u32[]{:S(2)}) copy-start(s32[16]{0:T(128)} %param.14) | copy-start | bytes 196
  0.0 20.8 %copy-start.3 = (s32[16,24]{1,0:T(8,128)S(1)}, s32[16,24]{1,0:T(8,128)}, u32[]{:S(2)}) copy-start(s32[16,24]{1,0:T(8,128)} %near_ids_in.1) | copy-start | bytes 4612
  2.5 2.5 %collective-permute-start = (bf16[24,8,128]{2,1,0:T(8,128)(2,1)}, bf16[24,8,128]{2,1,0:T(8,128)(2,1)S(1)}, u32[]{:S(2)}, u32[]{:S(2)}) collective-permute-start(bf16[24,8,128]{2,1,0:T(8,128)(2,1)} %get-tuple-element.13), channel_id=1, source_target_pairs={{0,1},{1,0},{2,3},{3,2},{4,5},{5,4},{6,7},{7,6},{8,9},{9,8},{10,11... | collective-permute-start | bytes 147464 | tf_op jit(solution)/shard_map/ppermute | solution.py:306
  5.0 13.3 %collective-permute-start.3 = (bf16[48,8,128]{2,1,0:T(8,128)(2,1)S(1)}, bf16[48,8,128]{2,1,0:T(8,128)(2,1)S(1)}, u32[]{:S(2)}, u32[]{:S(2)}) collective-permute-start(bf16[48,8,128]{2,1,0:T(8,128)(2,1)S(1)} %constant_dynamic-update-slice_fusion.own), channel_id=1, source_target_pairs={{2,4},{4,2},{6,8},{8,6},{10,12},{12,10},{14,16},{16,14},{18,20},{2... | collective-permute-start | bytes 294920 | tf_op jit(solution)/shard_map/ppermute | solution.py:308
  6.4 13.0 %collective-permute-start.1 = (bf16[48,8,128]{2,1,0:T(8,128)(2,1)S(1)}, bf16[48,8,128]{2,1,0:T(8,128)(2,1)S(1)}, u32[]{:S(2)}, u32[]{:S(2)}) collective-permute-start(bf16[48,8,128]{2,1,0:T(8,128)(2,1)S(1)} %constant_dynamic-update-slice_fusion.own), channel_id=1, source_target_pairs={{0,2},{2,0},{4,6},{6,4},{8,10},{10,8},{12,14},{14,12},{16,18},{18,... | collective-permute-start | bytes 294920 | tf_op jit(solution)/shard_map/ppermute | solution.py:307
  9.2 19.1 %all-to-all-start = ((bf16[128,4,128]{2,1,0:T(4,128)(2,1)}), bf16[128,4,128]{2,1,0:T(4,128)(2,1)S(1)}, u32[]{:S(2)}, u32[]{:S(2)}) async-start(bf16[128,4,128]{2,1,0:T(4,128)(2,1)} %get-tuple-element.12), calls=%async_computation | async-start | bytes 262144 | tf_op jit(solution)/shard_map/all_to_all | solution.py:309
  18.3 2.1 %collective-permute-start.4 = (bf16[48,8,128]{2,1,0:T(8,128)(2,1)S(1)}, bf16[48,8,128]{2,1,0:T(8,128)(2,1)S(1)}, u32[]{:S(2)}, u32[]{:S(2)}) collective-permute-start(bf16[48,8,128]{2,1,0:T(8,128)(2,1)S(1)} %collective-permute-done.3.outer_mine), channel_id=1, source_target_pairs={{0,1},{1,0},{2,3},{3,2},{4,5},{5,4},{6,7},{7,6},{8,9},{9,8},{10,11... | collective-permute-start | bytes 294920 | tf_op jit(solution)/shard_map/ppermute | solution.py:311
  19.5 1.3 %collective-permute-start.2 = (bf16[48,8,128]{2,1,0:T(8,128)(2,1)S(1)}, bf16[48,8,128]{2,1,0:T(8,128)(2,1)S(1)}, u32[]{:S(2)}, u32[]{:S(2)}) collective-permute-start(bf16[48,8,128]{2,1,0:T(8,128)(2,1)S(1)} %collective-permute-done.1.inner_mine), channel_id=1, source_target_pairs={{0,1},{1,0},{2,3},{3,2},{4,5},{5,4},{6,7},{7,6},{8,9},{9,8},{10,11... | collective-permute-start | bytes 294920 | tf_op jit(solution)/shard_map/ppermute | solution.py:310
  20.8 7.5 %copy-start = (bf16[126,64,128]{2,1,0:T(8,128)(2,1)S(1)}, bf16[126,64,128]{2,1,0:T(8,128)(2,1)}, u32[]{:S(2)}) copy-start(bf16[126,64,128]{2,1,0:T(8,128)(2,1)} %transfer.5) | copy-start | bytes 6193156
  20.8 7.5 %copy-start.5 = (s32[126,2]{0,1:T(2,128)S(1)}, s32[126,2]{0,1:T(2,128)}, u32[]{:S(2)}) copy-start(s32[126,2]{0,1:T(2,128)} %param.21) | copy-start | bytes 3028

commit v7 on v6

--- a/solution.py
+++ b/solution.py
@@ -85,12 +85,19 @@
 
 def upward_kernel(density, basis, transfer, pack, roots):
     level = []
-    for p in range(8):
-        pair = density[:, 128 * p : 128 * p + 128]
-        pack[p] = pair
-        joined = beside(dot(pair[:, :K], basis[2 * p]), dot(pair[:, K:], basis[2 * p + 1])).astype(BF)
-        pack[8 + p] = joined
-        level.append(joined)
+    block = lax.broadcasted_iota(jnp.int32, (4 * NV, 256), 0) // NV
+    own_lanes = block == lax.broadcasted_iota(jnp.int32, (4 * NV, 256), 1) // K
+    for q in range(4):
+        four = density[:, 256 * q : 256 * q + 256]
+        pack[2 * q], pack[2 * q + 1] = four[:, :128], four[:, 128:]
+        four = four.astype(F32)
+        spread = jnp.where(own_lanes, stacked(four, four, four, four), 0.0).astype(BF)
+        made = dot(spread, basis[4 * q : 4 * q + 4].reshape(256, K))
+        for half in range(2):
+            at = 16 * half
+            joined = beside(made[at : at + NV], made[at + NV : at + 16]).astype(BF)
+            pack[8 + 2 * q + half] = joined
+            level.append(joined)
     grand = [
         beside(
             dot(transfer[8 + q, :, :K], transfer[2 * q]).astype(BF),
@@ -238,22 +245,34 @@
     id_copy = pltpu.make_async_copy(ids, held_ids, sems.at[0])
     id_copy.start()
     low4 = lax.broadcasted_iota(jnp.int32, (4, 128), 1) < K
-    made = []
-    for m in range(64):
+
+    def pair(m):
         a, b = roots[2 * m].astype(F32), roots[2 * m + 1].astype(F32)
         upper = jnp.where(low4, a, pltpu.roll(b, K, 1))
         lower = jnp.where(low4, pltpu.roll(a, K, 1), b)
-        made.append(dot_t(transfer[m], stacked(upper, lower).astype(BF)).astype(BF))
+        return stacked(upper, lower)
+
+    side = lax.broadcasted_iota(jnp.int32, (128, 2 * NV), 1) // NV
+    blank, none = jnp.zeros((NV, 128), F32), jnp.zeros((128, 2 * NV), BF)
+    made = []
+    for m in range(32):
+        rows = stacked(beside(pair(m), blank), beside(blank, pair(m + 32))).astype(BF)
+        made.append(dot_t(beside(transfer[m], transfer[m + 32]), rows).astype(BF))
     for t, first in enumerate(FIRSTS):
+        half = 32 >> t
         if 0 < t < 4:
-            made = [
-                dot(transfer[first + m], stacked(made[2 * m], made[2 * m + 1])).astype(BF)
-                for m in range(len(made) // 2)
-            ]
-        elif t == 4:
-            made = [dot(fifth[m], stacked(*third[4 * m : 4 * m + 4])).astype(BF) for m in range(4)]
-        elif t == 5:
-            made = [dot(sixth[m], stacked(*third[8 * m : 8 * m + 8])).astype(BF) for m in range(2)]
+            below, made = made, []
+            for m in range(half):
+                both = stacked(below[2 * m], below[2 * m + 1])
+                both = stacked(jnp.where(side == 0, both, none), jnp.where(side == 1, both, none))
+                made.append(dot(beside(transfer[first + m], transfer[first + half + m]), both).astype(BF))
+        elif t >= 4:
+            maps, span = (fifth, 4) if t == 4 else (sixth, 8)
+            below, made = third, []
+            for m in range(half):
+                both = stacked(*below[span * m : span * m + span])
+                ends = dot(maps[m], both), dot(maps[half + m], both)
+                made.append(jnp.where(side[:K] == 0, *ends).astype(BF))
         if t == 2:
             third = made
         for m, node in enumerate(made):
@@ -261,9 +280,14 @@
     id_copy.wait()
     sources = []
     for t, first in enumerate(FIRSTS, 1):
-        row = first + jnp.right_shift(device, t)
-        sources += [nodes[first + held_ids[0, row]], nodes[first + held_ids[1, row]]]
-    incoming = dot(shares[...], stacked(*sources)).T.astype(BF)
+        row, half = first + jnp.right_shift(device, t), 64 >> t
+        for end in range(2):
+            node = held_ids[end, row]
+            upper_half = (node >= half).astype(jnp.int32)
+            found = nodes[first + jnp.bitwise_and(node, half - 1)]
+            sources.append(jnp.where(side[:K] == upper_half, found, none[:K]))
+    incoming = dot(shares[...], stacked(*sources)).T
+    incoming = (incoming[:NV] + incoming[NV:]).astype(BF)
     potential[...] = partial[...] + dot(incoming, onward[...])
 
 
@@ -360,7 +384,7 @@
         in_specs=[spec(VMEM)] * 2 + [spec(ANY)] + [spec(VMEM)] * 5,
         out_specs=spec(VMEM),
         scratch_shapes=[
-            pltpu.VMEM((TOP, K, NV), BF),
+            pltpu.VMEM((TOP, K, 2 * NV), BF),
             pltpu.SMEM((2, TOP), jnp.int32),
             pltpu.SemaphoreType.DMA((1,)),
         ],

time: 30.7 us -> 30.5 us (level)
  no operation moved by 1% of the time
where the time goes in v7:
time: 30.5 us; the launch traced here: 30.3 us
  starting transfers between devices  15.9 us (52%)
  Pallas kernels  10.6 us (35%)
  waiting for transfers between devices  2.86 us (9%)
  local copies, waits for them, and re-layouts  0.84 us (3%)
    all_to_all x1, starting transfers between devices, local(): all_roots = lax.all_to_all(roots, every, 0, 0, tiled=True)  9.08 us
    pallas_call x1, Pallas kernels, local(): pl.pallas_call(window_kernel, out_shape=(shape((NV, 1024), F32), shape((K...  6.14 us
    ppermute x1, starting transfers between devices, local(): inner_mine = lax.ppermute(own, every, INNER)  2.77 us
    pallas_call x1, Pallas kernels, local(): pl.pallas_call(upward_kernel, out_shape=(shape((PAIRS, NV, 128), BF), sha...  2.45 us
    pallas_call x1, Pallas kernels, local(): pl.pallas_call(top_kernel, out_shape=shape((NV, 1024), F32), in_specs=[sp...  2 us
    ppermute x1, starting transfers between devices, local(): own = jnp.concatenate([pack, lax.ppermute(pack, 'sub', [(0, 1), (1, 0)])])  1.41 us
    ppermute x1, starting transfers between devices, local(): outer_mine = lax.ppermute(own, every, OUTER)  1.4 us
    all_to_all x1, waiting for transfers between devices, local(): all_roots = lax.all_to_all(roots, every, 0, 0, tiled=True)  1.36 us
  transfers between devices with their start and end apart: 6, of which 4 were waited for; matrix products, arithmetic and copies ran while one was open for 3% of the time, Pallas kernels for 20%

profile of v7, /device:TPU:1, one launch (start us, length us, event | category | flops | bytes accessed | tf_op | source)
XLA Modules:
  0.0 30.3 jit_solution(15315273749664331767)
XLA Ops:
  0.0 0.0 copy-start.2
  0.0 0.0 copy-start.1
  0.0 0.0 copy-start.4
  0.0 0.0 copy-start.6
  0.0 0.0 copy-start.3
  0.0 2.4 %upward.1 = (bf16[24,8,128]{2,1,0:T(8,128)(2,1)}, bf16[128,4,128]{2,1,0:T(4,128)(2,1)}) custom-call(bf16[8,1024]{1,0:T(8,128)(2,1)} %density.1, bf16[16,64,64]{2,1,0:T(8,128)(2,1)} %basis.3, bf16[15,64,128]{2,1,0:T(8,128)(2,1)} %transfer.4), custom_call_target="tpu_custom_call" | custom-call | flops 20000000000 | bytes 1000000 | tf_op jit(solution)/shard_map/upward/pallas_call | solution.py:320
  2.5 1.4 %collective-permute-start = (bf16[24,8,128]{2,1,0:T(8,128)(2,1)}, bf16[24,8,128]{2,1,0:T(8,128)(2,1)S(1)}, u32[]{:S(2)}, u32[]{:S(2)}) collective-permute-start(bf16[24,8,128]{2,1,0:T(8,128)(2,1)} %get-tuple-element.13), channel_id=1, source_target_pairs={{0,1},{1,0},{2,3},{3,2},{4,5},{5,4},{6,7},{7,6},{8,9},{9,8},{10,11... | collective-permute-start | bytes 147464 | tf_op jit(solution)/shard_map/ppermute | solution.py:330
  3.9 0.8 %constant_dynamic-update-slice_fusion.1 = bf16[48,8,128]{2,1,0:T(8,128)(2,1)S(1)} fusion(bf16[24,8,128]{2,1,0:T(8,128)(2,1)} %get-tuple-element.13), kind=kLoop, calls=%fused_computation.1 | loop fusion | bytes 98304
  4.7 0.3 collective-permute-done
  5.0 1.4 %collective-permute-start.3 = (bf16[48,8,128]{2,1,0:T(8,128)(2,1)S(1)}, bf16[48,8,128]{2,1,0:T(8,128)(2,1)S(1)}, u32[]{:S(2)}, u32[]{:S(2)}) collective-permute-start(bf16[48,8,128]{2,1,0:T(8,128)(2,1)S(1)} %constant_dynamic-update-slice_fusion.own), channel_id=1, source_target_pairs={{2,4},{4,2},{6,8},{8,6},{10,12},{12,10},{14,16},{16,14},{18,20},{2... | collective-permute-start | bytes 294920 | tf_op jit(solution)/shard_map/ppermute | solution.py:332
  6.4 2.8 %collective-permute-start.1 = (bf16[48,8,128]{2,1,0:T(8,128)(2,1)S(1)}, bf16[48,8,128]{2,1,0:T(8,128)(2,1)S(1)}, u32[]{:S(2)}, u32[]{:S(2)}) collective-permute-start(bf16[48,8,128]{2,1,0:T(8,128)(2,1)S(1)} %constant_dynamic-update-slice_fusion.own), channel_id=1, source_target_pairs={{0,2},{2,0},{4,6},{6,4},{8,10},{10,8},{12,14},{14,12},{16,18},{18,... | collective-permute-start | bytes 294920 | tf_op jit(solution)/shard_map/ppermute | solution.py:331
  9.2 9.1 %all-to-all-start = ((bf16[128,4,128]{2,1,0:T(4,128)(2,1)}), bf16[128,4,128]{2,1,0:T(4,128)(2,1)S(1)}, u32[]{:S(2)}, u32[]{:S(2)}) async-start(bf16[128,4,128]{2,1,0:T(4,128)(2,1)} %get-tuple-element.12), calls=%async_computation | async-start | bytes 262144 | tf_op jit(solution)/shard_map/all_to_all | solution.py:333
  18.2 0.0 collective-permute-done.3.outer_mine
  18.3 1.1 %collective-permute-start.4 = (bf16[48,8,128]{2,1,0:T(8,128)(2,1)S(1)}, bf16[48,8,128]{2,1,0:T(8,128)(2,1)S(1)}, u32[]{:S(2)}, u32[]{:S(2)}) collective-permute-start(bf16[48,8,128]{2,1,0:T(8,128)(2,1)S(1)} %collective-permute-done.3.outer_mine), channel_id=1, source_target_pairs={{0,1},{1,0},{2,3},{3,2},{4,5},{5,4},{6,7},{7,6},{8,9},{9,8},{10,11... | collective-permute-start | bytes 294920 | tf_op jit(solution)/shard_map/ppermute | solution.py:335
  19.4 0.0 collective-permute-done.1.inner_mine
  19.4 0.1 collective-permute-start.2
  19.5 0.8 %collective-permute-done.4.outer_other = bf16[48,8,128]{2,1,0:T(8,128)(2,1)S(1)} collective-permute-done((bf16[48,8,128]{2,1,0:T(8,128)(2,1)S(1)}, bf16[48,8,128]{2,1,0:T(8,128)(2,1)S(1)}, u32[]{:S(2)}, u32[]{:S(2)}) %collective-permute-start.4) | collective-permute-done | bytes 98336 | tf_op jit(solution)/shard_map/ppermute | solution.py:335
  20.4 0.4 %collective-permute-done.2.inner_other = bf16[48,8,128]{2,1,0:T(8,128)(2,1)S(1)} collective-permute-done((bf16[48,8,128]{2,1,0:T(8,128)(2,1)S(1)}, bf16[48,8,128]{2,1,0:T(8,128)(2,1)S(1)}, u32[]{:S(2)}, u32[]{:S(2)}) %collective-permute-start.2) | collective-permute-done | bytes 98336 | tf_op jit(solution)/shard_map/ppermute | solution.py:334
  20.7 0.0 copy-done.2
  20.7 0.0 copy-done.1
  20.7 0.0 copy-done.4
  20.7 0.0 copy-done.6
  20.7 0.0 copy-done.3
  20.7 0.0 copy-start
  20.8 0.0 copy-start.5
  20.8 6.1 %window.1 = (f32[8,1024]{1,0:T(8,128)S(1)}, bf16[64,1024]{1,0:T(8,128)(2,1)S(1)}, bf16[64,768]{1,0:T(8,128)(2,1)S(1)}, bf16[4,64,256]{2,1,0:T(8,128)(2,1)S(1)}, bf16[2,64,512]{2,1,0:T(8,128)(2,1)S(1)}) custom-call(bf16[48,8,128]{2,1,0:T(8,128)(2,1)S(1)} %constant_dynamic-update-slice_fusion.own, bf16[48,8,128]{2,1,0:T(8,128)(2,1)S(1)} %collective-permute-done.1.inner_mine, ...), custom_call_target="tpu_custom_call" | custom-call | flops 120000000 | bytes 8000000 | tf_op jit(solution)/shard_map/window/pallas_call | solution.py:336
  26.9 1.4 %all-to-all-done.roots = bf16[128,4,128]{2,1,0:T(4,128)(2,1)S(1)} async-done(((bf16[128,4,128]{2,1,0:T(4,128)(2,1)}), bf16[128,4,128]{2,1,0:T(4,128)(2,1)S(1)}, u32[]{:S(2)}, u32[]{:S(2)}) %all-to-all-start) | async-done | bytes 131104 | tf_op jit(solution)/shard_map/all_to_all | solution.py:333
  28.3 0.0 copy-done
  28.3 0.0 copy-done.5
  28.3 2.0 %top.1 = f32[8,1024]{1,0:T(8,128)} custom-call(bf16[128,4,128]{2,1,0:T(4,128)(2,1)S(1)} %all-to-all-done.roots, bf16[126,64,128]{2,1,0:T(8,128)(2,1)S(1)} %copy-done, s32[2,126]{1,0:T(2,128)S(1)} %bitcast.4, f32[8,1024]{1,0:T(8,128)S(1)} %get-tuple-element.14.partial, bf16[64,1024]{1,0:T(8,128)(2,1)S(1)} %get-tuple-element.15.onward, ...), custom_call_target="tpu_custom_call" | custom-call | tf_op jit(solution)/shard_map/top/pallas_call | solution.py:381
  (1 shorter events, 0.0 us)
Async XLA Ops:
  0.0 20.7 %copy-start.2 = (bf16[15,64,128]{2,1,0:T(8,128)(2,1)S(1)}, bf16[15,64,128]{2,1,0:T(8,128)(2,1)}, u32[]{:S(2)}) copy-start(bf16[15,64,128]{2,1,0:T(8,128)(2,1)} %transfer.4) | copy-start | bytes 737284
  0.0 20.7 %copy-start.1 = (bf16[16,64,64]{2,1,0:T(8,128)(2,1)S(1)}, bf16[16,64,64]{2,1,0:T(8,128)(2,1)}, u32[]{:S(2)}) copy-start(bf16[16,64,64]{2,1,0:T(8,128)(2,1)} %basis.3) | copy-start | bytes 393220
  0.0 20.7 %copy-start.4 = (s32[31,16]{0,1:T(8,128)S(1)}, s32[31,16]{0,1:T(8,128)}, u32[]{:S(2)}) copy-start(s32[31,16]{0,1:T(8,128)} %param.18) | copy-start | bytes 5956
  0.0 20.7 %copy-start.6 = (s32[16]{0:T(128)S(1)}, s32[16]{0:T(128)}, u32[]{:S(2)}) copy-start(s32[16]{0:T(128)} %param.14) | copy-start | bytes 196
  0.0 20.7 %copy-start.3 = (s32[16,24]{1,0:T(8,128)S(1)}, s32[16,24]{1,0:T(8,128)}, u32[]{:S(2)}) copy-start(s32[16,24]{1,0:T(8,128)} %near_ids_in.1) | copy-start | bytes 4612
  2.5 2.5 %collective-permute-start = (bf16[24,8,128]{2,1,0:T(8,128)(2,1)}, bf16[24,8,128]{2,1,0:T(8,128)(2,1)S(1)}, u32[]{:S(2)}, u32[]{:S(2)}) collective-permute-start(bf16[24,8,128]{2,1,0:T(8,128)(2,1)} %get-tuple-element.13), channel_id=1, source_target_pairs={{0,1},{1,0},{2,3},{3,2},{4,5},{5,4},{6,7},{7,6},{8,9},{9,8},{10,11... | collective-permute-start | bytes 147464 | tf_op jit(solution)/shard_map/ppermute | solution.py:330
  5.0 13.3 %collective-permute-start.3 = (bf16[48,8,128]{2,1,0:T(8,128)(2,1)S(1)}, bf16[48,8,128]{2,1,0:T(8,128)(2,1)S(1)}, u32[]{:S(2)}, u32[]{:S(2)}) collective-permute-start(bf16[48,8,128]{2,1,0:T(8,128)(2,1)S(1)} %constant_dynamic-update-slice_fusion.own), channel_id=1, source_target_pairs={{2,4},{4,2},{6,8},{8,6},{10,12},{12,10},{14,16},{16,14},{18,20},{2... | collective-permute-start | bytes 294920 | tf_op jit(solution)/shard_map/ppermute | solution.py:332
  6.4 13.0 %collective-permute-start.1 = (bf16[48,8,128]{2,1,0:T(8,128)(2,1)S(1)}, bf16[48,8,128]{2,1,0:T(8,128)(2,1)S(1)}, u32[]{:S(2)}, u32[]{:S(2)}) collective-permute-start(bf16[48,8,128]{2,1,0:T(8,128)(2,1)S(1)} %constant_dynamic-update-slice_fusion.own), channel_id=1, source_target_pairs={{0,2},{2,0},{4,6},{6,4},{8,10},{10,8},{12,14},{14,12},{16,18},{18,... | collective-permute-start | bytes 294920 | tf_op jit(solution)/shard_map/ppermute | solution.py:331
  9.2 19.1 %all-to-all-start = ((bf16[128,4,128]{2,1,0:T(4,128)(2,1)}), bf16[128,4,128]{2,1,0:T(4,128)(2,1)S(1)}, u32[]{:S(2)}, u32[]{:S(2)}) async-start(bf16[128,4,128]{2,1,0:T(4,128)(2,1)} %get-tuple-element.12), calls=%async_computation | async-start | bytes 262144 | tf_op jit(solution)/shard_map/all_to_all | solution.py:333
  18.3 2.1 %collective-permute-start.4 = (bf16[48,8,128]{2,1,0:T(8,128)(2,1)S(1)}, bf16[48,8,128]{2,1,0:T(8,128)(2,1)S(1)}, u32[]{:S(2)}, u32[]{:S(2)}) collective-permute-start(bf16[48,8,128]{2,1,0:T(8,128)(2,1)S(1)} %collective-permute-done.3.outer_mine), channel_id=1, source_target_pairs={{0,1},{1,0},{2,3},{3,2},{4,5},{5,4},{6,7},{7,6},{8,9},{9,8},{10,11... | collective-permute-start | bytes 294920 | tf_op jit(solution)/shard_map/ppermute | solution.py:335
  19.4 1.3 %collective-permute-start.2 = (bf16[48,8,128]{2,1,0:T(8,128)(2,1)S(1)}, bf16[48,8,128]{2,1,0:T(8,128)(2,1)S(1)}, u32[]{:S(2)}, u32[]{:S(2)}) collective-permute-start(bf16[48,8,128]{2,1,0:T(8,128)(2,1)S(1)} %collective-permute-done.1.inner_mine), channel_id=1, source_target_pairs={{0,1},{1,0},{2,3},{3,2},{4,5},{5,4},{6,7},{7,6},{8,9},{9,8},{10,11... | collective-permute-start | bytes 294920 | tf_op jit(solution)/shard_map/ppermute | solution.py:334
  20.7 7.5 %copy-start = (bf16[126,64,128]{2,1,0:T(8,128)(2,1)S(1)}, bf16[126,64,128]{2,1,0:T(8,128)(2,1)}, u32[]{:S(2)}) copy-start(bf16[126,64,128]{2,1,0:T(8,128)(2,1)} %transfer.5) | copy-start | bytes 6193156
  20.8 7.5 %copy-start.5 = (s32[126,2]{0,1:T(2,128)S(1)}, s32[126,2]{0,1:T(2,128)}, u32[]{:S(2)}) copy-start(s32[126,2]{0,1:T(2,128)} %param.21) | copy-start | bytes 3028

commit v8 on v7

--- a/solution.py
+++ b/solution.py
@@ -112,10 +112,12 @@
     first = [dot_t(transfer[m], pair).astype(BF) for m, pair in enumerate(level)]
     top = dot(root_map, stacked(*second)).astype(BF)
     third = [dot(transfer[12 + q], stacked(second[2 * q], second[2 * q + 1])).astype(BF) for q in range(2)]
-    rows = stacked(*first, *second, *third, top).astype(F32).T
-    for q in range(7):
-        pack[16 + q] = rows[:, 128 * q : 128 * q + 128].astype(BF)
-    root = rows[:, 896:]
+    lower = stacked(*first, *second).astype(F32).T
+    rows = stacked(*third, top).astype(F32).T
+    for q in range(6):
+        pack[16 + q] = lower[:, 128 * q : 128 * q + 128].astype(BF)
+    pack[22] = rows[:, :128].astype(BF)
+    root = rows[:, 128:]
     pack[23] = beside(root, root).astype(BF)
     sent = beside(root[:4], root[4:]).astype(BF)
     roots[...] = jnp.broadcast_to(sent[None], roots.shape)

time: 30.5 us -> 30.5 us (level)
  no operation moved by 1% of the time
where the time goes in v8:
time: 30.5 us; the launch traced here: 30.3 us
  starting transfers between devices  15.9 us (52%)
  Pallas kernels  10.6 us (35%)
  waiting for transfers between devices  2.86 us (9%)
  local copies, waits for them, and re-layouts  0.84 us (3%)
    all_to_all x1, starting transfers between devices, local(): all_roots = lax.all_to_all(roots, every, 0, 0, tiled=True)  9.08 us
    pallas_call x1, Pallas kernels, local(): pl.pallas_call(window_kernel, out_shape=(shape((NV, 1024), F32), shape((K...  6.13 us
    ppermute x1, starting transfers between devices, local(): inner_mine = lax.ppermute(own, every, INNER)  2.77 us
    pallas_call x1, Pallas kernels, local(): pl.pallas_call(upward_kernel, out_shape=(shape((PAIRS, NV, 128), BF), sha...  2.45 us
    pallas_call x1, Pallas kernels, local(): pl.pallas_call(top_kernel, out_shape=shape((NV, 1024), F32), in_specs=[sp...  2 us
    ppermute x1, starting transfers between devices, local(): own = jnp.concatenate([pack, lax.ppermute(pack, 'sub', [(0, 1), (1, 0)])])  1.41 us
    ppermute x1, starting transfers between devices, local(): outer_mine = lax.ppermute(own, every, OUTER)  1.4 us
    all_to_all x1, waiting for transfers between devices, local(): all_roots = lax.all_to_all(roots, every, 0, 0, tiled=True)  1.37 us
  transfers between devices with their start and end apart: 6, of which 4 were waited for; matrix products, arithmetic and copies ran while one was open for 3% of the time, Pallas kernels for 20%

profile of v8, /device:TPU:1, one launch (start us, length us, event | category | flops | bytes accessed | tf_op | source)
XLA Modules:
  0.0 30.3 jit_solution(15315273749664331767)
XLA Ops:
  0.0 0.0 copy-start.2
  0.0 0.0 copy-start.1
  0.0 0.0 copy-start.4
  0.0 0.0 copy-start.6
  0.0 0.0 copy-start.3
  0.0 2.4 %upward.1 = (bf16[24,8,128]{2,1,0:T(8,128)(2,1)}, bf16[128,4,128]{2,1,0:T(4,128)(2,1)}) custom-call(bf16[8,1024]{1,0:T(8,128)(2,1)} %density.1, bf16[16,64,64]{2,1,0:T(8,128)(2,1)} %basis.3, bf16[15,64,128]{2,1,0:T(8,128)(2,1)} %transfer.4), custom_call_target="tpu_custom_call" | custom-call | flops 20000000000 | bytes 1000000 | tf_op jit(solution)/shard_map/upward/pallas_call | solution.py:322
  2.5 1.4 %collective-permute-start = (bf16[24,8,128]{2,1,0:T(8,128)(2,1)}, bf16[24,8,128]{2,1,0:T(8,128)(2,1)S(1)}, u32[]{:S(2)}, u32[]{:S(2)}) collective-permute-start(bf16[24,8,128]{2,1,0:T(8,128)(2,1)} %get-tuple-element.13), channel_id=1, source_target_pairs={{0,1},{1,0},{2,3},{3,2},{4,5},{5,4},{6,7},{7,6},{8,9},{9,8},{10,11... | collective-permute-start | bytes 147464 | tf_op jit(solution)/shard_map/ppermute | solution.py:332
  3.9 0.8 %constant_dynamic-update-slice_fusion.1 = bf16[48,8,128]{2,1,0:T(8,128)(2,1)S(1)} fusion(bf16[24,8,128]{2,1,0:T(8,128)(2,1)} %get-tuple-element.13), kind=kLoop, calls=%fused_computation.1 | loop fusion | bytes 98304
  4.7 0.3 collective-permute-done
  5.0 1.4 %collective-permute-start.3 = (bf16[48,8,128]{2,1,0:T(8,128)(2,1)S(1)}, bf16[48,8,128]{2,1,0:T(8,128)(2,1)S(1)}, u32[]{:S(2)}, u32[]{:S(2)}) collective-permute-start(bf16[48,8,128]{2,1,0:T(8,128)(2,1)S(1)} %constant_dynamic-update-slice_fusion.own), channel_id=1, source_target_pairs={{2,4},{4,2},{6,8},{8,6},{10,12},{12,10},{14,16},{16,14},{18,20},{2... | collective-permute-start | bytes 294920 | tf_op jit(solution)/shard_map/ppermute | solution.py:334
  6.4 2.8 %collective-permute-start.1 = (bf16[48,8,128]{2,1,0:T(8,128)(2,1)S(1)}, bf16[48,8,128]{2,1,0:T(8,128)(2,1)S(1)}, u32[]{:S(2)}, u32[]{:S(2)}) collective-permute-start(bf16[48,8,128]{2,1,0:T(8,128)(2,1)S(1)} %constant_dynamic-update-slice_fusion.own), channel_id=1, source_target_pairs={{0,2},{2,0},{4,6},{6,4},{8,10},{10,8},{12,14},{14,12},{16,18},{18,... | collective-permute-start | bytes 294920 | tf_op jit(solution)/shard_map/ppermute | solution.py:333
  9.2 9.1 %all-to-all-start = ((bf16[128,4,128]{2,1,0:T(4,128)(2,1)}), bf16[128,4,128]{2,1,0:T(4,128)(2,1)S(1)}, u32[]{:S(2)}, u32[]{:S(2)}) async-start(bf16[128,4,128]{2,1,0:T(4,128)(2,1)} %get-tuple-element.12), calls=%async_computation | async-start | bytes 262144 | tf_op jit(solution)/shard_map/all_to_all | solution.py:335
  18.2 0.0 collective-permute-done.3.outer_mine
  18.3 1.1 %collective-permute-start.4 = (bf16[48,8,128]{2,1,0:T(8,128)(2,1)S(1)}, bf16[48,8,128]{2,1,0:T(8,128)(2,1)S(1)}, u32[]{:S(2)}, u32[]{:S(2)}) collective-permute-start(bf16[48,8,128]{2,1,0:T(8,128)(2,1)S(1)} %collective-permute-done.3.outer_mine), channel_id=1, source_target_pairs={{0,1},{1,0},{2,3},{3,2},{4,5},{5,4},{6,7},{7,6},{8,9},{9,8},{10,11... | collective-permute-start | bytes 294920 | tf_op jit(solution)/shard_map/ppermute | solution.py:337
  19.4 0.0 collective-permute-done.1.inner_mine
  19.4 0.1 collective-permute-start.2
  19.5 0.8 %collective-permute-done.4.outer_other = bf16[48,8,128]{2,1,0:T(8,128)(2,1)S(1)} collective-permute-done((bf16[48,8,128]{2,1,0:T(8,128)(2,1)S(1)}, bf16[48,8,128]{2,1,0:T(8,128)(2,1)S(1)}, u32[]{:S(2)}, u32[]{:S(2)}) %collective-permute-start.4) | collective-permute-done | bytes 98336 | tf_op jit(solution)/shard_map/ppermute | solution.py:337
  20.4 0.4 %collective-permute-done.2.inner_other = bf16[48,8,128]{2,1,0:T(8,128)(2,1)S(1)} collective-permute-done((bf16[48,8,128]{2,1,0:T(8,128)(2,1)S(1)}, bf16[48,8,128]{2,1,0:T(8,128)(2,1)S(1)}, u32[]{:S(2)}, u32[]{:S(2)}) %collective-permute-start.2) | collective-permute-done | bytes 98336 | tf_op jit(solution)/shard_map/ppermute | solution.py:336
  20.7 0.0 copy-done.2
  20.7 0.0 copy-done.1
  20.7 0.0 copy-done.4
  20.7 0.0 copy-done.6
  20.7 0.0 copy-done.3
  20.7 0.0 copy-start
  20.8 0.0 copy-start.5
  20.8 6.1 %window.1 = (f32[8,1024]{1,0:T(8,128)S(1)}, bf16[64,1024]{1,0:T(8,128)(2,1)S(1)}, bf16[64,768]{1,0:T(8,128)(2,1)S(1)}, bf16[4,64,256]{2,1,0:T(8,128)(2,1)S(1)}, bf16[2,64,512]{2,1,0:T(8,128)(2,1)S(1)}) custom-call(bf16[48,8,128]{2,1,0:T(8,128)(2,1)S(1)} %constant_dynamic-update-slice_fusion.own, bf16[48,8,128]{2,1,0:T(8,128)(2,1)S(1)} %collective-permute-done.1.inner_mine, ...), custom_call_target="tpu_custom_call" | custom-call | flops 120000000 | bytes 8000000 | tf_op jit(solution)/shard_map/window/pallas_call | solution.py:338
  26.9 1.4 %all-to-all-done.roots = bf16[128,4,128]{2,1,0:T(4,128)(2,1)S(1)} async-done(((bf16[128,4,128]{2,1,0:T(4,128)(2,1)}), bf16[128,4,128]{2,1,0:T(4,128)(2,1)S(1)}, u32[]{:S(2)}, u32[]{:S(2)}) %all-to-all-start) | async-done | bytes 131104 | tf_op jit(solution)/shard_map/all_to_all | solution.py:335
  28.3 0.0 copy-done
  28.3 0.0 copy-done.5
  28.3 2.0 %top.1 = f32[8,1024]{1,0:T(8,128)} custom-call(bf16[128,4,128]{2,1,0:T(4,128)(2,1)S(1)} %all-to-all-done.roots, bf16[126,64,128]{2,1,0:T(8,128)(2,1)S(1)} %copy-done, s32[2,126]{1,0:T(2,128)S(1)} %bitcast.4, f32[8,1024]{1,0:T(8,128)S(1)} %get-tuple-element.14.partial, bf16[64,1024]{1,0:T(8,128)(2,1)S(1)} %get-tuple-element.15.onward, ...), custom_call_target="tpu_custom_call" | custom-call | tf_op jit(solution)/shard_map/top/pallas_call | solution.py:383
  (1 shorter events, 0.0 us)
Async XLA Ops:
  0.0 20.7 %copy-start.2 = (bf16[15,64,128]{2,1,0:T(8,128)(2,1)S(1)}, bf16[15,64,128]{2,1,0:T(8,128)(2,1)}, u32[]{:S(2)}) copy-start(bf16[15,64,128]{2,1,0:T(8,128)(2,1)} %transfer.4) | copy-start | bytes 737284
  0.0 20.7 %copy-start.1 = (bf16[16,64,64]{2,1,0:T(8,128)(2,1)S(1)}, bf16[16,64,64]{2,1,0:T(8,128)(2,1)}, u32[]{:S(2)}) copy-start(bf16[16,64,64]{2,1,0:T(8,128)(2,1)} %basis.3) | copy-start | bytes 393220
  0.0 20.7 %copy-start.4 = (s32[31,16]{0,1:T(8,128)S(1)}, s32[31,16]{0,1:T(8,128)}, u32[]{:S(2)}) copy-start(s32[31,16]{0,1:T(8,128)} %param.18) | copy-start | bytes 5956
  0.0 20.7 %copy-start.6 = (s32[16]{0:T(128)S(1)}, s32[16]{0:T(128)}, u32[]{:S(2)}) copy-start(s32[16]{0:T(128)} %param.14) | copy-start | bytes 196
  0.0 20.7 %copy-start.3 = (s32[16,24]{1,0:T(8,128)S(1)}, s32[16,24]{1,0:T(8,128)}, u32[]{:S(2)}) copy-start(s32[16,24]{1,0:T(8,128)} %near_ids_in.1) | copy-start | bytes 4612
  2.5 2.5 %collective-permute-start = (bf16[24,8,128]{2,1,0:T(8,128)(2,1)}, bf16[24,8,128]{2,1,0:T(8,128)(2,1)S(1)}, u32[]{:S(2)}, u32[]{:S(2)}) collective-permute-start(bf16[24,8,128]{2,1,0:T(8,128)(2,1)} %get-tuple-element.13), channel_id=1, source_target_pairs={{0,1},{1,0},{2,3},{3,2},{4,5},{5,4},{6,7},{7,6},{8,9},{9,8},{10,11... | collective-permute-start | bytes 147464 | tf_op jit(solution)/shard_map/ppermute | solution.py:332
  5.0 13.3 %collective-permute-start.3 = (bf16[48,8,128]{2,1,0:T(8,128)(2,1)S(1)}, bf16[48,8,128]{2,1,0:T(8,128)(2,1)S(1)}, u32[]{:S(2)}, u32[]{:S(2)}) collective-permute-start(bf16[48,8,128]{2,1,0:T(8,128)(2,1)S(1)} %constant_dynamic-update-slice_fusion.own), channel_id=1, source_target_pairs={{2,4},{4,2},{6,8},{8,6},{10,12},{12,10},{14,16},{16,14},{18,20},{2... | collective-permute-start | bytes 294920 | tf_op jit(solution)/shard_map/ppermute | solution.py:334
  6.4 13.0 %collective-permute-start.1 = (bf16[48,8,128]{2,1,0:T(8,128)(2,1)S(1)}, bf16[48,8,128]{2,1,0:T(8,128)(2,1)S(1)}, u32[]{:S(2)}, u32[]{:S(2)}) collective-permute-start(bf16[48,8,128]{2,1,0:T(8,128)(2,1)S(1)} %constant_dynamic-update-slice_fusion.own), channel_id=1, source_target_pairs={{0,2},{2,0},{4,6},{6,4},{8,10},{10,8},{12,14},{14,12},{16,18},{18,... | collective-permute-start | bytes 294920 | tf_op jit(solution)/shard_map/ppermute | solution.py:333
  9.2 19.1 %all-to-all-start = ((bf16[128,4,128]{2,1,0:T(4,128)(2,1)}), bf16[128,4,128]{2,1,0:T(4,128)(2,1)S(1)}, u32[]{:S(2)}, u32[]{:S(2)}) async-start(bf16[128,4,128]{2,1,0:T(4,128)(2,1)} %get-tuple-element.12), calls=%async_computation | async-start | bytes 262144 | tf_op jit(solution)/shard_map/all_to_all | solution.py:335
  18.3 2.1 %collective-permute-start.4 = (bf16[48,8,128]{2,1,0:T(8,128)(2,1)S(1)}, bf16[48,8,128]{2,1,0:T(8,128)(2,1)S(1)}, u32[]{:S(2)}, u32[]{:S(2)}) collective-permute-start(bf16[48,8,128]{2,1,0:T(8,128)(2,1)S(1)} %collective-permute-done.3.outer_mine), channel_id=1, source_target_pairs={{0,1},{1,0},{2,3},{3,2},{4,5},{5,4},{6,7},{7,6},{8,9},{9,8},{10,11... | collective-permute-start | bytes 294920 | tf_op jit(solution)/shard_map/ppermute | solution.py:337
  19.4 1.3 %collective-permute-start.2 = (bf16[48,8,128]{2,1,0:T(8,128)(2,1)S(1)}, bf16[48,8,128]{2,1,0:T(8,128)(2,1)S(1)}, u32[]{:S(2)}, u32[]{:S(2)}) collective-permute-start(bf16[48,8,128]{2,1,0:T(8,128)(2,1)S(1)} %collective-permute-done.1.inner_mine), channel_id=1, source_target_pairs={{0,1},{1,0},{2,3},{3,2},{4,5},{5,4},{6,7},{7,6},{8,9},{9,8},{10,11... | collective-permute-start | bytes 294920 | tf_op jit(solution)/shard_map/ppermute | solution.py:336
  20.7 7.5 %copy-start = (bf16[126,64,128]{2,1,0:T(8,128)(2,1)S(1)}, bf16[126,64,128]{2,1,0:T(8,128)(2,1)}, u32[]{:S(2)}) copy-start(bf16[126,64,128]{2,1,0:T(8,128)(2,1)} %transfer.5) | copy-start | bytes 6193156
  20.8 7.5 %copy-start.5 = (s32[126,2]{0,1:T(2,128)S(1)}, s32[126,2]{0,1:T(2,128)}, u32[]{:S(2)}) copy-start(s32[126,2]{0,1:T(2,128)} %param.21) | copy-start | bytes 3028
